TPU v7x, 32 devices: a whole 2x2x4 slice. The times are simulated.
32 devices in a mesh: wide: 8 (over y, x, core), narrow: 4 (over z).
Axes of the slice: x: 2, y: 2, z: 4, core: 2. Of those that a mesh axis runs over, the one named last changes fastest.
Arguments:
- long_in: bfloat16 [2, 32, 512, 768], P(None, ('wide', 'narrow')), may hold values from -6 to 6
- glob_in: bfloat16 [2, 32, 32, 768], P(None, ('wide', 'narrow')), may hold values from -6 to 6
- lengths: int32 [2, 32], P(None, ('wide', 'narrow')), may hold values from 128 to 512, as said below
- ln1_gain: bfloat16 [768], P(('wide', 'narrow')), may hold values from 0.5 to 1.5
- ln1_bias: bfloat16 [768], P(('wide', 'narrow')), may hold values from -1.5 to 1.5
- w_qkv: bfloat16 [768, 2304], P(('wide', 'narrow')), may hold values from -0.21875 to 0.21875
- qv_bias: bfloat16 [1536], P(('wide', 'narrow')), may hold values from -1.5 to 1.5
- rel_embed: bfloat16 [768, 169], P(('wide', 'narrow')), may hold values from -6 to 6
- w_out: bfloat16 [768, 768], P(('wide', 'narrow')), may hold values from -3 to 3
- out_bias: bfloat16 [768], P(('wide', 'narrow')), may hold values from -1.5 to 1.5
- ln2_gain: bfloat16 [768], P(('wide', 'narrow')), may hold values from 0.5 to 1.5
- ln2_bias: bfloat16 [768], P(('wide', 'narrow')), may hold values from -1.5 to 1.5
- w_in: bfloat16 [768, 3072], P(('wide', 'narrow')), may hold values from -0.21875 to 0.21875
- in_bias: bfloat16 [3072], P(('wide', 'narrow')), may hold values from -1.5 to 1.5
- w_down: bfloat16 [3072, 768], P(('wide', 'narrow')), may hold values from -0.109375 to 0.109375
- down_bias: bfloat16 [768], P(('wide', 'narrow')), may hold values from -1.5 to 1.5
- cot_long: bfloat16 [2, 32, 512, 768], P(None, ('wide', 'narrow')), may hold values from -6 to 6
- cot_glob: bfloat16 [2, 32, 32, 768], P(None, ('wide', 'narrow')), may hold values from -6 to 6
Outputs:
- block_long: bfloat16 [2, 32, 512, 768], P(None, ('wide', 'narrow'))
- block_glob: bfloat16 [2, 32, 32, 768], P(None, ('wide', 'narrow'))
- grad_long: bfloat16 [2, 32, 512, 768], P(None, ('wide', 'narrow'))
- grad_glob: bfloat16 [2, 32, 32, 768], P(None, ('wide', 'narrow'))
- grad_ln1_gain: float32 [768], P(('wide', 'narrow'))
- grad_ln1_bias: float32 [768], P(('wide', 'narrow'))
- grad_w_qkv: float32 [768, 2304], P(('wide', 'narrow'))
- grad_qv_bias: float32 [1536], P(('wide', 'narrow'))
- grad_rel_embed: float32 [768, 169], P(('wide', 'narrow'))
- grad_w_out: float32 [768, 768], P(('wide', 'narrow'))
- grad_out_bias: float32 [768], P(('wide', 'narrow'))
- grad_ln2_gain: float32 [768], P(('wide', 'narrow'))
- grad_ln2_bias: float32 [768], P(('wide', 'narrow'))
- grad_w_in: float32 [768, 3072], P(('wide', 'narrow'))
- grad_in_bias: float32 [3072], P(('wide', 'narrow'))
- grad_w_down: float32 [3072, 768], P(('wide', 'narrow'))
- grad_down_bias: float32 [768], P(('wide', 'narrow'))
Inputs may be any that keep to these rules, and one draw needn't show every extreme that they name: lengths[u, n] is the number of live long tokens of sequence n in micro-batch u; rows at or beyond it are padding. Every draw has an entry equal to 512 and one equal to 128.
All inputs are finite; a program needn't handle non-finite values.
Results may differ from a plain program's by a relative error of at most 0.012.
Values may be sent and summed in bfloat16 or wider, within the bound.
No kernel may reach another device: no remote copies, remote signals or barrier semaphores. Data moves between devices by JAX's collectives and lax.ppermute only.
A program may use at most 320 MiB of HBM per device.

v0:
```python
import jax
import jax.numpy as jnp
from jax import lax
from jax.sharding import PartitionSpec as P

HEAD_DIM = 64
RADIUS = 84
GLOBAL_STRIDE = 16
SEQ = 512
BLOCK = 512
MARGIN = 112
RELS = 169
GLOB = 32


eps_norm = 1e-06
neg_big = -1e30


def norm_apply(values, gain_vec, shift_vec):
    centred = values - jnp.mean(values, axis=-1, keepdims=True)
    spread = jnp.mean(centred * centred, axis=-1, keepdims=True)
    return centred * lax.rsqrt(spread + eps_norm) * gain_vec + shift_vec


def exact_gelu(values):
    return jax.nn.gelu(values, approximate=False)


def skew_rows(rel_scores):
    head_count = rel_scores.shape[0]
    win_cols = BLOCK + 2 * MARGIN
    lead_cols = MARGIN - RADIUS
    placed = jnp.pad(rel_scores, ((0, 0), (0, 0), (lead_cols, win_cols + 1 - lead_cols - RELS)))
    flat_rows = placed.reshape(head_count, BLOCK * (win_cols + 1))[:, : BLOCK * win_cols]
    return flat_rows.reshape(head_count, BLOCK, win_cols)


def live_rows(length):
    glob_count = (length + GLOBAL_STRIDE - 1) // GLOBAL_STRIDE
    glob_ok = jnp.arange(GLOB, dtype=jnp.int32) < glob_count
    long_ok = jnp.arange(SEQ, dtype=jnp.int32) < length
    return (glob_ok, long_ok)


def long_allowed(row_start, length, glob_ok):
    win_cols = BLOCK + 2 * MARGIN
    row_pos = row_start + jnp.arange(BLOCK, dtype=jnp.int32)
    col_pos = row_start - MARGIN + jnp.arange(win_cols, dtype=jnp.int32)
    near_band = jnp.abs(col_pos[None, :] - row_pos[:, None]) <= RADIUS
    inside = (col_pos >= 0) & (col_pos < length)
    glob_part = jnp.broadcast_to(glob_ok[None, :], (BLOCK, GLOB))
    return jnp.concatenate([glob_part, near_band & inside[None, :]], axis=1)


def block_inputs(queries, key_rows, value_rows, glob_ok, long_ok, length, block_num):
    if block_num < 0:
        allowed = jnp.broadcast_to(jnp.concatenate([glob_ok, long_ok])[None, :], (GLOB, GLOB + SEQ))
        return (queries[:GLOB], key_rows, value_rows, allowed)
    row_start = block_num * BLOCK
    win_cols = BLOCK + 2 * MARGIN
    pad_spec = ((MARGIN, MARGIN), (0, 0), (0, 0))
    keys_win = jnp.pad(key_rows[GLOB:], pad_spec)
    values_win = jnp.pad(value_rows[GLOB:], pad_spec)
    cols_k = jnp.concatenate([key_rows[:GLOB], keys_win], axis=0)
    cols_v = jnp.concatenate([value_rows[:GLOB], values_win], axis=0)
    block_q = queries[GLOB + row_start : GLOB + row_start + BLOCK]
    return (block_q, cols_k, cols_v, long_allowed(row_start, length, glob_ok))


def query_rows(block_num):
    if block_num < 0:
        return (0, GLOB)
    return (GLOB + block_num * BLOCK, BLOCK)


def block_scores(block_q, cols_k, rel_heads, allowed, with_rel):
    scores = jnp.einsum("qhd,khd->hqk", block_q, cols_k, preferred_element_type=jnp.float32)
    if with_rel:
        rel_scores = jnp.einsum(
            "qhd,hdl->hql", block_q, rel_heads, preferred_element_type=jnp.float32
        )
        scores = scores + jnp.pad(skew_rows(rel_scores), ((0, 0), (0, 0), (GLOB, 0)))
    return jnp.where(allowed[None], scores * 0.125, neg_big)


def block_forward(block_q, cols_k, cols_v, rel_heads, allowed, with_rel):
    scores = block_scores(block_q, cols_k, rel_heads, allowed, with_rel)
    row_max = jnp.max(scores, axis=-1, keepdims=True)
    exp_terms = jnp.exp(scores - row_max)
    row_sum = jnp.sum(exp_terms, axis=-1, keepdims=True)
    soft_weights = (exp_terms / row_sum).astype(jnp.bfloat16)
    mixed_part = jnp.einsum(
        "hqk,khd->qhd", soft_weights, cols_v, preferred_element_type=jnp.float32
    )
    return (mixed_part, row_max + jnp.log(row_sum))


def block_backward(block_q, cols_k, cols_v, rel_heads, allowed, with_rel, log_norm, grad_mix):
    scores = block_scores(block_q, cols_k, rel_heads, allowed, with_rel)
    soft_full = jnp.exp(scores - log_norm)
    soft_weights = soft_full.astype(jnp.bfloat16)
    grad_soft = jnp.einsum("qhd,khd->hqk", grad_mix, cols_v, preferred_element_type=jnp.float32)
    centre = jnp.sum(soft_full * grad_soft, axis=-1, keepdims=True)
    grad_scores = (soft_full * (grad_soft - centre)).astype(jnp.bfloat16)
    grad_q = (
        jnp.einsum("hqk,khd->qhd", grad_scores, cols_k, preferred_element_type=jnp.float32) * 0.125
    )
    grad_k = (
        jnp.einsum("hqk,qhd->khd", grad_scores, block_q, preferred_element_type=jnp.float32) * 0.125
    )
    grad_v = jnp.einsum("hqk,qhd->khd", soft_weights, grad_mix, preferred_element_type=jnp.float32)
    grad_rel = jnp.zeros(rel_heads.shape, jnp.float32)
    if with_rel:
        template = jnp.zeros((rel_heads.shape[0], BLOCK, RELS), jnp.float32)
        unskew = jax.vjp(skew_rows, template)[1]
        grad_rel_scores = unskew(grad_scores[:, :, GLOB:].astype(jnp.float32))[0].astype(
            jnp.bfloat16
        )
        grad_q = (
            grad_q
            + jnp.einsum(
                "hql,hdl->qhd", grad_rel_scores, rel_heads, preferred_element_type=jnp.float32
            )
            * 0.125
        )
        grad_rel = (
            jnp.einsum("qhd,hql->hdl", block_q, grad_rel_scores, preferred_element_type=jnp.float32)
            * 0.125
        )
    return (grad_q, grad_k, grad_v, grad_rel)


def add_key_grads(acc_glob, acc_long, grad_cols, block_num):
    if block_num < 0:
        return (grad_cols[:GLOB], acc_long.at[MARGIN : MARGIN + SEQ].add(grad_cols[GLOB:]))
    row_start = block_num * BLOCK
    win_cols = BLOCK + 2 * MARGIN
    return (
        acc_glob + grad_cols[:GLOB],
        acc_long.at[row_start : row_start + win_cols].add(grad_cols[GLOB:]),
    )


def forward_one(long_rows, glob_rows, length, attn_full, ffn_full):
    ln1_gain, ln1_bias, w_qkv, qv_bias, rel_embed, w_out, out_bias = attn_full
    ln2_gain, ln2_bias, w_in, in_bias, w_down, down_bias = ffn_full
    model_dim = w_out.shape[0]
    head_count = model_dim // HEAD_DIM
    row_count = GLOB + SEQ
    hidden_in = jnp.concatenate([glob_rows, long_rows], axis=0).astype(jnp.float32)
    normed = norm_apply(
        hidden_in, ln1_gain.astype(jnp.float32), ln1_bias.astype(jnp.float32)
    ).astype(jnp.bfloat16)
    full_bias = jnp.concatenate(
        [qv_bias[:model_dim], jnp.zeros((model_dim,), jnp.bfloat16), qv_bias[model_dim:]]
    ).astype(jnp.float32)
    projected = (jnp.dot(normed, w_qkv, preferred_element_type=jnp.float32) + full_bias).astype(
        jnp.bfloat16
    )
    head_view = projected.reshape(row_count, 3, head_count, HEAD_DIM)
    queries = head_view[:, 0]
    key_rows = head_view[:, 1]
    value_rows = head_view[:, 2]
    rel_heads = rel_embed.reshape(head_count, HEAD_DIM, RELS)
    glob_ok, long_ok = live_rows(length)
    pieces = []
    log_norms = []
    for block_num in range(-1, SEQ // BLOCK):
        block_q, cols_k, cols_v, allowed = block_inputs(
            queries, key_rows, value_rows, glob_ok, long_ok, length, block_num
        )
        mixed_part, log_norm = block_forward(
            block_q, cols_k, cols_v, rel_heads, allowed, block_num >= 0
        )
        pieces.append(mixed_part)
        log_norms.append(log_norm)
    mixed_rows = jnp.concatenate(pieces, axis=0).reshape(row_count, model_dim).astype(jnp.bfloat16)
    residual = (
        hidden_in
        + jnp.dot(mixed_rows, w_out, preferred_element_type=jnp.float32)
        + out_bias.astype(jnp.float32)
    )
    normed2 = norm_apply(
        residual, ln2_gain.astype(jnp.float32), ln2_bias.astype(jnp.float32)
    ).astype(jnp.bfloat16)
    pre_act = jnp.dot(normed2, w_in, preferred_element_type=jnp.float32) + in_bias.astype(
        jnp.float32
    )
    activated = exact_gelu(pre_act).astype(jnp.bfloat16)
    full_out = (
        residual
        + jnp.dot(activated, w_down, preferred_element_type=jnp.float32)
        + down_bias.astype(jnp.float32)
    )
    live_mask = jnp.concatenate([glob_ok, long_ok])[:, None]
    block_out = jnp.where(live_mask, full_out, 0.0).astype(jnp.bfloat16)
    kept_state = (
        normed,
        projected,
        tuple(log_norms),
        mixed_rows,
        residual,
        normed2,
        pre_act,
        activated,
    )
    return (kept_state, block_out[GLOB:], block_out[:GLOB])


def backward_ffn(kept_state, length, cot_long_rows, cot_glob_rows, ffn_full):
    ln2_gain, ln2_bias, w_in, in_bias, w_down, down_bias = ffn_full
    normed, projected, log_norms, mixed_rows, residual, normed2, pre_act, activated = kept_state
    glob_ok, long_ok = live_rows(length)
    live_mask = jnp.concatenate([glob_ok, long_ok])[:, None]
    cot_rows = jnp.concatenate([cot_glob_rows, cot_long_rows], axis=0).astype(jnp.float32)
    grad_top = jnp.where(live_mask, cot_rows, 0.0)
    grad_ffn = grad_top.astype(jnp.bfloat16)
    grad_w_down = jnp.einsum("nf,nd->fd", activated, grad_ffn, preferred_element_type=jnp.float32)
    grad_down_bias = jnp.sum(grad_ffn.astype(jnp.float32), axis=0)
    grad_act = jnp.einsum("nd,fd->nf", grad_ffn, w_down, preferred_element_type=jnp.float32)
    gelu_back = jax.vjp(exact_gelu, pre_act)[1]
    grad_pre = gelu_back(grad_act)[0].astype(jnp.bfloat16)
    grad_w_in = jnp.einsum("nd,nf->df", normed2, grad_pre, preferred_element_type=jnp.float32)
    grad_in_bias = jnp.sum(grad_pre.astype(jnp.float32), axis=0)
    grad_norm2 = jnp.einsum("nf,df->nd", grad_pre, w_in, preferred_element_type=jnp.float32)
    norm_back2 = jax.vjp(
        norm_apply, residual, ln2_gain.astype(jnp.float32), ln2_bias.astype(jnp.float32)
    )[1]
    grad_res_norm, grad_ln2_gain, grad_ln2_bias = norm_back2(grad_norm2)
    grad_residual = grad_top + grad_res_norm
    ffn_terms = (grad_ln2_gain, grad_ln2_bias, grad_w_in, grad_in_bias, grad_w_down, grad_down_bias)
    return (ffn_terms, grad_residual)


def backward_attn(kept_state, long_rows, glob_rows, length, grad_residual, attn_full):
    ln1_gain, ln1_bias, w_qkv, qv_bias, rel_embed, w_out, out_bias = attn_full
    normed, projected, log_norms, mixed_rows, residual, normed2, pre_act, activated = kept_state
    model_dim = w_out.shape[0]
    head_count = model_dim // HEAD_DIM
    row_count = GLOB + SEQ
    hidden_in = jnp.concatenate([glob_rows, long_rows], axis=0).astype(jnp.float32)
    glob_ok, long_ok = live_rows(length)
    grad_attn = grad_residual.astype(jnp.bfloat16)
    grad_w_out = jnp.einsum("nd,ne->de", mixed_rows, grad_attn, preferred_element_type=jnp.float32)
    grad_out_bias = jnp.sum(grad_attn.astype(jnp.float32), axis=0)
    grad_mixed = jnp.einsum("ne,de->nd", grad_attn, w_out, preferred_element_type=jnp.float32)
    grad_mixed = grad_mixed.astype(jnp.bfloat16).reshape(row_count, head_count, HEAD_DIM)
    head_view = projected.reshape(row_count, 3, head_count, HEAD_DIM)
    queries = head_view[:, 0]
    key_rows = head_view[:, 1]
    value_rows = head_view[:, 2]
    rel_heads = rel_embed.reshape(head_count, HEAD_DIM, RELS)
    acc_keys_glob = jnp.zeros((GLOB, head_count, HEAD_DIM), jnp.float32)
    acc_keys_long = jnp.zeros((SEQ + 2 * MARGIN, head_count, HEAD_DIM), jnp.float32)
    acc_vals_glob = jnp.zeros((GLOB, head_count, HEAD_DIM), jnp.float32)
    acc_vals_long = jnp.zeros((SEQ + 2 * MARGIN, head_count, HEAD_DIM), jnp.float32)
    grad_rel = jnp.zeros(rel_heads.shape, jnp.float32)
    grad_queries = []
    for block_num in range(-1, SEQ // BLOCK):
        block_q, cols_k, cols_v, allowed = block_inputs(
            queries, key_rows, value_rows, glob_ok, long_ok, length, block_num
        )
        first_row, row_span = query_rows(block_num)
        grad_q, grad_k, grad_v, grad_rel_part = block_backward(
            block_q,
            cols_k,
            cols_v,
            rel_heads,
            allowed,
            block_num >= 0,
            log_norms[block_num + 1],
            grad_mixed[first_row : first_row + row_span],
        )
        grad_queries.append(grad_q)
        acc_keys_glob, acc_keys_long = add_key_grads(
            acc_keys_glob, acc_keys_long, grad_k, block_num
        )
        acc_vals_glob, acc_vals_long = add_key_grads(
            acc_vals_glob, acc_vals_long, grad_v, block_num
        )
        grad_rel = grad_rel_part
    grad_keys = jnp.concatenate([acc_keys_glob, acc_keys_long[MARGIN : MARGIN + SEQ]], axis=0)
    grad_vals = jnp.concatenate([acc_vals_glob, acc_vals_long[MARGIN : MARGIN + SEQ]], axis=0)
    grad_proj = jnp.stack([jnp.concatenate(grad_queries, axis=0), grad_keys, grad_vals], axis=1)
    grad_proj = grad_proj.reshape(row_count, 3 * model_dim).astype(jnp.bfloat16)
    grad_w_qkv = jnp.einsum("nd,nc->dc", normed, grad_proj, preferred_element_type=jnp.float32)
    proj_sums = jnp.sum(grad_proj.astype(jnp.float32), axis=0)
    grad_qv_bias = jnp.concatenate([proj_sums[:model_dim], proj_sums[2 * model_dim :]])
    grad_norm1 = jnp.einsum("nc,dc->nd", grad_proj, w_qkv, preferred_element_type=jnp.float32)
    norm_back1 = jax.vjp(
        norm_apply, hidden_in, ln1_gain.astype(jnp.float32), ln1_bias.astype(jnp.float32)
    )[1]
    grad_in_norm, grad_ln1_gain, grad_ln1_bias = norm_back1(grad_norm1)
    grad_hidden = grad_residual + grad_in_norm
    attn_terms = (
        grad_ln1_gain,
        grad_ln1_bias,
        grad_w_qkv,
        grad_qv_bias,
        grad_rel.reshape(model_dim, RELS),
        grad_w_out,
        grad_out_bias,
    )
    return (
        attn_terms,
        grad_hidden[GLOB:].astype(jnp.bfloat16),
        grad_hidden[:GLOB].astype(jnp.bfloat16),
    )


def sum_attn(attn_terms):
    attn_shares = (
        lax.psum_scatter(attn_terms[0], ("wide", "narrow"), scatter_dimension=0, tiled=True),
        lax.psum_scatter(attn_terms[1], ("wide", "narrow"), scatter_dimension=0, tiled=True),
        lax.psum_scatter(attn_terms[2], ("wide", "narrow"), scatter_dimension=0, tiled=True),
        lax.psum_scatter(attn_terms[3], ("wide", "narrow"), scatter_dimension=0, tiled=True),
        lax.psum_scatter(attn_terms[4], ("wide", "narrow"), scatter_dimension=0, tiled=True),
        lax.psum_scatter(attn_terms[5], ("wide", "narrow"), scatter_dimension=0, tiled=True),
        lax.psum_scatter(attn_terms[6], ("wide", "narrow"), scatter_dimension=0, tiled=True),
    )
    return tuple(attn_shares)


def sum_ffn(ffn_terms):
    ffn_shares = (
        lax.psum_scatter(ffn_terms[0], ("wide", "narrow"), scatter_dimension=0, tiled=True),
        lax.psum_scatter(ffn_terms[1], ("wide", "narrow"), scatter_dimension=0, tiled=True),
        lax.psum_scatter(ffn_terms[2], ("wide", "narrow"), scatter_dimension=0, tiled=True),
        lax.psum_scatter(ffn_terms[3], ("wide", "narrow"), scatter_dimension=0, tiled=True),
        lax.psum_scatter(ffn_terms[4], ("wide", "narrow"), scatter_dimension=0, tiled=True),
        lax.psum_scatter(ffn_terms[5], ("wide", "narrow"), scatter_dimension=0, tiled=True),
    )
    return tuple(ffn_shares)


def add_terms(total, part):
    if total is None:
        return tuple(part)
    return tuple(jax.tree.map(jnp.add, total, part))


def body(
    long_in,
    glob_in,
    lengths,
    ln1_gain,
    ln1_bias,
    w_qkv,
    qv_bias,
    rel_embed,
    w_out,
    out_bias,
    ln2_gain,
    ln2_bias,
    w_in,
    in_bias,
    w_down,
    down_bias,
    cot_long,
    cot_glob,
):
    attn_full = (
        lax.all_gather(ln1_gain, ("wide", "narrow"), axis=0, tiled=True),
        lax.all_gather(ln1_bias, ("wide", "narrow"), axis=0, tiled=True),
        lax.all_gather(w_qkv, ("wide", "narrow"), axis=0, tiled=True),
        lax.all_gather(qv_bias, ("wide", "narrow"), axis=0, tiled=True),
        lax.all_gather(rel_embed, ("wide", "narrow"), axis=0, tiled=True),
        lax.all_gather(w_out, ("wide", "narrow"), axis=0, tiled=True),
        lax.all_gather(out_bias, ("wide", "narrow"), axis=0, tiled=True),
    )
    ffn_full = (
        lax.all_gather(ln2_gain, ("wide", "narrow"), axis=0, tiled=True),
        lax.all_gather(ln2_bias, ("wide", "narrow"), axis=0, tiled=True),
        lax.all_gather(w_in, ("wide", "narrow"), axis=0, tiled=True),
        lax.all_gather(in_bias, ("wide", "narrow"), axis=0, tiled=True),
        lax.all_gather(w_down, ("wide", "narrow"), axis=0, tiled=True),
        lax.all_gather(down_bias, ("wide", "narrow"), axis=0, tiled=True),
    )
    micro_count = long_in.shape[0]
    kept_all = []
    long_outs = []
    glob_outs = []
    for micro_idx in range(micro_count):
        kept_state, long_out, glob_out = forward_one(
            long_in[micro_idx, 0],
            glob_in[micro_idx, 0],
            lengths[micro_idx, 0],
            tuple(attn_full),
            tuple(ffn_full),
        )
        kept_all.append(kept_state)
        long_outs.append(long_out)
        glob_outs.append(glob_out)
    attn_back = (
        lax.all_gather(ln1_gain, ("wide", "narrow"), axis=0, tiled=True),
        lax.all_gather(ln1_bias, ("wide", "narrow"), axis=0, tiled=True),
        lax.all_gather(w_qkv, ("wide", "narrow"), axis=0, tiled=True),
        lax.all_gather(qv_bias, ("wide", "narrow"), axis=0, tiled=True),
        lax.all_gather(rel_embed, ("wide", "narrow"), axis=0, tiled=True),
        lax.all_gather(w_out, ("wide", "narrow"), axis=0, tiled=True),
        lax.all_gather(out_bias, ("wide", "narrow"), axis=0, tiled=True),
    )
    ffn_back = (
        lax.all_gather(ln2_gain, ("wide", "narrow"), axis=0, tiled=True),
        lax.all_gather(ln2_bias, ("wide", "narrow"), axis=0, tiled=True),
        lax.all_gather(w_in, ("wide", "narrow"), axis=0, tiled=True),
        lax.all_gather(in_bias, ("wide", "narrow"), axis=0, tiled=True),
        lax.all_gather(w_down, ("wide", "narrow"), axis=0, tiled=True),
        lax.all_gather(down_bias, ("wide", "narrow"), axis=0, tiled=True),
    )
    grad_longs = []
    grad_globs = []
    attn_total = None
    ffn_total = None
    for micro_idx in range(micro_count):
        ffn_terms, grad_residual = backward_ffn(
            kept_all[micro_idx],
            lengths[micro_idx, 0],
            cot_long[micro_idx, 0],
            cot_glob[micro_idx, 0],
            tuple(ffn_back),
        )
        ffn_total = add_terms(ffn_total, ffn_terms)
        attn_terms, grad_long_part, grad_glob_part = backward_attn(
            kept_all[micro_idx],
            long_in[micro_idx, 0],
            glob_in[micro_idx, 0],
            lengths[micro_idx, 0],
            grad_residual,
            tuple(attn_back),
        )
        grad_longs.append(grad_long_part)
        grad_globs.append(grad_glob_part)
        attn_total = add_terms(attn_total, attn_terms)
    attn_total = sum_attn(attn_total)
    ffn_total = sum_ffn(ffn_total)
    outputs = (
        jnp.stack(long_outs)[:, None],
        jnp.stack(glob_outs)[:, None],
        jnp.stack(grad_longs)[:, None],
        jnp.stack(grad_globs)[:, None],
    )
    return outputs + tuple(attn_total) + tuple(ffn_total)


def solution(mesh):
    placed = (
        P(None, ("wide", "narrow"), None, None),
        P(None, ("wide", "narrow"), None, None),
        P(None, ("wide", "narrow")),
        P(("wide", "narrow")),
        P(("wide", "narrow")),
        P(("wide", "narrow"), None),
        P(("wide", "narrow")),
        P(("wide", "narrow"), None),
        P(("wide", "narrow"), None),
        P(("wide", "narrow")),
        P(("wide", "narrow")),
        P(("wide", "narrow")),
        P(("wide", "narrow"), None),
        P(("wide", "narrow")),
        P(("wide", "narrow"), None),
        P(("wide", "narrow")),
        P(None, ("wide", "narrow"), None, None),
        P(None, ("wide", "narrow"), None, None),
    )
    return jax.shard_map(
        body,
        mesh=mesh,
        in_specs=placed,
        out_specs=(
            P(None, ("wide", "narrow"), None, None),
            P(None, ("wide", "narrow"), None, None),
            P(None, ("wide", "narrow"), None, None),
            P(None, ("wide", "narrow"), None, None),
            P(("wide", "narrow")),
            P(("wide", "narrow")),
            P(("wide", "narrow"), None),
            P(("wide", "narrow")),
            P(("wide", "narrow"), None),
            P(("wide", "narrow"), None),
            P(("wide", "narrow")),
            P(("wide", "narrow")),
            P(("wide", "narrow")),
            P(("wide", "narrow"), None),
            P(("wide", "narrow")),
            P(("wide", "narrow"), None),
            P(("wide", "narrow")),
        ),
        check_vma=False,
    )
```

profile of v0, /device:TPU:0, one launch (start us, length us, event | category | flops | bytes accessed | tf_op | source)
XLA Modules:
  0.0 1453.1 jit_solution(16897893097309594899)
XLA Ops:
  22.8 43.1 %all-reduce.31 = (bf16[1536]{0:T(1024)(128)(2,1)S(1)}, bf16[768]{0:T(1024)(128)(2,1)S(1)}, bf16[768]{0:T(1024)(128)(2,1)S(1)}, bf16[768]{0:T(1024)(128)(2,1)S(1)...) all-reduce(bf16[1536]{0:T(1024)(128)(2,1)S(1)} %dynamic-update-slic, ...), channel_id=1, replica_groups=mesh['wide'=8,'narrow'=4] {'wide','narrow'}, use_global_device_ids=true, to_apply=%add.16 | all-reduce | flops 9216 | bytes 36864
  70.6 70.8 %all_gather.50 = bf16[768,169]{1,0:T(8,128)(2,1)S(1)} all-gather(bf16[24,169]{1,0:T(8,128)(2,1)} %param.49), channel_id=1, replica_groups=mesh['wide'=8,'narrow'=4] {'wide','narrow'}, dimensions={0}, use_global_device_ids=true | all-gather | bytes 267696 | tf_op jit(solution)/shard_map/all_gather | solution.py:368
  148.8 5.7 add_convert_fusion.3
  154.6 4.0 copy.89
  164.6 3.7 add_convert_fusion.2
  168.3 4.7 copy.93
  181.0 4.2 fusion.111
  185.2 4.1 fusion.110
  192.8 12.8 pad.78.clone
  205.6 29.2 %reshape.575 = f32[12,377344]{1,0:T(8,128)} reshape(f32[12,512,737]{2,1,0:T(8,128)} %pad.78.clone) | data formatting | bytes 36225024 | tf_op jit(solution)/shard_map/reshape | solution.py:35
  234.8 16.6 %slice.574 = f32[12,376832]{1,0:T(8,128)} slice(f32[12,377344]{1,0:T(8,128)} %reshape.575), slice={[0:12], [0:376832]} | slice | bytes 36175872 | tf_op jit(solution)/shard_map/slice | solution.py:35
  251.4 30.1 %reshape.576 = f32[12,512,736]{2,1,0:T(8,128)} reshape(f32[12,376832]{1,0:T(8,128)} %slice.574) | data formatting | bytes 36175872 | tf_op jit(solution)/shard_map/reshape | solution.py:36
  281.6 17.9 %fusion.192 = (f32[12,512]{1,0:T(8,128)}, f32[12,512,768]{2,1,0:T(8,128)}) fusion(f32[12,512,736]{2,1,0:T(8,128)} %reshape.576, bf16[512,12,64]{0,2,1:T(8,128)(2,1)} %get-tuple-element.245, bf16[32,12,64]{0,2,1:T(8,128)(2,1)S(1)} %get-tuple-element.243, bf16[544,3,12,64]{0,3,2,1:T(8,128)(2,1)S(1)} %bitcast.243, pred[512,768]{1,0:T(8,128)(4,1)S(1)} %copy-done.76), kind=kOutput, calls=%fused_computation.347 | convolution fusion | flops 626386944 | bytes 39149568 | tf_op jit(solution)/shard_map/qhd,khd->hqk/dot_general | solution.py:78
  299.5 8.4 fusion
  311.4 6.3 fusion.80
  322.5 12.6 pad.82.clone
  335.1 29.0 %reshape.578 = f32[12,377344]{1,0:T(8,128)} reshape(f32[12,512,737]{2,1,0:T(8,128)} %pad.82.clone) | data formatting | bytes 36225024 | tf_op jit(solution)/shard_map/reshape | solution.py:35
  364.1 16.5 %slice.584 = f32[12,376832]{1,0:T(8,128)} slice(f32[12,377344]{1,0:T(8,128)} %reshape.578), slice={[0:12], [0:376832]} | slice | bytes 36175872 | tf_op jit(solution)/shard_map/slice | solution.py:35
  380.6 30.1 %reshape.579 = f32[12,512,736]{2,1,0:T(8,128)} reshape(f32[12,376832]{1,0:T(8,128)} %slice.584) | data formatting | bytes 36175872 | tf_op jit(solution)/shard_map/reshape | solution.py:36
  410.8 18.1 %fusion.190 = (f32[12,512]{1,0:T(8,128)S(1)}, f32[12,512,768]{2,1,0:T(8,128)}) fusion(f32[12,512,736]{2,1,0:T(8,128)} %reshape.579, bf16[512,12,64]{0,2,1:T(8,128)(2,1)S(1)} %copy-done.43, bf16[32,12,64]{0,2,1:T(8,128)(2,1)S(1)} %copy-done.73, bf16[544,3,12,64]{0,3,2,1:T(8,128)(2,1)} %bitcast.251, pred[512,768]{1,0:T(8,128)(4,1)S(1)} %copy-done.75), kind=kOutput, calls=%fused_computation.345 | convolution fusion | flops 626386944 | bytes 39788544 | tf_op jit(solution)/shard_map/qhd,khd->hqk/dot_general | solution.py:78
  428.9 8.4 fusion.1
  440.7 6.7 fusion.81
  453.0 5.5 fusion.177
  461.2 34.3 %multiply_convert_fusion.3 = (bf16[544,3072]{1,0:T(8,128)(2,1)}, f32[544,3072]{1,0:T(8,128)}, bf16[544,3072]{1,0:T(8,128)(2,1)}, f32[544,3072]{1,0:T(8,128)}, f32[544,3072]{1,0:T(8,128)}) fusion(f32[3072]{0:T(1024)S(1)} %copy-done.149, f32[544,3072]{1,0:T(8,128)S(1)} %fusion.177, bf16[768,3072]{1,0:T(8,128)(2,1)S(1)} %copy-done.161, ...), kind=kOutput, calls=%fused_computation.43 | convolution fusion | flops 2789597184 | bytes 39835904 | tf_op jit(solution)/shard_map/dot_general | solution.py:187
  495.5 9.8 convert_reduce_fusion
  509.2 9.1 convert_reduce_fusion.1
  518.3 3.9 multiply_reduce_fusion.3
  553.2 10.0 fusion.51
  563.2 16.1 %multiply_reduce_fusion = (f32[12,512]{1,0:T(8,128)S(1)}, f32[12,512,768]{2,1,0:T(8,128)}) fusion(f32[12,512,768]{2,1,0:T(8,128)} %get-tuple-element.279, f32[12,512]{1,0:T(8,128)S(1)} %copy-done.103, bf16[512,12,64]{0,2,1:T(8,128)(2,1)S(1)} %bitcast.265, bf16[512,12,64]{0,2,1:T(8,128)(2,1)S(1)} %copy-done.67, bf16[32,12,64]{0,2,1:T(8,128)(2,1)S(1)} %copy-done.90), kind=kOutput, calls=%fused_computation.1 | convolution fusion | flops 621668352 | bytes 39419904 | tf_op jit(solution)/shard_map/qhd,khd->hqk/dot_general | solution.py:103
  579.4 12.9 multiply_convert_fusion
  592.3 3.6 copy-done.3
  595.8 4.4 multiply_bitcast_fusion
  600.3 12.7 slice.604
  613.0 30.1 %reshape.582 = bf16[12,376832]{1,0:T(8,128)(2,1)} reshape(bf16[12,512,736]{2,1,0:T(8,128)(2,1)} %slice.604) | data formatting | bytes 18087936 | tf_op jit(solution)/shard_map/transpose(jvp())/reshape | solution.py:36
  643.1 10.7 pad.86
  653.8 33.4 %reshape.583 = bf16[12,512,737]{2,1,0:T(8,128)(2,1)} reshape(bf16[12,377344]{1,0:T(8,128)(2,1)} %pad.86) | data formatting | bytes 18112512 | tf_op jit(solution)/shard_map/transpose(jvp())/reshape | solution.py:35
  687.3 4.9 fusion.26
  692.2 4.7 fusion.24
  699.2 9.8 fusion.48
  709.0 16.0 %multiply_reduce_fusion.1 = (f32[12,512]{1,0:T(8,128)S(1)}, f32[12,512,768]{2,1,0:T(8,128)}) fusion(f32[12,512,768]{2,1,0:T(8,128)} %get-tuple-element.283, f32[12,512]{1,0:T(8,128)S(1)} %copy-done.102, bf16[512,12,64]{0,2,1:T(8,128)(2,1)S(1)} %bitcast.267, bf16[512,12,64]{0,2,1:T(8,128)(2,1)S(1)} %copy-done.65, bf16[32,12,64]{0,2,1:T(8,128)(2,1)S(1)} %copy-done.88), kind=kOutput, calls=%fused_computation.4 | convolution fusion | flops 621668352 | bytes 39419904 | tf_op jit(solution)/shard_map/qhd,khd->hqk/dot_general | solution.py:103
  725.0 12.9 multiply_convert_fusion.1
  737.9 3.6 copy-done.2
  744.7 12.7 slice.590
  757.4 4.7 convolution_add_fusion.3
  762.1 29.9 %reshape.580 = bf16[12,376832]{1,0:T(8,128)(2,1)} reshape(bf16[12,512,736]{2,1,0:T(8,128)(2,1)} %slice.590) | data formatting | bytes 18087936 | tf_op jit(solution)/shard_map/transpose(jvp())/reshape | solution.py:36
  792.0 10.7 pad.84
  802.7 33.4 %reshape.581 = bf16[12,512,737]{2,1,0:T(8,128)(2,1)} reshape(bf16[12,377344]{1,0:T(8,128)(2,1)} %pad.84) | data formatting | bytes 18112512 | tf_op jit(solution)/shard_map/transpose(jvp())/reshape | solution.py:35
  836.2 4.9 fusion.77
  865.4 7.7 fusion.68
  883.5 3.6 fusion.28
  896.9 5.7 convolution_add_fusion
  904.1 6.3 fusion.175
  910.4 7.0 convolution_add_fusion.2
  918.3 6.3 fusion.164
  924.6 6.7 convolution_add_fusion.1
  935.0 5.7 fusion.179
  942.4 4.4 fusion.178
  948.9 38.0 %all-reduce.30 = (f32[768]{0:T(1024)S(1)}, f32[768]{0:T(1024)S(1)}, f32[1536]{0:T(1024)S(1)}, f32[768]{0:T(1024)S(1)}, f32[768]{0:T(1024)S(1)}, /*index=5*/f32[7...) all-reduce(f32[768]{0:T(1024)S(1)} %add.452, ...), channel_id=2, replica_groups=mesh['wide'=8,'narrow'=4] {'wide','narrow'}, use_global_device_ids=true, to_apply=%region_30.31.clone | all-reduce | flops 9216 | bytes 73728
  991.6 6.7 select_convert_fusion
  998.4 5.3 select_convert_fusion.1
  1009.0 28.5 %reduce-scatter.10.cloned.1.call-done = f32[24,768]{1,0:T(8,128)} async-done(((f32[768,768]{1,0:T(8,128)}), f32[24,768]{1,0:T(8,128)}) %reduce-scatter.10.cloned.1.call-update) | async-done | bytes 73744 | tf_op jit(solution)/shard_map/reduce_scatter | solution.py:319
  1037.5 125.4 %reduce-scatter.6.cloned.1.call-done = f32[24,2304]{1,0:T(8,128)} async-done(((f32[768,2304]{1,0:T(8,128)}), f32[24,2304]{1,0:T(8,128)}) %reduce-scatter.6.cloned.1.call-update) | async-done | bytes 221200 | tf_op jit(solution)/shard_map/reduce_scatter | solution.py:316
  1162.9 141.4 %reduce-scatter.12.cloned.1.call-done = f32[24,3072]{1,0:T(8,128)} async-done(((f32[768,3072]{1,0:T(8,128)}), f32[24,3072]{1,0:T(8,128)}) %reduce-scatter.12.cloned.1.call-update) | async-done | bytes 294928 | tf_op jit(solution)/shard_map/reduce_scatter | solution.py:329
  1304.3 142.1 %reduce-scatter.14.cloned.1.call-done = f32[96,768]{1,0:T(8,128)} async-done(((f32[3072,768]{1,0:T(8,128)}), f32[96,768]{1,0:T(8,128)}) %reduce-scatter.14.cloned.1.call-update) | async-done | bytes 294928 | tf_op jit(solution)/shard_map/reduce_scatter | solution.py:331
  (541 shorter events, 166.6 us)
Async XLA Ops:
  7.2 141.6 %all-gather.5.cloned.1.call-start = ((), (), s32[]{:S(2)}) async-start(), calls=%async_computation.5 | async-start | bytes 3649536 | tf_op jit(solution)/shard_map/all_gather | solution.py:366
  7.9 310.4 %all-gather.7.cloned.1.call-start = ((), (), s32[]{:S(2)}) async-start(), calls=%async_computation.6 | async-start | bytes 1216512 | tf_op jit(solution)/shard_map/all_gather | solution.py:369
  8.7 444.3 %all-gather.9.cloned.1.call-start = ((), (), s32[]{:S(2)}) async-start(), calls=%async_computation.7 | async-start | bytes 4866048 | tf_op jit(solution)/shard_map/all_gather | solution.py:375
  9.4 486.1 %all-gather.11.cloned.1.call-start = ((), (), s32[]{:S(2)}) async-start(), calls=%async_computation.8 | async-start | bytes 4866048 | tf_op jit(solution)/shard_map/all_gather | solution.py:377
  10.0 999.0 %reduce-scatter.8.cloned.1.call-start = ((), (), s32[]{:S(2)}) async-start(), calls=%async_computation.10 | async-start | bytes 811008 | tf_op jit(solution)/shard_map/reduce_scatter | solution.py:318
  16.1 158.9 %copy-start.138 = (pred[544]{0:T(1024)(128)(4,1)}, pred[544]{0:T(1024)(128)(4,1)S(1)}, u32[]{:S(2)}) copy-start(pred[544]{0:T(1024)(128)(4,1)S(1)} %pad_add_fusion.3) | copy-start | bytes 1636
  65.9 98.6 %copy-start.120 = (f32[768]{0:T(1024)}, f32[768]{0:T(1024)S(1)}, u32[]{:S(2)}) copy-start(f32[768]{0:T(1024)S(1)} %convert_element_type.220) | copy-start | bytes 9220
  66.5 82.3 %copy-start.154 = (f32[768]{0:T(1024)}, f32[768]{0:T(1024)S(1)}, u32[]{:S(2)}) copy-start(f32[768]{0:T(1024)S(1)} %convert_element_type.221) | copy-start | bytes 9220
  69.1 74.6 %copy-start.78 = (bf16[32,768]{1,0:T(8,128)(2,1)}, bf16[32,768]{1,0:T(8,128)(2,1)S(1)}, u32[]{:S(2)}) copy-start(bf16[32,768]{1,0:T(8,128)(2,1)S(1)} %get-tuple-element.259) | copy-start | bytes 147460
  69.1 79.7 %copy-start.93 = (bf16[32,768]{1,0:T(8,128)(2,1)}, bf16[32,768]{1,0:T(8,128)(2,1)S(1)}, u32[]{:S(2)}) copy-start(bf16[32,768]{1,0:T(8,128)(2,1)S(1)} %get-tuple-element.258) | copy-start | bytes 147460
  141.4 43.8 %copy-start.34 = (bf16[768,169]{1,0:T(8,128)(2,1)}, bf16[768,169]{1,0:T(8,128)(2,1)S(1)}, u32[]{:S(2)}) copy-start(bf16[768,169]{1,0:T(8,128)(2,1)S(1)} %all_gather.50) | copy-start | bytes 778756
  143.3 21.3 %copy-start.122 = (f32[544]{0:T(1024)}, f32[544]{0:T(1024)S(1)}, u32[]{:S(2)}) copy-start(f32[544]{0:T(1024)S(1)} %broadcast_multiply_fusion.1) | copy-start | bytes 6532
  143.8 20.7 %copy-start.124 = (f32[544]{0:T(1024)}, f32[544]{0:T(1024)S(1)}, u32[]{:S(2)}) copy-start(f32[544]{0:T(1024)S(1)} %fusion.131) | copy-start | bytes 6532
  158.6 123.0 %copy-start.4 = (bf16[544,2304]{0,1:T(8,128)(2,1)}, bf16[544,2304]{0,1:T(8,128)(2,1)S(1)}, u32[]{:S(2)}) copy-start(bf16[544,2304]{0,1:T(8,128)(2,1)S(1)} %copy.89) | copy-start | bytes 7520260
  159.4 122.1 %copy-start.71 = (bf16[32,12,64]{0,2,1:T(8,128)(2,1)}, bf16[32,12,64]{0,2,1:T(8,128)(2,1)S(1)}, u32[]{:S(2)}) copy-start(bf16[32,12,64]{0,2,1:T(8,128)(2,1)S(1)} %get-tuple-element.243) | copy-start | bytes 147460
  251.4 30.2 %copy-start.76 = (pred[512,768]{1,0:T(8,128)(4,1)S(1)}, pred[512,768]{1,0:T(8,128)(4,1)}, u32[]{:S(2)}) copy-start(pred[512,768]{1,0:T(8,128)(4,1)} %get-tuple-element.308) | copy-start | bytes 1179652
  299.5 8.4 copy-start.108
  299.5 11.9 copy-start
  311.4 6.9 copy-start.27
  311.4 6.9 copy-start.94
  311.4 6.9 copy-start.157
  321.0 201.3 %copy-start.106 = (f32[544]{0:T(1024)}, f32[544]{0:T(1024)S(1)}, u32[]{:S(2)}) copy-start(f32[544]{0:T(1024)S(1)} %broadcast_multiply_fusion.2) | copy-start | bytes 6532
  322.5 12.6 copy-start.134
  322.5 199.8 %copy-start.109 = (f32[544]{0:T(1024)}, f32[544]{0:T(1024)S(1)}, u32[]{:S(2)}) copy-start(f32[544]{0:T(1024)S(1)} %fusion.130) | copy-start | bytes 6532
  380.6 30.2 %copy-start.43 = (bf16[512,12,64]{0,2,1:T(8,128)(2,1)S(1)}, bf16[512,12,64]{0,2,1:T(8,128)(2,1)}, u32[]{:S(2)}) copy-start(bf16[512,12,64]{0,2,1:T(8,128)(2,1)} %get-tuple-element.249) | copy-start | bytes 2359300
  380.6 30.2 %copy-start.73 = (bf16[32,12,64]{0,2,1:T(8,128)(2,1)S(1)}, bf16[32,12,64]{0,2,1:T(8,128)(2,1)}, u32[]{:S(2)}) copy-start(bf16[32,12,64]{0,2,1:T(8,128)(2,1)} %get-tuple-element.247) | copy-start | bytes 147460
  380.6 30.2 %copy-start.75 = (pred[512,768]{1,0:T(8,128)(4,1)S(1)}, pred[512,768]{1,0:T(8,128)(4,1)}, u32[]{:S(2)}) copy-start(pred[512,768]{1,0:T(8,128)(4,1)} %get-tuple-element.309) | copy-start | bytes 1179652
  410.8 27.1 %copy-start.66 = (bf16[512,12,64]{0,2,1:T(8,128)(2,1)S(1)}, bf16[512,12,64]{0,2,1:T(8,128)(2,1)}, u32[]{:S(2)}) copy-start(bf16[512,12,64]{0,2,1:T(8,128)(2,1)} %get-tuple-element.248) | copy-start | bytes 2359300
  410.8 27.1 %copy-start.89 = (bf16[32,12,64]{0,2,1:T(8,128)(2,1)S(1)}, bf16[32,12,64]{0,2,1:T(8,128)(2,1)}, u32[]{:S(2)}) copy-start(bf16[32,12,64]{0,2,1:T(8,128)(2,1)} %get-tuple-element.246) | copy-start | bytes 147460
  428.9 11.8 copy-start.1
  440.7 6.7 copy-start.96
  440.7 8.3 copy-start.14
  440.7 8.3 copy-start.80
  451.7 70.6 %copy-start.115 = (f32[544]{0:T(1024)}, f32[544]{0:T(1024)S(1)}, u32[]{:S(2)}) copy-start(f32[544]{0:T(1024)S(1)} %broadcast_multiply_fusion) | copy-start | bytes 6532
  452.9 69.5 %copy-start.118 = (f32[544]{0:T(1024)}, f32[544]{0:T(1024)S(1)}, u32[]{:S(2)}) copy-start(f32[544]{0:T(1024)S(1)} %fusion.132) | copy-start | bytes 6532
  452.9 8.3 copy-start.19
  452.9 8.3 copy-start.149
  453.0 8.2 copy-start.161
  461.2 34.3 %copy-start.29 = (bf16[512,768]{1,0:T(8,128)(2,1)S(1)}, bf16[512,768]{1,0:T(8,128)(2,1)}, u32[]{:S(2)}) copy-start(bf16[512,768]{1,0:T(8,128)(2,1)} %get-tuple-element.251) | copy-start | bytes 2359300
  461.2 34.3 %copy-start.91 = (bf16[32,768]{1,0:T(8,128)(2,1)S(1)}, bf16[32,768]{1,0:T(8,128)(2,1)}, u32[]{:S(2)}) copy-start(bf16[32,768]{1,0:T(8,128)(2,1)} %get-tuple-element.257) | copy-start | bytes 147460
  461.2 34.3 %copy-start.139 = (pred[544]{0:T(1024)(128)(4,1)S(1)}, pred[544]{0:T(1024)(128)(4,1)}, u32[]{:S(2)}) copy-start(pred[544]{0:T(1024)(128)(4,1)} %copy-done.138) | copy-start | bytes 1636
  495.5 9.9 copy-start.162
  509.2 9.1 copy-start.22
  553.2 10.0 copy-start.40
  553.2 10.0 copy-start.67
  553.2 10.0 copy-start.90
  692.2 7.0 copy-start.102
  699.2 9.8 copy-start.41
  699.2 9.9 copy-start.65
  699.2 9.9 copy-start.88
  841.1 196.4 %reduce-scatter.10.cloned.1.call-start = ((), (), s32[]{:S(2)}) async-start(), calls=%async_computation.11 | async-start | bytes 2433024 | tf_op jit(solution)/shard_map/reduce_scatter | solution.py:319
  841.2 6.9 copy-start.39
  873.1 289.8 %reduce-scatter.6.cloned.1.call-start = ((), (), s32[]{:S(2)}) async-start(), calls=%async_computation.9 | async-start | bytes 7299072 | tf_op jit(solution)/shard_map/reduce_scatter | solution.py:316
  873.1 6.9 copy-start.54
  877.4 9.7 slice-start
  880.0 7.1 slice-start.1
  902.6 7.7 copy-start.116
  902.6 7.7 copy-start.119
  902.6 401.6 %reduce-scatter.12.cloned.1.call-start = ((), (), s32[]{:S(2)}) async-start(), calls=%async_computation.12 | async-start | bytes 9732096 | tf_op jit(solution)/shard_map/reduce_scatter | solution.py:329
  917.5 528.9 %reduce-scatter.14.cloned.1.call-start = ((), (), s32[]{:S(2)}) async-start(), calls=%async_computation.13 | async-start | bytes 9732096 | tf_op jit(solution)/shard_map/reduce_scatter | solution.py:331
  935.0 6.7 copy-start.69
  935.0 6.7 copy-start.164
  946.8 44.8 %copy-start.158 = (f32[768]{0:T(1024)S(1)}, f32[768]{0:T(1024)}, u32[]{:S(2)}) copy-start(f32[768]{0:T(1024)} %convert_element_type.234) | copy-start | bytes 9220
  991.6 6.8 copy-start.167
  (117 other events, 373.5 us)
Sparse Core Ops, SparseCore 0:
  10.8 63.4 all-gather.4
  77.1 52.9 all-gather.6
  132.9 62.5 all-gather.8
  198.2 62.3 all-gather.10
  841.2 92.4 reduce-scatter.7
  939.4 97.9 reduce-scatter.9
  1044.7 118.1 reduce-scatter.5
  1169.4 134.8 reduce-scatter.11
  1311.7 134.5 reduce-scatter.13
where the time goes:
time: 1460 us; the launch traced here: 1450 us
  waiting for transfers between devices  440 us (30%)
  local copies, waits for them, and re-layouts  440 us (30%)
  matrix products  313 us (21%)
  blocking collectives  152 us (10%)
  other arithmetic  89.3 us (6%)
  between operations  17.7 us (1%)
    reduce_scatter x1, waiting for transfers between devices, sum_ffn(): lax.psum_scatter(ffn_terms[4], ('wide', 'narrow'), scatter_dimension=0, t...  142 us
    reduce_scatter x1, waiting for transfers between devices, sum_ffn(): lax.psum_scatter(ffn_terms[2], ('wide', 'narrow'), scatter_dimension=0, t...  141 us
    reduce_scatter x1, waiting for transfers between devices, sum_attn(): lax.psum_scatter(attn_terms[2], ('wide', 'narrow'), scatter_dimension=0,...  125 us
    reshape x4, local copies, waits for them, and re-layouts, skew_rows(): placed.reshape(head_count, BLOCK * (win_cols + 1))[:, :BLOCK * win_cols]  125 us
    reshape x4, local copies, waits for them, and re-layouts, skew_rows(): return flat_rows.reshape(head_count, BLOCK, win_cols)  120 us
    unnamed x2, blocking collectives  81.1 us
    all_gather x1, blocking collectives, body(): lax.all_gather(rel_embed, ('wide', 'narrow'), axis=0, tiled=True)  70.8 us
    unnamed x367, local copies, waits for them, and re-layouts  40.8 us
  transfers between devices with their start and end apart: 9, of which 4 were waited for; matrix products, arithmetic and copies ran while one was open for 33% of the time, Pallas kernels for 0%

commit v1 on v0

v1 whole, which is shorter than its diff:
```python
import functools
import jax
import jax.numpy as jnp
from jax import lax
from jax.experimental import pallas as pl
from jax.experimental.pallas import tpu as pltpu
from jax.sharding import PartitionSpec as P

HEAD_DIM = 64
RADIUS = 84
STRIDE = 16
SEQ = 512
GLOB = 32
RELS = 169
T = GLOB + SEQ
D = 768
FF = 3072
PAIRS = 6
LABELS = 256
LEAD = 4
BACK_LEAD = 3
EPS = 1e-06
NEG = -1e30
F32 = jnp.float32
BF16 = jnp.bfloat16
VMEM_LIMIT = 56 << 20
WINDOWS = ((0, 0, 256, 328, 0), (0, 0, 384, 72, 0), (1, 160, 384, 8, 352), (1, 288, 256, 8, 224))
OFFSETS = (0, 256, 640, 1024)
P_COLS = 1280
NN = (((1,), (0,)), ((), ()))
NT = (((1,), (1,)), ((), ()))
TN = (((0,), (0,)), ((), ()))


def dot(a, b, dims=NN):
    return lax.dot_general(a, b, dims, preferred_element_type=F32)


def params(*sem):
    return pltpu.CompilerParams(vmem_limit_bytes=VMEM_LIMIT, dimension_semantics=sem or None)


def iota(shape, dim):
    return lax.broadcasted_iota(jnp.int32, shape, dim)


def live_mask(length, cols):
    row = iota((T, cols), 0)
    glob_count = (length + STRIDE - 1) // STRIDE
    return row < jnp.where(row < GLOB, glob_count, length + GLOB)


def load_rows(pieces, pos_ref, lines, dst, sems, first_col):
    rows = dst.shape[0] // lines
    cols = dst.shape[1]
    copies = []
    k = 0
    for piece in pieces:
        for i in range(piece.shape[0] // rows):
            start = pl.multiple_of(pos_ref[k] * rows, 16)
            copies.append(
                pltpu.make_async_copy(
                    piece.at[pl.ds(i * rows, rows), pl.ds(first_col, cols)],
                    dst.at[pl.ds(start, rows), :],
                    sems.at[k],
                )
            )
            k += 1
    for copy in copies:
        copy.start()
    return copies


def project_kernel(lines, n_pieces, first_col, first_rel, pos_ref, hid_ref, gain_ref, bias_ref, full_bias_ref, *rest):
    pieces = rest[:n_pieces]
    normed_ref, proj_ref, rel_ref, relt_ref, w_s, sems = rest[n_pieces:]

    @pl.when(pl.program_id(0) == 0)
    def _():
        copies = load_rows(pieces, pos_ref, lines, w_s, sems.at[0], first_col)
        copies += load_rows(pieces, pos_ref, lines, rel_ref, sems.at[1], first_rel)
        for copy in copies:
            copy.wait()
        turned = rel_ref[...].astype(F32).T
        drop = LEAD - BACK_LEAD
        turned = jnp.concatenate([turned[drop:], turned[:drop]], axis=0)
        label = iota((LABELS, D), 0) - BACK_LEAD
        relt_ref[...] = jnp.where((label >= 0) & (label < RELS), turned, 0.0).astype(BF16)

    x = hid_ref[...].astype(F32)
    mean = jnp.mean(x, axis=1, keepdims=True)
    cen = x - mean
    var = jnp.mean(cen * cen, axis=1, keepdims=True)
    normed_ref[...] = (cen * lax.rsqrt(var + EPS) * gain_ref[...] + bias_ref[...]).astype(BF16)

    def step(j, _):
        col = pl.ds(pl.multiple_of(j * 256, 256), 256)
        proj_ref[:, col] = (dot(normed_ref[...], w_s[:, col]) + full_bias_ref[:, col]).astype(BF16)
        return 0

    lax.fori_loop(0, proj_ref.shape[1] // 256, step, 0)


def project(pos, hid, gain, bias, full_bias, pieces, first_col, first_rel):
    rows = hid.shape[0]
    n = len(pieces)
    lines = pos.shape[0]
    cols = full_bias.shape[1]
    spec = pl.BlockSpec((T, D), lambda s, *_: (s, 0))
    vec = lambda c: pl.BlockSpec((1, c), lambda s, *_: (0, 0))
    return pl.pallas_call(
        functools.partial(project_kernel, lines, n, first_col, first_rel),
        grid_spec=pltpu.PrefetchScalarGridSpec(
            num_scalar_prefetch=1,
            grid=(rows // T,),
            in_specs=[spec, vec(D), vec(D), vec(cols)] + [pl.BlockSpec(memory_space=pl.ANY)] * n,
            out_specs=[
                spec,
                pl.BlockSpec((T, cols), lambda s, *_: (s, 0)),
                pl.BlockSpec((D, LABELS), lambda s, *_: (0, 0)),
                pl.BlockSpec((LABELS, D), lambda s, *_: (0, 0)),
            ],
            scratch_shapes=[pltpu.VMEM((D, cols), BF16), pltpu.SemaphoreType.DMA((2, lines))],
        ),
        out_shape=[
            jax.ShapeDtypeStruct((rows, D), BF16),
            jax.ShapeDtypeStruct((rows, cols), BF16),
            jax.ShapeDtypeStruct((D, LABELS), BF16),
            jax.ShapeDtypeStruct((LABELS, D), BF16),
        ],
        compiler_params=params(),
        cost_estimate=pl.CostEstimate(flops=4 * rows * D * cols, bytes_accessed=12 << 20, transcendentals=0),
        name="project",
    )(pos, hid, gain, bias, full_bias, *pieces)


def flip_matrix():
    return (iota((128, 128), 0) + iota((128, 128), 1) == 127).astype(F32).astype(BF16)


def attend_kernel(len_ref, q_ref, k_ref, v_ref, rel_ref, mix_ref, p_ref, pg_ref, k_s, v_s):
    length = len_ref[pl.program_id(0)]
    live = live_mask(length, 128)
    lane = iota((T, 128), 1)
    q = q_ref[...].astype(F32) * 0.125
    k = k_ref[...].astype(F32)
    v = v_ref[...].astype(F32)
    rel = rel_ref[...].astype(F32)
    rel_row = iota((128, LABELS), 0)
    label = iota((128, LABELS), 1)
    outside = (label < LEAD) | (label >= LEAD + RELS)
    flip = flip_matrix()
    pad_tile = jnp.full((128, 128), NEG, F32)
    col = iota((128, 128), 1)
    out = [jnp.zeros((GLOB, 128), F32)] + [jnp.zeros((128, 128), F32) for _ in range(4)]
    for par in range(2):
        own = (lane // 64) == par
        flag = 64 * (1 - par)
        km = jnp.where(own, k, jnp.where((lane == flag) & ~live, NEG, 0.0)).astype(BF16)
        qm = jnp.where(own, q, jnp.where(lane == flag, 1.0, 0.0)).astype(BF16)
        vm = jnp.where(own, v, 0.0).astype(BF16)
        relm = jnp.where(
            (rel_row // 64) == par, rel, jnp.where((rel_row == flag) & outside, NEG, 0.0)
        ).astype(BF16)
        for s, m in ((k_s, km), (v_s, vm)):
            s[0] = m
            s[1, :SEQ] = m[GLOB:]
            s[1, SEQ:] = m[:GLOB]
        scores = dot(qm[:GLOB], km, NT)
        top = jnp.max(scores, axis=1, keepdims=True)
        e = jnp.exp(scores - top)
        p = (e * (1.0 / jnp.sum(e, axis=1, keepdims=True))).astype(BF16)
        pg_ref[0, 0, par] = p
        out[0] = out[0] + dot(p, vm)
        for b, (arr, first, width, shift, glob_at) in enumerate(WINDOWS):
            qb = qm[GLOB + 128 * b : GLOB + 128 * (b + 1)]
            scores = dot(qb, k_s[arr, first : first + width], NT)
            bias = dot(qb, relm)
            bias = pltpu.roll(
                jnp.concatenate([bias, pad_tile], axis=1), shift, 1, stride=1, stride_axis=0
            )
            tiles = [bias[:, 128 * i : 128 * (i + 1)] for i in range(width // 128)]
            tile, at = glob_at // 128, glob_at % 128
            tiles[tile] = jnp.where((col >= at) & (col < at + GLOB), 0.0, tiles[tile])
            scores = scores + jnp.concatenate(tiles, axis=1)
            top = jnp.max(scores, axis=1, keepdims=True)
            e = jnp.exp(scores - top)
            p = (e * (1.0 / jnp.sum(e, axis=1, keepdims=True))).astype(BF16)
            out[b + 1] = out[b + 1] + dot(p, v_s[arr, first : first + width])
            p_ref[0, 0, par, :, OFFSETS[b] : OFFSETS[b] + width] = dot(flip, p).astype(BF16)
    mix_ref[:GLOB] = out[0].astype(BF16)
    for b in range(4):
        mix_ref[GLOB + 128 * b : GLOB + 128 * (b + 1)] = out[b + 1].astype(BF16)


def attend(lengths, proj, rel, first_pair, n_pairs):
    rows = proj.shape[0]
    seqs = rows // T

    def part(n):
        return pl.BlockSpec((T, 128), lambda s, p, *_: (s, n * PAIRS + first_pair + p))

    return pl.pallas_call(
        attend_kernel,
        grid_spec=pltpu.PrefetchScalarGridSpec(
            num_scalar_prefetch=1,
            grid=(seqs, n_pairs),
            in_specs=[part(0), part(1), part(2), pl.BlockSpec((128, LABELS), lambda s, p, *_: (first_pair + p, 0))],
            out_specs=[
                pl.BlockSpec((T, 128), lambda s, p, *_: (s, p)),
                pl.BlockSpec((1, 1, 2, 128, P_COLS), lambda s, p, *_: (s, p, 0, 0, 0)),
                pl.BlockSpec((1, 1, 2, GLOB, T), lambda s, p, *_: (s, p, 0, 0, 0)),
            ],
            scratch_shapes=[pltpu.VMEM((2, T, 128), BF16)] * 2,
        ),
        out_shape=[
            jax.ShapeDtypeStruct((rows, n_pairs * 128), BF16),
            jax.ShapeDtypeStruct((seqs, n_pairs, 2, 128, P_COLS), BF16),
            jax.ShapeDtypeStruct((seqs, n_pairs, 2, GLOB, T), BF16),
        ],
        compiler_params=params(),
        cost_estimate=pl.CostEstimate(flops=n_pairs * 1600 << 20, bytes_accessed=n_pairs << 21, transcendentals=0),
        name="attend",
    )(lengths, proj, proj, proj, rel)


def attend_back_kernel(q_ref, k_ref, v_ref, relt_ref, do_ref, o_ref, p_ref, pg_ref, gq_ref, gk_ref, gv_ref, grel_ref, gk_s, gv_s, k_s, v_s, kt_s):
    s = pl.program_id(1)
    lane = iota((T, 128), 1)
    lane_b = iota((128, 128), 1)
    flip = flip_matrix()
    q = q_ref[...]
    k = k_ref[...]
    v = v_ref[...]
    do = do_ref[...]
    kf = k.astype(F32)
    v_s[0] = v
    v_s[1, :SEQ] = v[GLOB:]
    v_s[1, SEQ:] = v[:GLOB]
    for par in range(2):
        km = jnp.where((lane // 64) == par, kf, 0.0).astype(BF16)
        k_s[par, 0] = km
        k_s[par, 1, :SEQ] = km[GLOB:]
        k_s[par, 1, SEQ:] = km[:GLOB]

    @pl.when(s == 0)
    def _():
        grel_ref[...] = jnp.zeros_like(grel_ref)

    relt = relt_ref[...].astype(F32)
    rel_lane = iota((LABELS, 128), 1)
    reltm = [jnp.where((rel_lane // 64) == par, relt, 0.0).astype(BF16) for par in range(2)]
    qg_t = jnp.concatenate([q[:GLOB].astype(F32), jnp.zeros((96, 128), F32)], axis=0).T.astype(BF16)[:, :GLOB]
    dog_t = jnp.concatenate([do[:GLOB].astype(F32), jnp.zeros((96, 128), F32)], axis=0).T.astype(BF16)[:, :GLOB]
    do_g = do[:GLOB].astype(F32)
    prod = do_g * o_ref[:GLOB].astype(F32)
    gq = jnp.zeros((GLOB, 128), F32)
    gk_t, gv_t = [], []
    for par in range(2):
        own = (lane_b[:GLOB] // 64) == par
        dom = jnp.where(own, do_g, 0.0).astype(BF16)
        centre = jnp.sum(jnp.where(own, prod, 0.0), axis=1, keepdims=True)
        p = pg_ref[0, 0, par]
        ds = (p.astype(F32) * (dot(dom, v, NT) - centre)).astype(BF16)
        gq = gq + dot(ds, k_s[par, 0])
        gk_t.append(dot(qg_t[64 * par : 64 * par + 64], ds))
        gv_t.append(dot(dog_t[64 * par : 64 * par + 64], p))
    gq_ref[:GLOB] = (gq * 0.125).astype(BF16)
    kt_s[:, :T] = jnp.concatenate(gk_t, axis=0)
    kt_s[:, T:] = jnp.zeros((128, 640 - T), F32)
    gk_s[...] = kt_s[...].T[:T]
    kt_s[:, :T] = jnp.concatenate(gv_t, axis=0)
    gv_s[...] = kt_s[...].T[:T]
    for b, (arr, first, width, shift, glob_at) in enumerate(WINDOWS):
        rows = slice(GLOB + 128 * b, GLOB + 128 * (b + 1))
        qb = dot(flip, q[rows])
        dob = dot(flip, do[rows])
        prod = dob * dot(flip, o_ref[rows])
        qb_t = qb.T.astype(BF16)
        dob_t = dob.T.astype(BF16)
        v_win = v_s[arr, first : first + width]
        gq = jnp.zeros((128, 128), F32)
        gk_t, gv_t, grel = [], [], []
        for par in range(2):
            own = (lane_b // 64) == par
            dom = jnp.where(own, dob, 0.0).astype(BF16)
            centre = jnp.sum(jnp.where(own, prod, 0.0), axis=1, keepdims=True)
            p = p_ref[0, 0, par, :, OFFSETS[b] : OFFSETS[b] + width]
            ds = p.astype(F32) * (dot(dom, v_win, NT) - centre)
            ds16 = ds.astype(BF16)
            gq = gq + dot(ds16, k_s[par, arr, first : first + width])
            gk_t.append(dot(qb_t[64 * par : 64 * par + 64], ds16))
            gv_t.append(dot(dob_t[64 * par : 64 * par + 64], p))
            tiles = [ds[:, 128 * i : 128 * (i + 1)] for i in range(width // 128)]
            tile, at = glob_at // 128, glob_at % 128
            tiles[tile] = jnp.where((lane_b >= at) & (lane_b < at + GLOB), 0.0, tiles[tile])
            if width < 384:
                tiles.append(jnp.zeros((128, 128), F32))
            back = (256 - shift) % 384
            lab = pltpu.roll(jnp.concatenate(tiles, axis=1), back, 1, stride=1, stride_axis=0)
            lab = lab[:, :LABELS].astype(BF16)
            gq = gq + dot(lab, reltm[par])
            grel.append(dot(qb_t[64 * par : 64 * par + 64], lab))
        gq_ref[rows] = dot(flip, (gq * 0.125).astype(BF16)).astype(BF16)
        gk_b = jnp.concatenate(gk_t, axis=0).T
        gv_b = jnp.concatenate(gv_t, axis=0).T
        for acc, part in ((gk_s, gk_b), (gv_s, gv_b)):
            if arr == 0:
                acc[first : first + width] += part
            else:
                acc[GLOB + first : T] += part[: width - GLOB]
                acc[:GLOB] += part[width - GLOB :]
        grel_ref[...] += jnp.concatenate(grel, axis=0) * 0.125
    gk_ref[...] = (gk_s[...] * 0.125).astype(BF16)
    gv_ref[...] = gv_s[...].astype(BF16)


def attend_back(proj, relt, gmixed, mixed, p, pg, first_pair, n_pairs, mix_pair):
    rows = proj.shape[0]
    seqs = rows // T

    def part(n, at):
        return pl.BlockSpec((T, 128), lambda p, s: (s, n * PAIRS + at + p))

    grad = pl.BlockSpec((T, 128), lambda p, s: (s, p))
    return pl.pallas_call(
        attend_back_kernel,
        grid=(n_pairs, seqs),
        in_specs=[
            part(0, first_pair),
            part(1, first_pair),
            part(2, first_pair),
            pl.BlockSpec((LABELS, 128), lambda p, s: (0, first_pair + p)),
            part(0, first_pair),
            part(0, mix_pair),
            pl.BlockSpec((1, 1, 2, 128, P_COLS), lambda p, s: (s, p, 0, 0, 0)),
            pl.BlockSpec((1, 1, 2, GLOB, T), lambda p, s: (s, p, 0, 0, 0)),
        ],
        out_specs=[grad, grad, grad, pl.BlockSpec((128, LABELS), lambda p, s: (p, 0))],
        scratch_shapes=[
            pltpu.VMEM((T, 128), F32),
            pltpu.VMEM((T, 128), F32),
            pltpu.VMEM((2, 2, T, 128), BF16),
            pltpu.VMEM((2, T, 128), BF16),
            pltpu.VMEM((128, 640), F32),
        ],
        out_shape=[jax.ShapeDtypeStruct((rows, n_pairs * 128), BF16)] * 3
        + [jax.ShapeDtypeStruct((n_pairs * 128, LABELS), F32)],
        compiler_params=params(),
        cost_estimate=pl.CostEstimate(flops=n_pairs * 3200 << 20, bytes_accessed=n_pairs << 21, transcendentals=0),
        name="attend_back",
    )(proj, proj, proj, relt, gmixed, mixed, p, pg)


def norm_stats(x):
    cen = x - jnp.mean(x, axis=1, keepdims=True)
    rstd = lax.rsqrt(jnp.mean(cen * cen, axis=1, keepdims=True) + EPS)
    return cen * rstd, rstd


def mix_out_kernel(lines, n_pieces, first_col, n_mix, pos_ref, len_ref, hid_ref, bias_ref, gain2_ref, bias2_ref, cot_ref, *rest):
    mixed = rest[:n_mix]
    pieces = rest[n_mix : n_mix + n_pieces]
    res_ref, n2_ref, g_ref, w_s, sems = rest[n_mix + n_pieces :]
    s = pl.program_id(0)

    @pl.when(s == 0)
    def _():
        for copy in load_rows(pieces, pos_ref, lines, w_s, sems, first_col):
            copy.wait()

    def step(j, _):
        col = pl.ds(pl.multiple_of(j * 256, 256), 256)
        acc = hid_ref[:, col].astype(F32) + bias_ref[:, col]
        at = 0
        for m in mixed:
            acc = acc + dot(m[...], w_s[at : at + m.shape[1], col])
            at += m.shape[1]
        res_ref[:, col] = acc
        return 0

    lax.fori_loop(0, D // 256, step, 0)
    xhat, _ = norm_stats(res_ref[...])
    n2_ref[...] = (xhat * gain2_ref[...] + bias2_ref[...]).astype(BF16)
    live = live_mask(len_ref[s], D)
    g_ref[...] = jnp.where(live, cot_ref[...].astype(F32), 0.0).astype(BF16)


def mix_out(pos, lengths, hid, bias, gain2, bias2, cot, mixed, pieces, first_col):
    rows = hid.shape[0]
    n = len(pieces)
    lines = pos.shape[0]
    spec = pl.BlockSpec((T, D), lambda s, *_: (s, 0))
    vec = pl.BlockSpec((1, D), lambda s, *_: (0, 0))
    return pl.pallas_call(
        functools.partial(mix_out_kernel, lines, n, first_col, len(mixed)),
        grid_spec=pltpu.PrefetchScalarGridSpec(
            num_scalar_prefetch=2,
            grid=(rows // T,),
            in_specs=[spec, vec, vec, vec, spec]
            + [pl.BlockSpec((T, m.shape[1]), lambda s, *_: (s, 0)) for m in mixed]
            + [pl.BlockSpec(memory_space=pl.ANY)] * n,
            out_specs=[spec, spec, spec],
            scratch_shapes=[pltpu.VMEM((D, D), BF16), pltpu.SemaphoreType.DMA((lines,))],
        ),
        out_shape=[
            jax.ShapeDtypeStruct((rows, D), F32),
            jax.ShapeDtypeStruct((rows, D), BF16),
            jax.ShapeDtypeStruct((rows, D), BF16),
        ],
        compiler_params=params(),
        cost_estimate=pl.CostEstimate(flops=4 * rows * D * D, bytes_accessed=12 << 20, transcendentals=0),
        name="mix_out",
    )(pos, lengths, hid, bias, gain2, bias2, cot, *mixed, *pieces)


def store_rows(src, outs, rows, src_pos_ref, sems, first_col):
    cols = src.shape[1]
    copies = []
    k = 0
    for out in outs:
        for i in range(out.shape[0]):
            start = pl.multiple_of(src_pos_ref[k] * rows, 16)
            copies.append(
                pltpu.make_async_copy(
                    src.at[pl.ds(start, rows), :], out.at[i, :, pl.ds(first_col, cols)], sems.at[k]
                )
            )
            k += 1
    return copies


def gelu_parts(v):
    cdf = 0.5 * (1.0 + lax.erf(v * 0.7071067811865476))
    pdf = jnp.exp(v * v * -0.5) * 0.3989422804014327
    return v * cdf, cdf + v * pdf


def ffn_kernel(lines, n_in, first_in, first_down, n_parts, n_out, pos_ref, out_pos_ref, n2_ref, g_ref, b_ref, *rest):
    pieces = rest[:n_in]
    y_ref, gn2_ref, gb_ref = rest[n_in : n_in + 3]
    outs = rest[n_in + 3 : n_in + 3 + n_out]
    w_in_s, w_down_s, act_s, gpre_s, gw_s, sems, out_sems = rest[n_in + 3 + n_out :]
    part = pl.program_id(0)
    rows = n2_ref.shape[0]
    piece_rows = outs[0].shape[1]

    @pl.when(part == 0)
    def _():
        copies = load_rows(pieces, pos_ref, lines, w_in_s, sems.at[0], first_in)
        copies += load_rows(pieces, pos_ref, lines, w_down_s, sems.at[1], first_down)
        for copy in copies:
            copy.wait()
        y_ref[...] = jnp.zeros_like(y_ref)
        gn2_ref[...] = jnp.zeros_like(gn2_ref)

    cols = pl.ds(pl.multiple_of(part * D, 128), D)
    gb_ref[...] = jnp.zeros_like(gb_ref)
    tile = rows // 4

    def step(t, _):
        at = pl.ds(pl.multiple_of(t * tile, 16), tile)
        for n in range(D // 256):
            c = slice(256 * n, 256 * (n + 1))
            cc = pl.ds(pl.multiple_of(part * D + 256 * n, 128), 256)
            pre = dot(n2_ref[at, :], w_in_s[:, cc]) + b_ref[:, c]
            act, slope = gelu_parts(pre)
            act_s[at, c] = act.astype(BF16)
            gact = dot(g_ref[at, :], w_down_s[c, cols], NT)
            gpre = (gact * slope).astype(BF16)
            gpre_s[at, c] = gpre
            gb_ref[:, c] += jnp.sum(gpre.astype(F32), axis=0, keepdims=True)
        y_ref[at, :] += dot(act_s[at, :], w_down_s[:, cols])
        gn2_ref[at, :] += dot(gpre_s[at, :], w_in_s[:, cols], NT)
        return 0

    lax.fori_loop(0, 4, step, 0)

    def flush(which, first):
        return store_rows(gw_s.at[which], outs, piece_rows, out_pos_ref, out_sems.at[which], first)

    for which, (lhs, rhs) in enumerate(((n2_ref, gpre_s), (act_s, g_ref))):
        for n in range(D // 256):
            c = slice(256 * n, 256 * (n + 1))
            gw_s[which, :, c] = dot(lhs[...], rhs[:, c], TN).astype(BF16)
        for copy in flush(which, pl.multiple_of((which * n_parts + part) * D, 128)):
            copy.start()
    for which in range(2):
        for copy in flush(which, pl.multiple_of((which * n_parts + part) * D, 128)):
            copy.wait()


def ffn(pos, out_pos, n2, g, bias, pieces, first_in, first_down, n_parts, out_groups):
    rows = n2.shape[0]
    n = len(pieces)
    lines = pos.shape[0]
    full = pl.BlockSpec((rows, D), lambda q, *_: (0, 0))
    vec = pl.BlockSpec((1, D), lambda q, *_: (0, q))
    anywhere = pl.BlockSpec(memory_space=pl.ANY)
    return pl.pallas_call(
        functools.partial(ffn_kernel, lines, n, first_in, first_down, n_parts, len(out_groups)),
        grid_spec=pltpu.PrefetchScalarGridSpec(
            num_scalar_prefetch=2,
            grid=(n_parts,),
            in_specs=[full, full, vec] + [anywhere] * n,
            out_specs=[full, full, vec] + [anywhere] * len(out_groups),
            scratch_shapes=[
                pltpu.VMEM((D, n_parts * D), BF16),
                pltpu.VMEM((D, n_parts * D), BF16),
                pltpu.VMEM((rows, D), BF16),
                pltpu.VMEM((rows, D), BF16),
                pltpu.VMEM((2, D, D), BF16),
                pltpu.SemaphoreType.DMA((2, lines)),
                pltpu.SemaphoreType.DMA((2, lines)),
            ],
        ),
        out_shape=[
            jax.ShapeDtypeStruct((rows, D), F32),
            jax.ShapeDtypeStruct((rows, D), F32),
            jax.ShapeDtypeStruct((1, n_parts * D), F32),
        ]
        + [jax.ShapeDtypeStruct((k, D // lines, 2 * n_parts * D), BF16) for k in out_groups],
        compiler_params=params(),
        cost_estimate=pl.CostEstimate(flops=24 * n_parts * rows * D * D, bytes_accessed=30 << 20, transcendentals=0),
        name="ffn",
    )(pos, out_pos, n2, g, bias, *pieces)


def norm_back(grad, xhat, rstd, gain):
    gg = grad * gain
    return rstd * (
        gg - jnp.mean(gg, axis=1, keepdims=True) - xhat * jnp.mean(gg * xhat, axis=1, keepdims=True)
    )


def mid_kernel(lines, n_in, first_col, n_mix, n_part, pos_ref, len_ref, res_ref, g_ref, gain2_ref, down_ref, *rest):
    ys = rest[:n_part]
    gns = rest[n_part : 2 * n_part]
    mixed = rest[2 * n_part : 2 * n_part + n_mix]
    rest = rest[2 * n_part + n_mix :]
    pieces = rest[:n_in]
    long_ref, glob_ref, gres_ref, gmix_ref, small_ref, gw_ref = rest[n_in : n_in + 6]
    w_s, gattn_s, gw_s, sems = rest[n_in + 6 :]
    s = pl.program_id(0)

    @pl.when(s == 0)
    def _():
        for copy in load_rows(pieces, pos_ref, lines, w_s, sems, first_col):
            copy.wait()
        gw_s[...] = jnp.zeros_like(gw_s)
        small_ref[...] = jnp.zeros_like(small_ref)

    live = live_mask(len_ref[s], D)
    res = res_ref[...]
    y = res + down_ref[...]
    gn2 = gns[0][...]
    for ref in ys:
        y = y + ref[...]
    for ref in gns[1:]:
        gn2 = gn2 + ref[...]
    y = jnp.where(live, y, 0.0).astype(BF16)
    glob_ref[0, 0] = y[:GLOB]
    long_ref[0, 0] = y[GLOB:]
    xhat, rstd = norm_stats(res)
    g = g_ref[...].astype(F32)
    gres = g + norm_back(gn2, xhat, rstd, gain2_ref[...])
    gres_ref[...] = gres
    gattn = gres.astype(BF16)
    gattn_s[...] = gattn
    small_ref[0:1] += jnp.sum(gn2 * xhat, axis=0, keepdims=True)
    small_ref[1:2] += jnp.sum(gn2, axis=0, keepdims=True)
    small_ref[2:3] += jnp.sum(gattn.astype(F32), axis=0, keepdims=True)
    small_ref[3:4] += jnp.sum(g, axis=0, keepdims=True)

    for n in range(D // 256):
        c = slice(256 * n, 256 * (n + 1))
        gmix_ref[:, c] = dot(gattn_s[...], w_s[c, :], NT).astype(BF16)
        at = 0
        for m in mixed:
            gw_s[at : at + m.shape[1], c] += dot(m[...], gattn_s[:, c], TN)
            at += m.shape[1]

    @pl.when(s == pl.num_programs(0) - 1)
    def _():
        gw_ref[...] = gw_s[...].astype(BF16)


def mid(pos, lengths, res, g, gain2, down, ys, gns, mixed, pieces, first_col, long_shape, glob_shape):
    rows = res.shape[0]
    n = len(pieces)
    lines = pos.shape[0]
    spec = pl.BlockSpec((T, D), lambda s, *_: (s, 0))
    vec = pl.BlockSpec((1, D), lambda s, *_: (0, 0))
    anywhere = pl.BlockSpec(memory_space=pl.ANY)
    return pl.pallas_call(
        functools.partial(mid_kernel, lines, n, first_col, len(mixed), len(ys)),
        grid_spec=pltpu.PrefetchScalarGridSpec(
            num_scalar_prefetch=2,
            grid=(rows // T,),
            in_specs=[spec, spec, vec, vec]
            + [spec] * (2 * len(ys))
            + [pl.BlockSpec((T, m.shape[1]), lambda s, *_: (s, 0)) for m in mixed]
            + [anywhere] * n,
            out_specs=[
                pl.BlockSpec((1, 1, SEQ, D), lambda s, *_: (s, 0, 0, 0)),
                pl.BlockSpec((1, 1, GLOB, D), lambda s, *_: (s, 0, 0, 0)),
                spec,
                spec,
                pl.BlockSpec((8, D), lambda s, *_: (0, 0)),
                pl.BlockSpec((D, D), lambda s, *_: (0, 0)),
            ],
            scratch_shapes=[
                pltpu.VMEM((D, D), BF16),
                pltpu.VMEM((T, D), BF16),
                pltpu.VMEM((D, D), F32),
                pltpu.SemaphoreType.DMA((lines,)),
            ],
        ),
        out_shape=[
            jax.ShapeDtypeStruct(long_shape, BF16),
            jax.ShapeDtypeStruct(glob_shape, BF16),
            jax.ShapeDtypeStruct((rows, D), F32),
            jax.ShapeDtypeStruct((rows, D), BF16),
            jax.ShapeDtypeStruct((8, D), F32),
            jax.ShapeDtypeStruct((D, D), BF16),
        ],
        compiler_params=params(),
        cost_estimate=pl.CostEstimate(flops=8 * rows * D * D, bytes_accessed=30 << 20, transcendentals=0),
        name="mid",
    )(pos, lengths, res, g, gain2, down, *ys, *gns, *mixed, *pieces)


def weight_kernel(n_rhs, n_out, out_pos_ref, normed_ref, *rest):
    rhs = rest[:n_rhs]
    extra = rest[n_rhs : len(rest) - n_out - 2]
    outs = rest[len(rest) - n_out - 2 : len(rest) - 2]
    gw_s, out_sems = rest[len(rest) - 2 :]
    piece_rows = outs[0].shape[1]
    at = 0
    for ref in rhs:
        for n in range(ref.shape[1] // 128):
            c = slice(128 * n, 128 * (n + 1))
            gw_s[:, at : at + 128] = dot(normed_ref[...], ref[:, c], TN).astype(BF16)
            at += 128
    for ref in extra:
        gw_s[:, at : at + ref.shape[1]] = ref[...].astype(BF16)
        at += ref.shape[1]
    copies = store_rows(gw_s, outs, piece_rows, out_pos_ref, out_sems, 0)
    for copy in copies:
        copy.start()
    for copy in copies:
        copy.wait()


def weight_grad(out_pos, normed, rhs, extra, out_groups):
    rows = normed.shape[0]
    lines = sum(out_groups)
    cols = sum(r.shape[1] for r in rhs) + sum(r.shape[1] for r in extra)
    anywhere = pl.BlockSpec(memory_space=pl.ANY)
    vmem = pl.BlockSpec(memory_space=pltpu.VMEM)
    return pl.pallas_call(
        functools.partial(weight_kernel, len(rhs), len(out_groups)),
        grid_spec=pltpu.PrefetchScalarGridSpec(
            num_scalar_prefetch=1,
            grid=(1,),
            in_specs=[vmem] * (1 + len(rhs) + len(extra)),
            out_specs=[anywhere] * len(out_groups),
            scratch_shapes=[pltpu.VMEM((D, cols), BF16), pltpu.SemaphoreType.DMA((lines,))],
        ),
        out_shape=[jax.ShapeDtypeStruct((k, D // lines, cols), BF16) for k in out_groups],
        compiler_params=params(),
        cost_estimate=pl.CostEstimate(flops=4 * rows * D * cols, bytes_accessed=10 << 20, transcendentals=0),
        name="weight_grad",
    )(out_pos, normed, *rhs, *extra)


def input_kernel(lines, n_in, first_col, n_rhs, pos_ref, hid_ref, gres_ref, gain_ref, *rest):
    grads = rest[:n_rhs]
    pieces = rest[n_rhs : n_rhs + n_in]
    long_ref, glob_ref, small_ref, w_s, sems = rest[n_rhs + n_in :]
    s = pl.program_id(0)

    @pl.when(s == 0)
    def _():
        for copy in load_rows(pieces, pos_ref, lines, w_s, sems, first_col):
            copy.wait()
        small_ref[...] = jnp.zeros_like(small_ref)

    xhat, rstd = norm_stats(hid_ref[...].astype(F32))
    groups = n_rhs // 3
    gn1 = jnp.zeros((T, D), F32)
    for part in range(3):
        at = part * D
        for g in range(groups):
            ref = grads[3 * g + part]
            width = ref.shape[1]
            gn1 = gn1 + dot(ref[...], w_s[:, at : at + width], NT)
            if part != 1:
                row = 2 + part // 2
                first = at - part * D
                small_ref[row : row + 1, first : first + width] += jnp.sum(
                    ref[...].astype(F32), axis=0, keepdims=True
                )
            at += width
    small_ref[0:1] += jnp.sum(gn1 * xhat, axis=0, keepdims=True)
    small_ref[1:2] += jnp.sum(gn1, axis=0, keepdims=True)
    ghid = (gres_ref[...] + norm_back(gn1, xhat, rstd, gain_ref[...])).astype(BF16)
    glob_ref[0, 0] = ghid[:GLOB]
    long_ref[0, 0] = ghid[GLOB:]


def input_grad(pos, hid, gres, gain, grads, pieces, first_col, long_shape, glob_shape):
    rows = hid.shape[0]
    n = len(pieces)
    lines = pos.shape[0]
    spec = pl.BlockSpec((T, D), lambda s, *_: (s, 0))
    vec = pl.BlockSpec((1, D), lambda s, *_: (0, 0))
    anywhere = pl.BlockSpec(memory_space=pl.ANY)
    return pl.pallas_call(
        functools.partial(input_kernel, lines, n, first_col, len(grads)),
        grid_spec=pltpu.PrefetchScalarGridSpec(
            num_scalar_prefetch=1,
            grid=(rows // T,),
            in_specs=[spec, spec, vec]
            + [pl.BlockSpec((T, r.shape[1]), lambda s, *_: (s, 0)) for r in grads]
            + [anywhere] * n,
            out_specs=[
                pl.BlockSpec((1, 1, SEQ, D), lambda s, *_: (s, 0, 0, 0)),
                pl.BlockSpec((1, 1, GLOB, D), lambda s, *_: (s, 0, 0, 0)),
                pl.BlockSpec((8, D), lambda s, *_: (0, 0)),
            ],
            scratch_shapes=[pltpu.VMEM((D, 3 * D), BF16), pltpu.SemaphoreType.DMA((lines,))],
        ),
        out_shape=[
            jax.ShapeDtypeStruct(long_shape, BF16),
            jax.ShapeDtypeStruct(glob_shape, BF16),
            jax.ShapeDtypeStruct((8, D), F32),
        ],
        compiler_params=params(),
        cost_estimate=pl.CostEstimate(flops=12 * rows * D * D, bytes_accessed=20 << 20, transcendentals=0),
        name="input_grad",
    )(pos, hid, gres, gain, *grads, *pieces)


AXES = ("wide", "narrow")


class Links:
    def __init__(self, mesh):
        self.wide = mesh.shape["wide"]
        self.narrow = mesh.shape["narrow"]
        self.count = self.wide * self.narrow
        self.pairwise = self.wide == 8 and self.narrow == 4
        self.lines = self.wide if self.pairwise else 1

    def setup(self):
        if not self.pairwise:
            self.pos = jnp.zeros((1,), jnp.int32)
            return
        w = lax.axis_index("wide")
        self.z = lax.axis_index("narrow")
        near = jnp.where(w % 2 == 0, 2, 4)
        far = 6 - near
        order = [0, near, far, 6, 1, 1 ^ far, 1 ^ near, 7]
        self.pos = jnp.stack([w ^ m for m in order]).astype(jnp.int32)

    def swap(self, x, wide_mask=0, narrow_mask=0):
        masks = wide_mask if isinstance(wide_mask, tuple) else (wide_mask, wide_mask)
        pairs = []
        for w in range(self.wide):
            for z in range(self.narrow):
                pairs.append(
                    (w * self.narrow + z, (w ^ masks[w % 2]) * self.narrow + (z ^ narrow_mask))
                )
        return lax.ppermute(x, AXES, pairs)

    def gather(self, x):
        if not self.pairwise:
            return [lax.all_gather(x, AXES, axis=0, tiled=True)]
        for mask in (1, 2):
            other = self.swap(x, 0, mask)
            low = (self.z & mask) == 0
            x = jnp.concatenate([jnp.where(low, x, other), jnp.where(low, other, x)], axis=0)
        near = self.swap(x, (2, 4))
        own = jnp.concatenate([x, near], axis=0)
        own_core = self.swap(own, 1)
        far = self.swap(own, (4, 2))
        far_core = self.swap(far, 1)
        return [own, far, own_core, far_core]

    def gather_small(self, x):
        if not self.pairwise:
            return lax.all_gather(x, AXES, axis=0, tiled=True)
        pieces = jnp.concatenate(self.gather(x), axis=0).reshape(self.lines, self.narrow, -1)
        place = (self.pos[None, :] == jnp.arange(self.lines)[:, None]).astype(jnp.bfloat16)
        flat = pieces.reshape(self.lines, -1)
        return jnp.dot(place, flat, preferred_element_type=jnp.float32).reshape(self.count, -1)

    def groups(self):
        return (2, 2, 2, 2) if self.pairwise else (1,)

    def add(self, *parts):
        total = parts[0].astype(F32)
        for p in parts[1:]:
            total = total + p.astype(F32)
        return total

    def sum(self, parts):
        if not self.pairwise:
            return lax.psum_scatter(parts[0][0].astype(F32), AXES, scatter_dimension=0, tiled=True)
        kind = parts[0].dtype
        keep_a, keep_b, send_a, send_b = parts
        got_b = self.swap(send_b, 1)
        got_a = self.swap(send_a, 1)
        far = self.swap(self.add(keep_b, got_b).astype(kind), (4, 2))
        near = self.swap(self.add(keep_a[1], got_a[1], far[1]).astype(kind), (2, 4))
        x = self.add(keep_a[0], got_a[0], far[0], near)
        for mask in (2, 1):
            half = x.shape[0] // 2
            low = (self.z & mask) == 0
            mine = jnp.where(low, x[:half], x[half:])
            theirs = jnp.where(low, x[half:], x[:half])
            x = mine + self.swap(theirs.astype(kind), 0, mask).astype(F32)
        return x

    def sum_small(self, x):
        if not self.pairwise:
            return lax.psum_scatter(x, AXES, scatter_dimension=0, tiled=True)
        blocks = x.reshape(self.lines, self.narrow, -1)
        blocks = jnp.take(blocks, self.pos, axis=0)
        return self.sum([blocks[0:2], blocks[2:4], blocks[4:6], blocks[6:8]])


GROUPS = 2
CHUNKS = 2
PARTS = FF // D


def row_vector(v):
    return v.astype(F32).reshape(1, -1)


def body(links, long_in, glob_in, lengths, ln1_gain, ln1_bias, w_qkv, qv_bias, rel_embed, w_out, out_bias, ln2_gain, ln2_bias, w_in, in_bias, w_down, down_bias, cot_long, cot_glob):
    links.setup()
    pos = links.pos
    groups = links.groups()
    count = links.count
    micro = long_in.shape[0]
    r = w_qkv.shape[0]
    smalls = [ln1_gain, ln1_bias, qv_bias, out_bias, ln2_gain, ln2_bias, down_bias, in_bias]
    sizes = [v.shape[0] for v in smalls]

    rel = jnp.pad(rel_embed, ((0, 0), (LEAD, LABELS - LEAD - RELS)))
    attn_packed = jnp.concatenate([w_qkv, w_out, rel], axis=1)
    w_in_parts = w_in.reshape(r, count, PARTS, r).transpose(2, 0, 1, 3).reshape(PARTS, r, D)
    w_down_parts = w_down.reshape(PARTS, r, D)
    per = PARTS // CHUNKS
    ffn_packed = []
    for c in range(CHUNKS):
        which = range(per * c, per * (c + 1))
        ffn_packed.append(
            jnp.concatenate([w_in_parts[i] for i in which] + [w_down_parts[i] for i in which], axis=1)
        )

    small_all = links.gather_small(jnp.concatenate(smalls).reshape(1, -1))
    attn = links.gather(attn_packed)
    ffns = [links.gather(x) for x in ffn_packed]

    at = 0
    whole = []
    for n in sizes:
        whole.append(small_all[:, at : at + n])
        at += n
    gain1, bias1, qv, out_b, gain2, bias2, down_b = [row_vector(v) for v in whole[:7]]
    in_b = row_vector(whole[7].reshape(count, PARTS, r).transpose(1, 0, 2))
    full_bias = jnp.concatenate([qv[:, :D], jnp.zeros((1, D), F32), qv[:, D:]], axis=1)

    hid = jnp.concatenate([glob_in, long_in], axis=2).reshape(micro * T, D)
    cot = jnp.concatenate([cot_glob, cot_long], axis=2).reshape(micro * T, D)
    lens = lengths.reshape(micro)

    normed, proj, rel_all, rel_turned = project(pos, hid, gain1, bias1, full_bias, attn, 0, 4 * D)
    pairs = PAIRS // GROUPS
    heads = [attend(lens, proj, rel_all, pairs * g, pairs) for g in range(GROUPS)]
    mixed = [h[0] for h in heads]
    res, n2, g_ffn = mix_out(pos, lens, hid, out_b, gain2, bias2, cot, mixed, attn, 3 * D)
    ys, gns, gbs, w_sums = [], [], [], []
    for c in range(CHUNKS):
        cols = slice(per * c * D, per * (c + 1) * D)
        out = ffn(pos, pos, n2, g_ffn, in_b[:, cols], ffns[c], 0, per * D, per, groups)
        ys.append(out[0])
        gns.append(out[1])
        gbs.append(out[2])
        w_sums.append(links.sum(out[3:]))
    block_long, block_glob, gres, gmix, small2, gw_out = mid(
        pos, lens, res, g_ffn, gain2, down_b, ys, gns, mixed, attn, 3 * D, long_in.shape, glob_in.shape
    )
    grads, grels, a_sums = [], [], []
    for g in range(GROUPS):
        out = attend_back(proj, rel_turned, gmix, mixed[g], heads[g][1], heads[g][2], pairs * g, pairs, 0)
        grads.append(out[:3])
        grels.append(out[3])
        extra = []
        if g == 0:
            extra.append(gw_out)
        if g == GROUPS - 1:
            extra.append(jnp.concatenate(grels, axis=0))
        a_sums.append(links.sum(weight_grad(pos, normed, grads[g], extra, groups)))
    grad_long, grad_glob, small1 = input_grad(
        pos, hid, gres, gain1, [t for gr in grads for t in gr], attn, 0, long_in.shape, glob_in.shape
    )
    gin = jnp.concatenate(gbs, axis=1).reshape(PARTS, count, r).transpose(1, 0, 2).reshape(count, -1)
    small_parts = [
        small1[0].reshape(count, -1),
        small1[1].reshape(count, -1),
        small1[2:4].reshape(count, -1),
        small2[2].reshape(count, -1),
        small2[0].reshape(count, -1),
        small2[1].reshape(count, -1),
        small2[3].reshape(count, -1),
        gin,
    ]
    small_sum = links.sum_small(jnp.concatenate(small_parts, axis=1)).reshape(-1)
    small_grads = []
    at = 0
    for n in sizes:
        small_grads.append(small_sum[at : at + n])
        at += n
    g_gain1, g_bias1, g_qv, g_out_b, g_gain2, g_bias2, g_down_b, g_in_b = small_grads

    width = pairs * 128
    g_qkv = jnp.concatenate(
        [a_sums[g][:, width * n : width * (n + 1)] for n in range(3) for g in range(GROUPS)], axis=1
    )
    g_out = a_sums[0][:, 3 * width : 3 * width + D]
    at = 3 * width + (D if GROUPS == 1 else 0) + BACK_LEAD
    g_rel = a_sums[-1][:, at : at + RELS]
    g_in = jnp.stack(
        [w_sums[c][:, D * i : D * (i + 1)] for c in range(CHUNKS) for i in range(per)], axis=0
    )
    g_in = g_in.reshape(PARTS, r, count, r).transpose(1, 2, 0, 3).reshape(r, FF)
    g_down = jnp.concatenate(
        [w_sums[c][:, D * (per + i) : D * (per + i + 1)] for c in range(CHUNKS) for i in range(per)], axis=0
    )
    return (
        block_long, block_glob, grad_long, grad_glob,
        g_gain1, g_bias1, g_qkv, g_qv, g_rel, g_out, g_out_b,
        g_gain2, g_bias2, g_in, g_in_b, g_down, g_down_b,
    )


def solution(mesh):
    rows = P(None, AXES, None, None)
    vec = P(AXES)
    mat = P(AXES, None)
    placed = (rows, rows, P(None, AXES), vec, vec, mat, vec, mat, mat, vec, vec, vec, mat, vec, mat, vec, rows, rows)
    return jax.shard_map(
        functools.partial(body, Links(mesh)),
        mesh=mesh,
        in_specs=placed,
        out_specs=(rows, rows, rows, rows, vec, vec, mat, vec, mat, mat, vec, vec, vec, mat, vec, mat, vec),
        check_vma=False,
    )
```

time: 1460 us -> 508 us (0.35)
  local copies, waits for them, and re-layouts: 440 us -> 28.7 us
  matrix products: 313 us -> 0.12 us
  waiting for transfers between devices: 440 us -> 160 us
  Pallas kernels: 0 us -> 237 us
  blocking collectives: 152 us -> 0 us
  other arithmetic: 89.3 us -> 16.3 us
  starting transfers between devices: 0.53 us -> 54.4 us
  between operations: 17.7 us -> 2.29 us
    reduce_scatter x5 -> x0, waiting for transfers between devices: 437 us -> none  [the longest x1 142 us: sum_ffn(): lax.psum_scatter(ffn_terms[4], ('wide', 'narrow'), scatter_dimension=0, t...]
    dot_general x52 -> x1, matrix products: 305 us -> 0.12 us  [gather_small(): jnp.dot(place, flat, preferred_element_type=jnp.float32)]
    pallas_call x0 -> x12, Pallas kernels: none -> 237 us  [the longest x2 59.9 us: ffn(): pl.pallas_call(functools.partial(ffn_kernel, lines, n, first_in, first_do...]
    reshape x8 -> x14, local copies, waits for them, and re-layouts: 245 us -> 9.14 us  [the longest x8 4.21 us: row_vector(): return v.astype(F32).reshape(1, -1)]
    ppermute x0 -> x54, waiting for transfers between devices: none -> 160 us  [swap(): return lax.ppermute(x, AXES, pairs)]
    unnamed x2 -> x0, blocking collectives: 81.1 us -> none
    slice x33 -> x18, local copies, waits for them, and re-layouts: 88.6 us -> 10.2 us  [the longest x1 4.56 us: body(): w_in_parts[i]]
    all_gather x1 -> x0, blocking collectives: 70.8 us -> none  [body(): lax.all_gather(rel_embed, ('wide', 'narrow'), axis=0, tiled=True)]
  transfers between devices with their start and end apart: 9 -> 54, of which waited for: 4 -> 29; matrix products, arithmetic and copies ran while one was open for 33% -> 5% of each run, Pallas kernels for 0% -> 25%
where the time goes in v1:
time: 508 us; the launch traced here: 500 us
  Pallas kernels  237 us (47%)
  waiting for transfers between devices  160 us (31%)
  starting transfers between devices  54.4 us (11%)
  local copies, waits for them, and re-layouts  28.7 us (6%)
  other arithmetic  16.3 us (3%)
    ppermute x54, waiting for transfers between devices, swap(): return lax.ppermute(x, AXES, pairs)  160 us
    pallas_call x2, Pallas kernels, ffn(): pl.pallas_call(functools.partial(ffn_kernel, lines, n, first_in, first_do...  59.9 us
    ppermute x54, starting transfers between devices, swap(): return lax.ppermute(x, AXES, pairs)  54.4 us
    pallas_call x2, Pallas kernels, attend(): pl.pallas_call(attend_kernel, grid_spec=pltpu.PrefetchScalarGridSpec(num_...  53 us
    pallas_call x2, Pallas kernels, attend_back(): pl.pallas_call(attend_back_kernel, grid=(n_pairs, seqs), in_specs=[part(0...  50.1 us
    pallas_call x2, Pallas kernels, weight_grad(): pl.pallas_call(functools.partial(weight_kernel, len(rhs), len(out_groups)...  18.3 us
    pallas_call x1, Pallas kernels, mid(): pl.pallas_call(functools.partial(mid_kernel, lines, n, first_col, len(mix...  17.3 us
    pallas_call x1, Pallas kernels, project(): pl.pallas_call(functools.partial(project_kernel, lines, n, first_col, fir...  14.6 us
  transfers between devices with their start and end apart: 54, of which 29 were waited for; matrix products, arithmetic and copies ran while one was open for 5% of the time, Pallas kernels for 25%

profile of v1, /device:TPU:0, one launch (start us, length us, event | category | flops | bytes accessed | tf_op | source)
XLA Modules:
  0.0 499.5 jit_solution(2576118673935040563)
XLA Ops:
  0.7 2.1 reshape.552
  2.9 4.6 slice_reduce_fusion.1
  8.1 3.1 collective-permute-start.12
  11.5 2.0 collective-permute-start.6
  14.3 1.5 collective-permute-done
  15.9 3.1 collective-permute-start.1
  19.5 1.4 collective-permute-done.1
  21.0 1.7 collective-permute-start.2
  22.6 1.3 pad_maximum_fusion
  24.6 1.7 collective-permute-start.3
  29.8 3.4 collective-permute-start.13
  33.5 3.0 collective-permute-start.19
  36.5 30.9 %collective-permute-done.7 = bf16[48,3328]{1,0:T(8,128)(2,1)S(1)} collective-permute-done((bf16[48,3328]{1,0:T(8,128)(2,1)S(1)}, bf16[48,3328]{1,0:T(8,128)(2,1)S(1)}, u32[]{:S(2)}, u32[]{:S(2)}) %collective-permute-start.7) | collective-permute-done | bytes 319520 | tf_op jit(solution)/shard_map/ppermute | solution.py:775
  67.5 1.6 collective-permute-start.8
  70.6 7.4 %collective-permute-done.8 = bf16[96,3328]{1,0:T(8,128)(2,1)S(1)} collective-permute-done((bf16[96,3328]{1,0:T(8,128)(2,1)S(1)}, bf16[96,3328]{1,0:T(8,128)(2,1)S(1)}, u32[]{:S(2)}, u32[]{:S(2)}) %collective-permute-start.8) | collective-permute-done | bytes 639008 | tf_op jit(solution)/shard_map/ppermute | solution.py:775
  78.1 1.6 collective-permute-start.9
  81.4 1.5 collective-permute-start.20
  83.3 6.2 %collective-permute-done.14 = bf16[96,3072]{1,0:T(8,128)(2,1)} collective-permute-done((bf16[96,3072]{1,0:T(8,128)(2,1)}, bf16[96,3072]{1,0:T(8,128)(2,1)}, u32[]{:S(2)}, u32[]{:S(2)}) %collective-permute-start.14) | collective-permute-done | bytes 589856 | tf_op jit(solution)/shard_map/ppermute | solution.py:775
  89.6 2.2 pad_maximum_fusion.3.rest_0_
  91.7 1.5 collective-permute-start.15
  93.2 9.3 %collective-permute-done.9.rest_1_.rest_3_.rest_7_ = bf16[192,3328]{1,0:T(8,128)(2,1)S(1)} collective-permute-done((bf16[192,3328]{1,0:T(8,128)(2,1)S(1)}, bf16[192,3328]{1,0:T(8,128)(2,1)S(1)}, u32[]{:S(2)}, u32[]{:S(2)}) %collective-permute-start.9) | collective-permute-done | bytes 1277984 | tf_op jit(solution)/shard_map/ppermute | solution.py:775
  102.6 2.0 collective-permute-start.11
  104.6 2.2 pad_maximum_fusion.4.rest_0_
  106.7 1.5 collective-permute-start.21
  113.9 1.4 collective-permute-done.15.rest_1_
  115.3 1.9 collective-permute-start.22
  117.2 10.8 %collective-permute-done.21.rest_1_ = bf16[192,3072]{1,0:T(8,128)(2,1)} collective-permute-done((bf16[192,3072]{1,0:T(8,128)(2,1)}, bf16[192,3072]{1,0:T(8,128)(2,1)}, u32[]{:S(2)}, u32[]{:S(2)}) %collective-permute-start.21) | collective-permute-done | bytes 1179680 | tf_op jit(solution)/shard_map/ppermute | solution.py:775
  128.0 1.6 collective-permute-start.17
  129.6 14.6 %project.1 = (bf16[1088,768]{1,0:T(8,128)(2,1)}, bf16[1088,2304]{1,0:T(8,128)(2,1)}, bf16[768,256]{1,0:T(8,128)(2,1)}, bf16[256,768]{1,0:T(8,128)(2,1)}) custom-call(s32[8]{0:T(128)} %copy-done.22, bf16[1088,768]{1,0:T(8,128)(2,1)} %bitcast.66, f32[1,768]{1,0:T(1,128)} %reshape.546.gain_ref, f32[1,768]{1,0:T(1,128)} %reshape.547.bias_ref, ...), custom_call_target="tpu_custom_call" | custom-call | flops 7700742144 | bytes 12582912 | tf_op jit(solution)/shard_map/project/pallas_call | solution.py:111
  144.2 26.5 %attend.3 = (bf16[1088,384]{1,0:T(8,128)(2,1)}, bf16[2,3,2,128,1280]{4,3,2,1,0:T(8,128)(2,1)}, bf16[2,3,2,32,544]{4,3,2,1,0:T(8,128)(2,1)}) custom-call(s32[2]{0:T(128)} %bitcast.72, bf16[1088,2304]{1,0:T(8,128)(2,1)} %get-tuple-element.69.q_ref.k_ref.v_ref, bf16[1088,2304]{1,0:T(8,128)(2,1)} %get-tuple-element.69.q_ref.k_ref.v_ref, ...), custom_call_target="tpu_custom_call" | custom-call | flops 5033164800 | bytes 6291456 | tf_op jit(solution)/shard_map/attend/pallas_call | solution.py:203
  170.7 26.5 %attend.2 = (bf16[1088,384]{1,0:T(8,128)(2,1)}, bf16[2,3,2,128,1280]{4,3,2,1,0:T(8,128)(2,1)}, bf16[2,3,2,32,544]{4,3,2,1,0:T(8,128)(2,1)}) custom-call(s32[2]{0:T(128)} %bitcast.73, bf16[1088,2304]{1,0:T(8,128)(2,1)} %get-tuple-element.69.q_ref.k_ref.v_ref, bf16[1088,2304]{1,0:T(8,128)(2,1)} %get-tuple-element.69.q_ref.k_ref.v_ref, ...), custom_call_target="tpu_custom_call" | custom-call | flops 5033164800 | bytes 6291456 | tf_op jit(solution)/shard_map/attend/pallas_call | solution.py:203
  197.2 9.4 %mix_out.1 = (f32[1088,768]{1,0:T(8,128)}, bf16[1088,768]{1,0:T(8,128)(2,1)}, bf16[1088,768]{1,0:T(8,128)(2,1)}) custom-call(s32[8]{0:T(128)} %copy-done.22, s32[2]{0:T(128)} %bitcast.74, bf16[1088,768]{1,0:T(8,128)(2,1)} %bitcast.67, f32[1,768]{1,0:T(1,128)} %reshape.542.bias_ref, f32[1,768]{1,0:T(1,128)} %reshape.543.gain2_ref, ...), custom_call_target="tpu_custom_call" | custom-call | flops 2566914048 | bytes 12582912 | tf_op jit(solution)/shard_map/mix_out/pallas_call | solution.py:395
  208.0 30.1 %ffn.2 = (f32[1088,768]{1,0:T(8,128)}, f32[1088,768]{1,0:T(8,128)}, f32[1,1536]{1,0:T(1,128)}, bf16[2,96,3072]{2,1,0:T(8,128)(2,1)}, bf16[2,96,3072]{2,1,0:T(8,1...) custom-call(s32[8]{0:T(128)} %copy-done.22, s32[8]{0:T(128)} %copy-done.22, ...), custom_call_target="tpu_custom_call" | custom-call | flops 30802968576 | bytes 31457280 | tf_op jit(solution)/shard_map/ffn/pallas_call | solution.py:500
  239.6 29.8 %ffn.3 = (f32[1088,768]{1,0:T(8,128)}, f32[1088,768]{1,0:T(8,128)}, f32[1,1536]{1,0:T(1,128)}, bf16[2,96,3072]{2,1,0:T(8,128)(2,1)}, bf16[2,96,3072]{2,1,0:T(8,1...) custom-call(s32[8]{0:T(128)} %copy-done.22, s32[8]{0:T(128)} %copy-done.22, ...), custom_call_target="tpu_custom_call" | custom-call | flops 30802968576 | bytes 31457280 | tf_op jit(solution)/shard_map/ffn/pallas_call | solution.py:500
  269.4 17.3 %mid.1 = (bf16[2,1,512,768]{3,2,1,0:T(8,128)(2,1)}, bf16[2,1,32,768]{3,2,1,0:T(8,128)(2,1)}, f32[1088,768]{1,0:T(8,128)}, bf16[1088,768]{1,0:T(8,128)(2,1)}, f32[8,768]{1,0:T(8,128)}, /*index=5*/bf16[768,768]{1,0:T(8,128)(2,1)}) custom-call(s32[8]{0:T(128)} %copy-done.22, s32[2]{0:T(128)} %bitcast.75, f32[1088,768]{1,0:T(8,128)} %get-tuple-element.73.res_ref, ...), custom_call_target="tpu_custom_call" | custom-call | flops 5133828096 | bytes 31457280 | tf_op jit(solution)/shard_map/mid/pallas_call | solution.py:595
  286.6 25.1 %attend_back.3 = (bf16[1088,384]{1,0:T(8,128)(2,1)}, bf16[1088,384]{1,0:T(8,128)(2,1)}, bf16[1088,384]{1,0:T(8,128)(2,1)}, f32[384,256]{1,0:T(8,128)}) custom-call(bf16[1088,2304]{1,0:T(8,128)(2,1)} %get-tuple-element.69.q_ref.k_ref.v_ref, bf16[1088,2304]{1,0:T(8,128)(2,1)} %get-tuple-element.69.q_ref.k_ref.v_ref, ...), custom_call_target="tpu_custom_call" | custom-call | flops 10066329600 | bytes 6291456 | tf_op jit(solution)/shard_map/attend_back/pallas_call | solution.py:326
  311.8 25.0 %attend_back.2 = (bf16[1088,384]{1,0:T(8,128)(2,1)}, bf16[1088,384]{1,0:T(8,128)(2,1)}, bf16[1088,384]{1,0:T(8,128)(2,1)}, f32[384,256]{1,0:T(8,128)}) custom-call(bf16[1088,2304]{1,0:T(8,128)(2,1)} %get-tuple-element.69.q_ref.k_ref.v_ref, bf16[1088,2304]{1,0:T(8,128)(2,1)} %get-tuple-element.69.q_ref.k_ref.v_ref, ...), custom_call_target="tpu_custom_call" | custom-call | flops 10066329600 | bytes 6291456 | tf_op jit(solution)/shard_map/attend_back/pallas_call | solution.py:326
  336.8 14.6 %input_grad.1 = (bf16[2,1,512,768]{3,2,1,0:T(8,128)(2,1)}, bf16[2,1,32,768]{3,2,1,0:T(8,128)(2,1)}, f32[8,768]{1,0:T(8,128)}) custom-call(s32[8]{0:T(128)} %copy-done.22, bf16[1088,768]{1,0:T(8,128)(2,1)} %bitcast.68, f32[1088,768]{1,0:T(8,128)} %get-tuple-element.82.gres_ref, f32[1,768]{1,0:T(1,128)} %reshape.546.gain_ref, ...), custom_call_target="tpu_custom_call" | custom-call | flops 7700742144 | bytes 20971520 | tf_op jit(solution)/shard_map/input_grad/pallas_call | solution.py:719
  356.3 1.5 collective-permute-start.26
  358.3 1.7 collective-permute-done.26
  360.0 1.5 collective-permute-start.27
  363.7 8.9 %weight_grad.3 = (bf16[2,96,1408]{2,1,0:T(8,128)(2,1)}, bf16[2,96,1408]{2,1,0:T(8,128)(2,1)}, bf16[2,96,1408]{2,1,0:T(8,128)(2,1)}, bf16[2,96,1408]{2,1,0:T(8,128)(2,1)}) custom-call(s32[8]{0:T(128)} %copy-done.22, bf16[1088,768]{1,0:T(8,128)(2,1)} %get-tuple-element.101.normed_ref, bf16[1088,384]{1,0:T(8,128)(2,1)} %get-tuple-element.92.rest_3_.rest_0_, ...), custom_call_target="tpu_custom_call" | custom-call | flops 4706009088 | bytes 10485760 | tf_op jit(solution)/shard_map/weight_grad/pallas_call | solution.py:661
  373.2 3.8 collective-permute-start.29
  377.0 9.5 %weight_grad.2 = (bf16[2,96,1920]{2,1,0:T(8,128)(2,1)}, bf16[2,96,1920]{2,1,0:T(8,128)(2,1)}, bf16[2,96,1920]{2,1,0:T(8,128)(2,1)}, bf16[2,96,1920]{2,1,0:T(8,128)(2,1)}) custom-call(s32[8]{0:T(128)} %copy-done.22, bf16[1088,768]{1,0:T(8,128)(2,1)} %get-tuple-element.101.normed_ref, bf16[1088,384]{1,0:T(8,128)(2,1)} %get-tuple-element.87.rest_0_, ...), custom_call_target="tpu_custom_call" | custom-call | flops 6417285120 | bytes 10485760 | tf_op jit(solution)/shard_map/weight_grad/pallas_call | solution.py:661
  387.9 1.6 collective-permute-start.38
  390.9 6.5 %collective-permute-done.38 = bf16[2,96,1408]{2,1,0:T(8,128)(2,1)S(1)} collective-permute-done((bf16[2,96,1408]{2,1,0:T(8,128)(2,1)S(1)}, bf16[2,96,1408]{2,1,0:T(8,128)(2,1)S(1)}, u32[]{:S(2)}, u32[]{:S(2)}) %collective-permute-start.38) | collective-permute-done | bytes 540704 | tf_op jit(solution)/shard_map/ppermute | solution.py:775
  397.5 1.6 collective-permute-start.32
  399.5 1.6 collective-permute-start.39
  401.4 7.5 %collective-permute-done.39 = bf16[96,1408]{1,0:T(8,128)(2,1)S(1)} collective-permute-done((bf16[96,1408]{1,0:T(8,128)(2,1)S(1)}, bf16[96,1408]{1,0:T(8,128)(2,1)S(1)}, u32[]{:S(2)}, u32[]{:S(2)}) %collective-permute-start.39) | collective-permute-done | bytes 270368 | tf_op jit(solution)/shard_map/ppermute | solution.py:775
  409.9 1.6 collective-permute-start.50
  412.0 8.3 %collective-permute-done.40 = bf16[48,1408]{1,0:T(8,128)(2,1)S(1)} collective-permute-done((bf16[48,1408]{1,0:T(8,128)(2,1)S(1)}, bf16[48,1408]{1,0:T(8,128)(2,1)S(1)}, u32[]{:S(2)}, u32[]{:S(2)}) %collective-permute-start.40) | collective-permute-done | bytes 135200 | tf_op jit(solution)/shard_map/ppermute | solution.py:775
  420.3 1.5 collective-permute-start.33
  421.9 10.0 %collective-permute-done.33 = bf16[96,1920]{1,0:T(8,128)(2,1)S(1)} collective-permute-done((bf16[96,1920]{1,0:T(8,128)(2,1)S(1)}, bf16[96,1920]{1,0:T(8,128)(2,1)S(1)}, u32[]{:S(2)}, u32[]{:S(2)}) %collective-permute-start.33) | collective-permute-done | bytes 368672 | tf_op jit(solution)/shard_map/ppermute | solution.py:775
  432.2 8.5 %collective-permute-done.34 = bf16[48,1920]{1,0:T(8,128)(2,1)S(1)} collective-permute-done((bf16[48,1920]{1,0:T(8,128)(2,1)S(1)}, bf16[48,1920]{1,0:T(8,128)(2,1)S(1)}, u32[]{:S(2)}, u32[]{:S(2)}) %collective-permute-start.34) | collective-permute-done | bytes 184352 | tf_op jit(solution)/shard_map/ppermute | solution.py:775
  440.8 4.2 collective-permute-done.41
  445.7 3.8 collective-permute-done.35
  451.0 1.5 collective-permute-start.45
  453.5 7.4 %collective-permute-done.45 = bf16[96,3072]{1,0:T(8,128)(2,1)S(1)} collective-permute-done((bf16[96,3072]{1,0:T(8,128)(2,1)S(1)}, bf16[96,3072]{1,0:T(8,128)(2,1)S(1)}, u32[]{:S(2)}, u32[]{:S(2)}) %collective-permute-start.45) | collective-permute-done | bytes 589856 | tf_op jit(solution)/shard_map/ppermute | solution.py:775
  462.4 4.8 collective-permute-done.51
  468.7 12.6 %collective-permute-done.46 = bf16[48,3072]{1,0:T(8,128)(2,1)S(1)} collective-permute-done((bf16[48,3072]{1,0:T(8,128)(2,1)S(1)}, bf16[48,3072]{1,0:T(8,128)(2,1)S(1)}, u32[]{:S(2)}, u32[]{:S(2)}) %collective-permute-start.46) | collective-permute-done | bytes 294944 | tf_op jit(solution)/shard_map/ppermute | solution.py:775
  481.6 5.4 %collective-permute-done.52 = bf16[48,3072]{1,0:T(8,128)(2,1)S(1)} collective-permute-done((bf16[48,3072]{1,0:T(8,128)(2,1)S(1)}, bf16[48,3072]{1,0:T(8,128)(2,1)S(1)}, u32[]{:S(2)}, u32[]{:S(2)}) %collective-permute-start.52) | collective-permute-done | bytes 294944 | tf_op jit(solution)/shard_map/ppermute | solution.py:775
  487.2 2.9 collective-permute-done.47
  490.2 3.0 collective-permute-done.53
  495.8 2.6 reshape.554
  (280 shorter events, 42.4 us)
Async XLA Ops:
  7.5 15.1 %copy-start.4 = (bf16[2,1,512,768]{3,2,1,0:T(8,128)(2,1)S(1)}, bf16[2,1,512,768]{3,2,1,0:T(8,128)(2,1)}, u32[]{:S(2)}) copy-start(bf16[2,1,512,768]{3,2,1,0:T(8,128)(2,1)} %param.18) | copy-start | bytes 4718596
  7.5 15.1 %copy-start.19 = (bf16[2,1,32,768]{3,2,1,0:T(8,128)(2,1)S(1)}, bf16[2,1,32,768]{3,2,1,0:T(8,128)(2,1)}, u32[]{:S(2)}) copy-start(bf16[2,1,32,768]{3,2,1,0:T(8,128)(2,1)} %param.19) | copy-start | bytes 294916
  8.1 21.6 %collective-permute-start.12 = (bf16[24,3072]{1,0:T(8,128)(2,1)S(1)}, bf16[24,3072]{1,0:T(8,128)(2,1)S(1)}, u32[]{:S(2)}, u32[]{:S(2)}) collective-permute-start(bf16[24,3072]{1,0:T(8,128)(2,1)S(1)} %pad_maximum_fusion.13), channel_id=1, source_target_pairs={{0,1},{1,0},{2,3},{3,2},{4,5},{5,4},{6,7},{7,6},{8,9},{9,8},{10,11... | collective-permute-start | bytes 442376 | tf_op jit(solution)/shard_map/ppermute | solution.py:775
  11.3 4.5 collective-permute-start
  11.5 21.8 %collective-permute-start.6 = (bf16[24,3328]{1,0:T(8,128)(2,1)S(1)}, bf16[24,3328]{1,0:T(8,128)(2,1)S(1)}, u32[]{:S(2)}, u32[]{:S(2)}) collective-permute-start(bf16[24,3328]{1,0:T(8,128)(2,1)S(1)} %fusion.5), channel_id=1, source_target_pairs={{0,1},{1,0},{2,3},{3,2},{4,5},{5,4},{6,7},{7,6},{8,9},{9,8},{10,11... | collective-permute-start | bytes 479240 | tf_op jit(solution)/shard_map/ppermute | solution.py:775
  14.0 19.2 %collective-permute-start.18 = (bf16[24,3072]{1,0:T(8,128)(2,1)S(1)}, bf16[24,3072]{1,0:T(8,128)(2,1)S(1)}, u32[]{:S(2)}, u32[]{:S(2)}) collective-permute-start(bf16[24,3072]{1,0:T(8,128)(2,1)S(1)} %pad_maximum_fusion.14), channel_id=1, source_target_pairs={{0,1},{1,0},{2,3},{3,2},{4,5},{5,4},{6,7},{7,6},{8,9},{9,8},{10,11... | collective-permute-start | bytes 442376 | tf_op jit(solution)/shard_map/ppermute | solution.py:775
  14.3 68.5 %copy-start.22 = (s32[8]{0:T(128)}, s32[8]{0:T(128)S(1)}, u32[]{:S(2)}) copy-start(s32[8]{0:T(128)S(1)} %stack.68.pos_ref.out_pos_ref) | copy-start | bytes 100
  15.9 5.0 %collective-permute-start.1 = (bf16[2,288]{1,0:T(2,128)(2,1)S(1)}, bf16[2,288]{1,0:T(2,128)(2,1)S(1)}, u32[]{:S(2)}, u32[]{:S(2)}) collective-permute-start(bf16[2,288]{1,0:T(2,128)(2,1)S(1)} %pad_maximum_fusion.17), channel_id=1, source_target_pairs={{0,2},{1,3},{2,0},{3,1},{4,6},{5,7},{6,4},{7,5},{8,10},{9,11},{10,... | collective-permute-start | bytes 3464 | tf_op jit(solution)/shard_map/ppermute | solution.py:775
  21.0 3.7 collective-permute-start.2
  24.6 3.7 collective-permute-start.3
  27.6 1.2 collective-permute-start.4
  28.3 1.2 collective-permute-start.5
  29.8 39.3 %collective-permute-start.13 = (bf16[48,3072]{1,0:T(8,128)(2,1)S(1)}, bf16[48,3072]{1,0:T(8,128)(2,1)S(1)}, u32[]{:S(2)}, u32[]{:S(2)}) collective-permute-start(bf16[48,3072]{1,0:T(8,128)(2,1)S(1)} %pad_maximum_fusion.10), channel_id=1, source_target_pairs={{0,2},{1,3},{2,0},{3,1},{4,6},{5,7},{6,4},{7,5},{8,10},{9,11},{10,... | collective-permute-start | bytes 884744 | tf_op jit(solution)/shard_map/ppermute | solution.py:775
  33.4 33.9 %collective-permute-start.7 = (bf16[48,3328]{1,0:T(8,128)(2,1)S(1)}, bf16[48,3328]{1,0:T(8,128)(2,1)S(1)}, u32[]{:S(2)}, u32[]{:S(2)}) collective-permute-start(bf16[48,3328]{1,0:T(8,128)(2,1)S(1)} %pad_maximum_fusion.9), channel_id=1, source_target_pairs={{0,2},{1,3},{2,0},{3,1},{4,6},{5,7},{6,4},{7,5},{8,10},{9,11},{10,... | collective-permute-start | bytes 958472 | tf_op jit(solution)/shard_map/ppermute | solution.py:775
  33.5 46.2 %collective-permute-start.19 = (bf16[48,3072]{1,0:T(8,128)(2,1)S(1)}, bf16[48,3072]{1,0:T(8,128)(2,1)S(1)}, u32[]{:S(2)}, u32[]{:S(2)}) collective-permute-start(bf16[48,3072]{1,0:T(8,128)(2,1)S(1)} %pad_maximum_fusion.11), channel_id=1, source_target_pairs={{0,2},{1,3},{2,0},{3,1},{4,6},{5,7},{6,4},{7,5},{8,10},{9,11},{10,... | collective-permute-start | bytes 884744 | tf_op jit(solution)/shard_map/ppermute | solution.py:775
  67.5 10.5 %collective-permute-start.8 = (bf16[96,3328]{1,0:T(8,128)(2,1)S(1)}, bf16[96,3328]{1,0:T(8,128)(2,1)S(1)}, u32[]{:S(2)}, u32[]{:S(2)}) collective-permute-start(bf16[96,3328]{1,0:T(8,128)(2,1)S(1)} %pad_maximum_fusion.6), channel_id=1, source_target_pairs={{0,8},{1,9},{2,10},{3,11},{4,20},{5,21},{6,22},{7,23},{8,0},{9,1},... | collective-permute-start | bytes 1916936 | tf_op jit(solution)/shard_map/ppermute | solution.py:775
  70.1 19.5 %collective-permute-start.14 = (bf16[96,3072]{1,0:T(8,128)(2,1)}, bf16[96,3072]{1,0:T(8,128)(2,1)}, u32[]{:S(2)}, u32[]{:S(2)}) collective-permute-start(bf16[96,3072]{1,0:T(8,128)(2,1)} %pad_maximum_fusion.7), channel_id=1, source_target_pairs={{0,8},{1,9},{2,10},{3,11},{4,20},{5,21},{6,22},{7,23},{8,0},{9,1},... | collective-permute-start | bytes 1769480 | tf_op jit(solution)/shard_map/ppermute | solution.py:775
  78.1 15.1 %copy-start = (bf16[192,3328]{1,0:T(8,128)(2,1)}, bf16[192,3328]{1,0:T(8,128)(2,1)S(1)}, u32[]{:S(2)}) copy-start(bf16[192,3328]{1,0:T(8,128)(2,1)S(1)} %pad_maximum_fusion.2.rest_0_.rest_2_.rest_6_) | copy-start | bytes 3833860
  78.1 24.5 %collective-permute-start.9 = (bf16[192,3328]{1,0:T(8,128)(2,1)S(1)}, bf16[192,3328]{1,0:T(8,128)(2,1)S(1)}, u32[]{:S(2)}, u32[]{:S(2)}) collective-permute-start(bf16[192,3328]{1,0:T(8,128)(2,1)S(1)} %pad_maximum_fusion.2.rest_0_.rest_2_.rest_6_), channel_id=1, source_target_pairs={{0,16},{1,17},{2,18},{3,19},{4,12},{5,13},{6,14},{7,15},{8,24},{9,... | collective-permute-start | bytes 3833864 | tf_op jit(solution)/shard_map/ppermute | solution.py:775
  81.4 23.2 %collective-permute-start.20 = (bf16[96,3072]{1,0:T(8,128)(2,1)}, bf16[96,3072]{1,0:T(8,128)(2,1)}, u32[]{:S(2)}, u32[]{:S(2)}) collective-permute-start(bf16[96,3072]{1,0:T(8,128)(2,1)} %pad_maximum_fusion.8), channel_id=1, source_target_pairs={{0,8},{1,9},{2,10},{3,11},{4,20},{5,21},{6,22},{7,23},{8,0},{9,1},... | collective-permute-start | bytes 1769480 | tf_op jit(solution)/shard_map/ppermute | solution.py:775
  83.3 21.2 %copy-start.3 = (bf16[48,3072]{1,0:T(8,128)(2,1)S(1)}, bf16[48,3072]{1,0:T(8,128)(2,1)}, u32[]{:S(2)}) copy-start(bf16[48,3072]{1,0:T(8,128)(2,1)} %copy-done.2) | copy-start | bytes 884740
  91.7 23.6 %collective-permute-start.15 = (bf16[192,3072]{1,0:T(8,128)(2,1)}, bf16[192,3072]{1,0:T(8,128)(2,1)}, u32[]{:S(2)}, u32[]{:S(2)}) collective-permute-start(bf16[192,3072]{1,0:T(8,128)(2,1)} %pad_maximum_fusion.3.rest_0_), channel_id=1, source_target_pairs={{0,16},{1,17},{2,18},{3,19},{4,12},{5,13},{6,14},{7,15},{8,24},{9,... | collective-permute-start | bytes 3538952 | tf_op jit(solution)/shard_map/ppermute | solution.py:775
  93.2 36.3 %collective-permute-start.10 = (bf16[192,3328]{1,0:T(8,128)(2,1)S(1)}, bf16[192,3328]{1,0:T(8,128)(2,1)}, u32[]{:S(2)}, u32[]{:S(2)}) collective-permute-start(bf16[192,3328]{1,0:T(8,128)(2,1)S(1)} %pad_maximum_fusion.2.rest_0_.rest_2_.rest_6_), channel_id=1, source_target_pairs={{0,4},{1,5},{2,6},{3,7},{4,0},{5,1},{6,2},{7,3},{8,12},{9,13},{10,... | collective-permute-start | bytes 3833864 | tf_op jit(solution)/shard_map/ppermute | solution.py:775
  102.6 27.0 %collective-permute-start.11 = (bf16[192,3328]{1,0:T(8,128)(2,1)S(1)}, bf16[192,3328]{1,0:T(8,128)(2,1)}, u32[]{:S(2)}, u32[]{:S(2)}) collective-permute-start(bf16[192,3328]{1,0:T(8,128)(2,1)S(1)} %collective-permute-done.9.rest_1_.rest_3_.rest_7_), channel_id=1, source_target_pairs={{0,4},{1,5},{2,6},{3,7},{4,0},{5,1},{6,2},{7,3},{8,12},{9,13},{10,... | collective-permute-start | bytes 3833864 | tf_op jit(solution)/shard_map/ppermute | solution.py:775
  106.7 21.2 %collective-permute-start.21 = (bf16[192,3072]{1,0:T(8,128)(2,1)}, bf16[192,3072]{1,0:T(8,128)(2,1)}, u32[]{:S(2)}, u32[]{:S(2)}) collective-permute-start(bf16[192,3072]{1,0:T(8,128)(2,1)} %pad_maximum_fusion.4.rest_0_), channel_id=1, source_target_pairs={{0,16},{1,17},{2,18},{3,19},{4,12},{5,13},{6,14},{7,15},{8,24},{9,... | collective-permute-start | bytes 3538952 | tf_op jit(solution)/shard_map/ppermute | solution.py:775
  113.8 92.8 %collective-permute-start.16 = (bf16[192,3072]{1,0:T(8,128)(2,1)}, bf16[192,3072]{1,0:T(8,128)(2,1)S(1)}, u32[]{:S(2)}, u32[]{:S(2)}) collective-permute-start(bf16[192,3072]{1,0:T(8,128)(2,1)} %pad_maximum_fusion.3.rest_0_), channel_id=1, source_target_pairs={{0,4},{1,5},{2,6},{3,7},{4,0},{5,1},{6,2},{7,3},{8,12},{9,13},{10,... | collective-permute-start | bytes 3538952 | tf_op jit(solution)/shard_map/ppermute | solution.py:775
  115.3 122.9 %collective-permute-start.22 = (bf16[192,3072]{1,0:T(8,128)(2,1)}, bf16[192,3072]{1,0:T(8,128)(2,1)S(1)}, u32[]{:S(2)}, u32[]{:S(2)}) collective-permute-start(bf16[192,3072]{1,0:T(8,128)(2,1)} %pad_maximum_fusion.4.rest_0_), channel_id=1, source_target_pairs={{0,4},{1,5},{2,6},{3,7},{4,0},{5,1},{6,2},{7,3},{8,12},{9,13},{10,... | collective-permute-start | bytes 3538952 | tf_op jit(solution)/shard_map/ppermute | solution.py:775
  128.0 78.7 %collective-permute-start.17 = (bf16[192,3072]{1,0:T(8,128)(2,1)}, bf16[192,3072]{1,0:T(8,128)(2,1)S(1)}, u32[]{:S(2)}, u32[]{:S(2)}) collective-permute-start(bf16[192,3072]{1,0:T(8,128)(2,1)} %collective-permute-done.15.rest_1_), channel_id=1, source_target_pairs={{0,4},{1,5},{2,6},{3,7},{4,0},{5,1},{6,2},{7,3},{8,12},{9,13},{10,... | collective-permute-start | bytes 3538952 | tf_op jit(solution)/shard_map/ppermute | solution.py:775
  129.5 108.7 %collective-permute-start.23 = (bf16[192,3072]{1,0:T(8,128)(2,1)}, bf16[192,3072]{1,0:T(8,128)(2,1)S(1)}, u32[]{:S(2)}, u32[]{:S(2)}) collective-permute-start(bf16[192,3072]{1,0:T(8,128)(2,1)} %collective-permute-done.21.rest_1_), channel_id=1, source_target_pairs={{0,4},{1,5},{2,6},{3,7},{4,0},{5,1},{6,2},{7,3},{8,12},{9,13},{10,... | collective-permute-start | bytes 3538952 | tf_op jit(solution)/shard_map/ppermute | solution.py:775
  336.7 16.3 %copy-start.25 = (f32[1,1536]{1,0:T(1,128)S(1)}, f32[1,1536]{1,0:T(1,128)}, u32[]{:S(2)}) copy-start(f32[1,1536]{1,0:T(1,128)} %get-tuple-element.99) | copy-start | bytes 18436
  336.7 16.3 %copy-start.26 = (f32[1,1536]{1,0:T(1,128)S(1)}, f32[1,1536]{1,0:T(1,128)}, u32[]{:S(2)}) copy-start(f32[1,1536]{1,0:T(1,128)} %get-tuple-element.100) | copy-start | bytes 18436
  336.7 16.8 %copy-start.23 = (f32[8,768]{1,0:T(8,128)S(1)}, f32[8,768]{1,0:T(8,128)}, u32[]{:S(2)}) copy-start(f32[8,768]{1,0:T(8,128)} %get-tuple-element.98) | copy-start | bytes 73732
  336.8 18.0 %copy-start.27 = (pred[8]{0:T(512)(128)(4,1)S(1)}, pred[8]{0:T(512)(128)(4,1)}, u32[]{:S(2)}) copy-start(pred[8]{0:T(512)(128)(4,1)} %compare_and_fusion) | copy-start | bytes 28
  336.8 21.1 %copy-start.36 = (bf16[2,96,3072]{2,1,0:T(8,128)(2,1)S(1)}, bf16[2,96,3072]{2,1,0:T(8,128)(2,1)}, u32[]{:S(2)}) copy-start(bf16[2,96,3072]{2,1,0:T(8,128)(2,1)} %get-tuple-element.114) | copy-start | bytes 3538948
  354.9 1.4 collective-permute-start.25
  355.4 2.9 collective-permute-start.24
  356.3 3.7 collective-permute-start.26
  357.8 39.6 %collective-permute-start.43 = (bf16[2,96,3072]{2,1,0:T(8,128)(2,1)}, bf16[2,96,3072]{2,1,0:T(8,128)(2,1)S(1)}, u32[]{:S(2)}, u32[]{:S(2)}) collective-permute-start(bf16[2,96,3072]{2,1,0:T(8,128)(2,1)} %get-tuple-element.116), channel_id=1, source_target_pairs={{0,4},{1,5},{2,6},{3,7},{4,0},{5,1},{6,2},{7,3},{8,12},{9,13},{10,... | collective-permute-start | bytes 3538952 | tf_op jit(solution)/shard_map/ppermute | solution.py:775
  357.8 92.5 %collective-permute-start.42 = (bf16[2,96,3072]{2,1,0:T(8,128)(2,1)S(1)}, bf16[2,96,3072]{2,1,0:T(8,128)(2,1)S(1)}, u32[]{:S(2)}, u32[]{:S(2)}) collective-permute-start(bf16[2,96,3072]{2,1,0:T(8,128)(2,1)S(1)} %copy-done.36), channel_id=1, source_target_pairs={{0,4},{1,5},{2,6},{3,7},{4,0},{5,1},{6,2},{7,3},{8,12},{9,13},{10,... | collective-permute-start | bytes 3538952 | tf_op jit(solution)/shard_map/ppermute | solution.py:775
  360.0 3.6 collective-permute-start.27
  363.6 9.5 %collective-permute-start.28 = (f32[2,288]{1,0:T(2,128)S(1)}, f32[2,288]{1,0:T(2,128)S(1)}, u32[]{:S(2)}, u32[]{:S(2)}) collective-permute-start(f32[2,288]{1,0:T(2,128)S(1)} %broadcast_select_fusion.17), channel_id=1, source_target_pairs={{0,2},{1,3},{2,0},{3,1},{4,6},{5,7},{6,4},{7,5},{8,10},{9,11},{10,... | collective-permute-start | bytes 6920 | tf_op jit(solution)/shard_map/ppermute | solution.py:775
  372.6 15.1 %collective-permute-start.37 = (bf16[2,96,1408]{2,1,0:T(8,128)(2,1)}, bf16[2,96,1408]{2,1,0:T(8,128)(2,1)S(1)}, u32[]{:S(2)}, u32[]{:S(2)}) collective-permute-start(bf16[2,96,1408]{2,1,0:T(8,128)(2,1)} %get-tuple-element.112), channel_id=1, source_target_pairs={{0,4},{1,5},{2,6},{3,7},{4,0},{5,1},{6,2},{7,3},{8,12},{9,13},{10,... | collective-permute-start | bytes 1622024 | tf_op jit(solution)/shard_map/ppermute | solution.py:775
  372.7 17.8 %collective-permute-start.36 = (bf16[2,96,1408]{2,1,0:T(8,128)(2,1)}, bf16[2,96,1408]{2,1,0:T(8,128)(2,1)S(1)}, u32[]{:S(2)}, u32[]{:S(2)}) collective-permute-start(bf16[2,96,1408]{2,1,0:T(8,128)(2,1)} %get-tuple-element.110), channel_id=1, source_target_pairs={{0,4},{1,5},{2,6},{3,7},{4,0},{5,1},{6,2},{7,3},{8,12},{9,13},{10,... | collective-permute-start | bytes 1622024 | tf_op jit(solution)/shard_map/ppermute | solution.py:775
  373.2 13.2 %collective-permute-start.29 = (f32[1,288]{1,0:T(1,128)S(1)}, f32[1,288]{1,0:T(1,128)S(1)}, u32[]{:S(2)}, u32[]{:S(2)}) collective-permute-start(f32[1,288]{1,0:T(1,128)S(1)} %broadcast_select_fusion.13), channel_id=1, source_target_pairs={{0,1},{1,0},{2,3},{3,2},{4,5},{5,4},{6,7},{7,6},{8,9},{9,8},{10,11... | collective-permute-start | bytes 3464 | tf_op jit(solution)/shard_map/ppermute | solution.py:775
  386.5 3.6 collective-permute-start.31
  387.9 9.4 %collective-permute-start.38 = (bf16[2,96,1408]{2,1,0:T(8,128)(2,1)S(1)}, bf16[2,96,1408]{2,1,0:T(8,128)(2,1)S(1)}, u32[]{:S(2)}, u32[]{:S(2)}) collective-permute-start(bf16[2,96,1408]{2,1,0:T(8,128)(2,1)S(1)} %add_convert_fusion.5), channel_id=1, source_target_pairs={{0,16},{1,17},{2,18},{3,19},{4,12},{5,13},{6,14},{7,15},{8,24},{9,... | collective-permute-start | bytes 1622024 | tf_op jit(solution)/shard_map/ppermute | solution.py:775
  390.1 9.4 %collective-permute-start.49 = (bf16[2,96,3072]{2,1,0:T(8,128)(2,1)S(1)}, bf16[2,96,3072]{2,1,0:T(8,128)(2,1)S(1)}, u32[]{:S(2)}, u32[]{:S(2)}) collective-permute-start(bf16[2,96,3072]{2,1,0:T(8,128)(2,1)S(1)} %copy-done.38), channel_id=1, source_target_pairs={{0,4},{1,5},{2,6},{3,7},{4,0},{5,1},{6,2},{7,3},{8,12},{9,13},{10,... | collective-permute-start | bytes 3538952 | tf_op jit(solution)/shard_map/ppermute | solution.py:775
  390.5 62.0 %collective-permute-start.48 = (bf16[2,96,3072]{2,1,0:T(8,128)(2,1)S(1)}, bf16[2,96,3072]{2,1,0:T(8,128)(2,1)S(1)}, u32[]{:S(2)}, u32[]{:S(2)}) collective-permute-start(bf16[2,96,3072]{2,1,0:T(8,128)(2,1)S(1)} %copy-done.37), channel_id=1, source_target_pairs={{0,4},{1,5},{2,6},{3,7},{4,0},{5,1},{6,2},{7,3},{8,12},{9,13},{10,... | collective-permute-start | bytes 3538952 | tf_op jit(solution)/shard_map/ppermute | solution.py:775
  397.3 12.5 %collective-permute-start.30 = (bf16[2,96,1920]{2,1,0:T(8,128)(2,1)S(1)}, bf16[2,96,1920]{2,1,0:T(8,128)(2,1)S(1)}, u32[]{:S(2)}, u32[]{:S(2)}) collective-permute-start(bf16[2,96,1920]{2,1,0:T(8,128)(2,1)S(1)} %copy-done.43), channel_id=1, source_target_pairs={{0,4},{1,5},{2,6},{3,7},{4,0},{5,1},{6,2},{7,3},{8,12},{9,13},{10,... | collective-permute-start | bytes 2211848 | tf_op jit(solution)/shard_map/ppermute | solution.py:775
  397.5 14.4 %collective-permute-start.32 = (bf16[2,96,1920]{2,1,0:T(8,128)(2,1)S(1)}, bf16[2,96,1920]{2,1,0:T(8,128)(2,1)S(1)}, u32[]{:S(2)}, u32[]{:S(2)}) collective-permute-start(bf16[2,96,1920]{2,1,0:T(8,128)(2,1)S(1)} %add_convert_fusion.2), channel_id=1, source_target_pairs={{0,16},{1,17},{2,18},{3,19},{4,12},{5,13},{6,14},{7,15},{8,24},{9,... | collective-permute-start | bytes 2211848 | tf_op jit(solution)/shard_map/ppermute | solution.py:775
  399.5 9.5 %collective-permute-start.39 = (bf16[96,1408]{1,0:T(8,128)(2,1)S(1)}, bf16[96,1408]{1,0:T(8,128)(2,1)S(1)}, u32[]{:S(2)}, u32[]{:S(2)}) collective-permute-start(bf16[96,1408]{1,0:T(8,128)(2,1)S(1)} %fusion.4), channel_id=1, source_target_pairs={{0,8},{1,9},{2,10},{3,11},{4,20},{5,21},{6,22},{7,23},{8,0},{9,1},... | collective-permute-start | bytes 811016 | tf_op jit(solution)/shard_map/ppermute | solution.py:775
  409.0 41.4 %collective-permute-start.44 = (bf16[2,96,3072]{2,1,0:T(8,128)(2,1)S(1)}, bf16[2,96,3072]{2,1,0:T(8,128)(2,1)S(1)}, u32[]{:S(2)}, u32[]{:S(2)}) collective-permute-start(bf16[2,96,3072]{2,1,0:T(8,128)(2,1)S(1)} %add_convert_fusion.1), channel_id=1, source_target_pairs={{0,16},{1,17},{2,18},{3,19},{4,12},{5,13},{6,14},{7,15},{8,24},{9,... | collective-permute-start | bytes 3538952 | tf_op jit(solution)/shard_map/ppermute | solution.py:775
  409.9 42.6 %collective-permute-start.50 = (bf16[2,96,3072]{2,1,0:T(8,128)(2,1)S(1)}, bf16[2,96,3072]{2,1,0:T(8,128)(2,1)S(1)}, u32[]{:S(2)}, u32[]{:S(2)}) collective-permute-start(bf16[2,96,3072]{2,1,0:T(8,128)(2,1)S(1)} %add_convert_fusion), channel_id=1, source_target_pairs={{0,16},{1,17},{2,18},{3,19},{4,12},{5,13},{6,14},{7,15},{8,24},{9,... | collective-permute-start | bytes 3538952 | tf_op jit(solution)/shard_map/ppermute | solution.py:775
  411.9 8.5 %collective-permute-start.40 = (bf16[48,1408]{1,0:T(8,128)(2,1)S(1)}, bf16[48,1408]{1,0:T(8,128)(2,1)S(1)}, u32[]{:S(2)}, u32[]{:S(2)}) collective-permute-start(bf16[48,1408]{1,0:T(8,128)(2,1)S(1)} %select_convert_fusion.5), channel_id=1, source_target_pairs={{0,2},{1,3},{2,0},{3,1},{4,6},{5,7},{6,4},{7,5},{8,10},{9,11},{10,... | collective-permute-start | bytes 405512 | tf_op jit(solution)/shard_map/ppermute | solution.py:775
  420.3 11.5 %collective-permute-start.33 = (bf16[96,1920]{1,0:T(8,128)(2,1)S(1)}, bf16[96,1920]{1,0:T(8,128)(2,1)S(1)}, u32[]{:S(2)}, u32[]{:S(2)}) collective-permute-start(bf16[96,1920]{1,0:T(8,128)(2,1)S(1)} %fusion.2), channel_id=1, source_target_pairs={{0,8},{1,9},{2,10},{3,11},{4,20},{5,21},{6,22},{7,23},{8,0},{9,1},... | collective-permute-start | bytes 1105928 | tf_op jit(solution)/shard_map/ppermute | solution.py:775
  432.1 8.6 %collective-permute-start.34 = (bf16[48,1920]{1,0:T(8,128)(2,1)S(1)}, bf16[48,1920]{1,0:T(8,128)(2,1)S(1)}, u32[]{:S(2)}, u32[]{:S(2)}) collective-permute-start(bf16[48,1920]{1,0:T(8,128)(2,1)S(1)} %select_convert_fusion.2), channel_id=1, source_target_pairs={{0,2},{1,3},{2,0},{3,1},{4,6},{5,7},{6,4},{7,5},{8,10},{9,11},{10,... | collective-permute-start | bytes 552968 | tf_op jit(solution)/shard_map/ppermute | solution.py:775
  440.7 4.3 collective-permute-start.41
  445.0 4.6 collective-permute-start.35
  451.0 9.9 %collective-permute-start.45 = (bf16[96,3072]{1,0:T(8,128)(2,1)S(1)}, bf16[96,3072]{1,0:T(8,128)(2,1)S(1)}, u32[]{:S(2)}, u32[]{:S(2)}) collective-permute-start(bf16[96,3072]{1,0:T(8,128)(2,1)S(1)} %fusion), channel_id=1, source_target_pairs={{0,8},{1,9},{2,10},{3,11},{4,20},{5,21},{6,22},{7,23},{8,0},{9,1},... | collective-permute-start | bytes 1769480 | tf_op jit(solution)/shard_map/ppermute | solution.py:775
  452.7 14.5 %collective-permute-start.51 = (bf16[96,3072]{1,0:T(8,128)(2,1)S(1)}, bf16[96,3072]{1,0:T(8,128)(2,1)S(1)}, u32[]{:S(2)}, u32[]{:S(2)}) collective-permute-start(bf16[96,3072]{1,0:T(8,128)(2,1)S(1)} %fusion.1), channel_id=1, source_target_pairs={{0,8},{1,9},{2,10},{3,11},{4,20},{5,21},{6,22},{7,23},{8,0},{9,1},... | collective-permute-start | bytes 1769480 | tf_op jit(solution)/shard_map/ppermute | solution.py:775
  461.3 20.1 %collective-permute-start.46 = (bf16[48,3072]{1,0:T(8,128)(2,1)S(1)}, bf16[48,3072]{1,0:T(8,128)(2,1)S(1)}, u32[]{:S(2)}, u32[]{:S(2)}) collective-permute-start(bf16[48,3072]{1,0:T(8,128)(2,1)S(1)} %select_convert_fusion.1), channel_id=1, source_target_pairs={{0,2},{1,3},{2,0},{3,1},{4,6},{5,7},{6,4},{7,5},{8,10},{9,11},{10,... | collective-permute-start | bytes 884744 | tf_op jit(solution)/shard_map/ppermute | solution.py:775
  467.6 19.5 %collective-permute-start.52 = (bf16[48,3072]{1,0:T(8,128)(2,1)S(1)}, bf16[48,3072]{1,0:T(8,128)(2,1)S(1)}, u32[]{:S(2)}, u32[]{:S(2)}) collective-permute-start(bf16[48,3072]{1,0:T(8,128)(2,1)S(1)} %select_convert_fusion), channel_id=1, source_target_pairs={{0,2},{1,3},{2,0},{3,1},{4,6},{5,7},{6,4},{7,5},{8,10},{9,11},{10,... | collective-permute-start | bytes 884744 | tf_op jit(solution)/shard_map/ppermute | solution.py:775
  481.5 8.7 %collective-permute-start.47 = (bf16[24,3072]{1,0:T(8,128)(2,1)S(1)}, bf16[24,3072]{1,0:T(8,128)(2,1)S(1)}, u32[]{:S(2)}, u32[]{:S(2)}) collective-permute-start(bf16[24,3072]{1,0:T(8,128)(2,1)S(1)} %select_convert_fusion.4), channel_id=1, source_target_pairs={{0,1},{1,0},{2,3},{3,2},{4,5},{5,4},{6,7},{7,6},{8,9},{9,8},{10,11... | collective-permute-start | bytes 442376 | tf_op jit(solution)/shard_map/ppermute | solution.py:775
  487.2 6.1 %collective-permute-start.53 = (bf16[24,3072]{1,0:T(8,128)(2,1)S(1)}, bf16[24,3072]{1,0:T(8,128)(2,1)S(1)}, u32[]{:S(2)}, u32[]{:S(2)}) collective-permute-start(bf16[24,3072]{1,0:T(8,128)(2,1)S(1)} %select_convert_fusion.3), channel_id=1, source_target_pairs={{0,1},{1,0},{2,3},{3,2},{4,5},{5,4},{6,7},{7,6},{8,9},{9,8},{10,11... | collective-permute-start | bytes 442376 | tf_op jit(solution)/shard_map/ppermute | solution.py:775
  (34 other events, 221.1 us)

commit v2 on v1

v2 whole, which is shorter than its diff:
```python
import functools
import jax
import jax.numpy as jnp
from jax import lax
from jax.experimental import pallas as pl
from jax.experimental.pallas import tpu as pltpu
from jax.sharding import PartitionSpec as P

HEAD_DIM = 64
RADIUS = 84
STRIDE = 16
SEQ = 512
GLOB = 32
RELS = 169
T = GLOB + SEQ
D = 768
FF = 3072
PAIRS = 6
LABELS = 256
LEAD = 4
BACK_LEAD = 3
LABEL_END = LEAD + RELS
EPS = 1e-06
NEG = -1e30
F32 = jnp.float32
BF16 = jnp.bfloat16
VMEM_LIMIT = 63 << 20
WINDOWS = ((0, 0, 256, 328, 0), (0, 0, 384, 72, 0), (1, 160, 384, 8, 352), (1, 288, 256, 8, 224))
OFFSETS = (0, 256, 640, 1024)
WAYS = 3 * 128
VEC_AT = 176
GAIN1, BIAS1, QV, OUT_B, GAIN2, BIAS2, DOWN_B, IN_B, VECS = 0, 1, 2, 4, 5, 6, 7, 8, 16
P_COLS = 1280
NN = (((1,), (0,)), ((), ()))
NT = (((1,), (1,)), ((), ()))
TN = (((0,), (0,)), ((), ()))


def dot(a, b, dims=NN):
    return lax.dot_general(a, b, dims, preferred_element_type=F32)


def run(kernel, deps, prefetch, inputs, out_shape, name, cost, grid, in_specs, out_specs, scratch_shapes):
    n = len(prefetch)

    def with_deps(*refs):
        kernel(*refs[:n], *refs[n + len(deps) :])

    anywhere = pl.BlockSpec(memory_space=pl.ANY)
    return pl.pallas_call(
        with_deps,
        grid_spec=pltpu.PrefetchScalarGridSpec(
            num_scalar_prefetch=n,
            grid=grid,
            in_specs=[anywhere] * len(deps) + in_specs,
            out_specs=out_specs,
            scratch_shapes=scratch_shapes,
        ),
        out_shape=out_shape,
        compiler_params=pltpu.CompilerParams(vmem_limit_bytes=VMEM_LIMIT),
        cost_estimate=pl.CostEstimate(flops=int(cost * 1.15e9), bytes_accessed=1 << 20, transcendentals=0),
        name=name,
    )(*prefetch, *deps, *inputs)


def after(x, deps):
    anywhere = pl.BlockSpec(memory_space=pl.ANY)
    return pl.pallas_call(
        lambda *refs: None,
        in_specs=[anywhere] * (1 + len(deps)),
        out_specs=anywhere,
        out_shape=jax.ShapeDtypeStruct(x.shape, x.dtype),
        input_output_aliases={0: 0},
        name="after",
    )(x, *deps)


def iota(shape, dim):
    return lax.broadcasted_iota(jnp.int32, shape, dim)


def norm_stats(x):
    cen = x - jnp.mean(x, axis=1, keepdims=True)
    rstd = lax.rsqrt(jnp.mean(cen * cen, axis=1, keepdims=True) + EPS)
    return cen * rstd, rstd


def norm_back(grad, xhat, rstd, gain):
    gg = grad * gain
    return rstd * (
        gg - jnp.mean(gg, axis=1, keepdims=True) - xhat * jnp.mean(gg * xhat, axis=1, keepdims=True)
    )


def tiles(cols, size=256):
    return [slice(at, min(at + size, cols)) for at in range(0, cols, size)]


def live_mask(length, cols):
    row = iota((T, cols), 0)
    glob_count = (length + STRIDE - 1) // STRIDE
    return row < jnp.where(row < GLOB, glob_count, length + GLOB)


def load_rows(pieces, pos_ref, lines, dst, sems, first_col):
    rows = dst.shape[0] // lines
    cols = dst.shape[1]
    copies = []
    k = 0
    for piece in pieces:
        for i in range(piece.shape[0] // rows):
            start = pl.multiple_of(pos_ref[k] * rows, 16)
            copies.append(
                pltpu.make_async_copy(
                    piece.at[pl.ds(i * rows, rows), pl.ds(first_col, cols)],
                    dst.at[pl.ds(start, rows), :],
                    sems.at[k],
                )
            )
            k += 1
    for copy in copies:
        copy.start()
    return copies


FIRST = 2 * 128
SECOND = D - FIRST


def owner_order(rows):
    k = iota((D, 1), 0)
    late = (k >= D // 2).astype(jnp.int32)
    k = k - late * (D // 2)
    owner = ((k.astype(F32) + 0.5) * (1.0 / rows)).astype(jnp.int32)
    col = rows * owner + k + late * rows
    return (iota((D, D), 1) == col).astype(F32).astype(BF16)


def project_kernel(lines, n_pieces, first, rows, pos_ref, *rest):
    if first:
        long_ref, glob_ref = rest[:2]
    else:
        normed_ref, vec_ref = rest[:2]
    pieces = rest[2 : 2 + n_pieces]
    if first:
        proj_ref, normed_ref, rel_ref, relt_ref, vec_ref, w_s, sems = rest[2 + n_pieces :]
    else:
        proj_ref, w_s, sems = rest[2 + n_pieces :]
    cols = proj_ref.shape[1]
    width = cols // 3
    copies = load_rows(pieces, pos_ref, lines, w_s, sems.at[0], 0)
    if first:
        for copy in load_rows(pieces, pos_ref, lines, rel_ref, sems.at[1], cols):
            copy.wait()
        turned = rel_ref[...].astype(F32).T
        vec_ref[...] = turned[VEC_AT : VEC_AT + VECS]
        drop = LEAD - BACK_LEAD
        labels = jnp.concatenate([turned[drop:], turned[:drop]], axis=0)
        label = iota((LABELS, D), 0) - BACK_LEAD
        relt_ref[...] = jnp.where((label >= 0) & (label < RELS), labels, 0.0).astype(BF16)
        a, b = vec_ref[QV : QV + 1], vec_ref[QV + 1 : QV + 2]
        half = D // 2
        sides = jnp.concatenate(
            [
                jnp.concatenate([a[:, :half], b[:, :half]], axis=1),
                jnp.concatenate([a[:, half:], b[:, half:]], axis=1),
            ],
            axis=0,
        )
        vec_ref[QV : QV + 2] = dot(sides.astype(BF16), owner_order(rows))
        for s in range(long_ref.shape[0]):
            for part, at, size in ((glob_ref, T * s, GLOB), (long_ref, T * s + GLOB, SEQ)):
                xhat, _ = norm_stats(part[s, 0].astype(F32))
                normed_ref[at : at + size] = (
                    xhat * vec_ref[GAIN1 : GAIN1 + 1] + vec_ref[BIAS1 : BIAS1 + 1]
                ).astype(BF16)
    own = slice(0, width) if first else slice(D - width, D)
    full_bias = jnp.concatenate(
        [vec_ref[QV : QV + 1, own], jnp.zeros((1, width), F32), vec_ref[QV + 1 : QV + 2, own]], axis=1
    )
    for copy in copies:
        copy.wait()
    for c in tiles(cols):
        out = (dot(normed_ref[...], w_s[:, c]) + full_bias[:, c]).astype(BF16)
        for at in range(c.start, c.stop, 128):
            to = by_pair(at, width)
            proj_ref[:, to : to + 128] = out[:, at - c.start : at - c.start + 128]


def by_pair(col, width):
    return WAYS * (col % width // 128) + 128 * (col // width)


VMEM = pl.BlockSpec(memory_space=pltpu.VMEM)
ANY = pl.BlockSpec(memory_space=pl.ANY)


def project_first(deps, pos, long_in, glob_in, pieces, owned, cols):
    rows = long_in.shape[0] * T
    lines = pos.shape[0]
    shape = lambda *dims: jax.ShapeDtypeStruct(dims, BF16)
    return run(
        functools.partial(project_kernel, lines, len(pieces), True, owned),
        deps,
        [pos],
        [long_in, glob_in, *pieces],
        [
            shape(rows, cols),
            shape(rows, D),
            shape(D, LABELS),
            shape(LABELS, D),
            jax.ShapeDtypeStruct((VECS, D), F32),
        ],
        "project",
        9,
        grid=(1,),
        in_specs=[VMEM] * 2 + [ANY] * len(pieces),
        out_specs=[VMEM] * 5,
        scratch_shapes=[pltpu.VMEM((D, cols), BF16), pltpu.SemaphoreType.DMA((2, lines))],
    )


def project_next(deps, pos, normed, vec, pieces, cols):
    rows = normed.shape[0]
    lines = pos.shape[0]
    return run(
        functools.partial(project_kernel, lines, len(pieces), False, 0),
        deps,
        [pos],
        [normed, vec, *pieces],
        [jax.ShapeDtypeStruct((rows, cols), BF16)],
        "project",
        8,
        grid=(1,),
        in_specs=[VMEM] * 2 + [ANY] * len(pieces),
        out_specs=[VMEM],
        scratch_shapes=[pltpu.VMEM((D, cols), BF16), pltpu.SemaphoreType.DMA((2, lines))],
    )[0]


def flip_matrix(size):
    row, col = iota((size, size), 0), iota((size, size), 1)
    return ((row // 128 == col // 128) & (row % 128 + col % 128 == 127)).astype(F32).astype(BF16)


def by_head(x):
    even = iota(x.shape, 1) < HEAD_DIM
    return jnp.concatenate([jnp.where(even, x, 0.0), jnp.where(even, 0.0, x)], axis=0)


def by_lane(x):
    half = x.shape[0] // 2
    even = iota((half, x.shape[1]), 1) < HEAD_DIM
    return jnp.where(even, x[:half], x[half:])


def spread(x, b):
    _, _, width, shift, _ = WINDOWS[b]
    shift = shift if shift < 256 else shift - 384
    lane = iota((64, 128), 1)
    none = jnp.full((64, 128), NEG, F32)
    parts = []
    for at in range(0, 256, 64):
        start = shift + at % 128
        turned = pltpu.roll(x[at : at + 64], start % 256, 1, stride=1, stride_axis=0)
        low, high = turned[:, :128], turned[:, 128:]
        if start < 0:
            cols = [low, jnp.where(lane < 64, high, NEG), none]
        elif start + 64 + LABEL_END <= 256:
            cols = [low, high, none]
        elif start >= 128:
            cols = [none, high, low]
        else:
            cols = [jnp.where(lane >= 64, low, NEG), high, jnp.where(lane < 64, low, NEG)]
        parts.append(jnp.concatenate(cols[: width // 128], axis=1))
    return jnp.concatenate(parts, axis=0)


def collect(cols, b):
    _, _, width, shift, _ = WINDOWS[b]
    shift = shift if shift < 256 else shift - 384
    lane = iota((64, 128), 1)
    parts = []
    for at in range(0, 256, 64):
        start = shift + 64 - at % 128
        tiles_ = [c[at : at + 64] for c in cols]
        if start < 0:
            low, high = tiles_[0], jnp.where(lane < 64, tiles_[1], 0.0)
        elif start + 64 + LABEL_END <= 256:
            low, high = tiles_[0], tiles_[1]
        elif start >= 128:
            low, high = tiles_[2], tiles_[1]
        elif len(tiles_) > 2:
            low, high = jnp.where(lane >= 64, tiles_[0], tiles_[2]), tiles_[1]
        else:
            low, high = jnp.where(lane >= 64, tiles_[0], 0.0), tiles_[1]
        back = (BACK_LEAD - LEAD - 63 - start) % 256
        parts.append(
            pltpu.roll(jnp.concatenate([low, high], axis=1), back, 1, stride=1, stride_axis=0)
        )
    return jnp.concatenate(parts, axis=0)


def zero_glob(x, at):
    cols = [x[:, 128 * i : 128 * (i + 1)] for i in range(x.shape[1] // 128)]
    lane = iota(cols[0].shape, 1) - at % 128
    cols[at // 128] = jnp.where((lane >= 0) & (lane < GLOB), 0.0, cols[at // 128])
    return cols


def attend_kernel(len_ref, qkv_ref, rel_ref, mix_ref, inv_ref, p_ref, pg_ref, k_s, v_s, rel_s):
    dead = jnp.where(live_mask(len_ref[pl.program_id(0)], 128), 0.0, NEG)
    flag = iota((T, 128), 1) == 0
    k = jnp.concatenate(
        [qkv_ref[:, 128:256], jnp.where(flag, dead, 0.0).astype(BF16)], axis=1
    )
    v = jnp.concatenate([qkv_ref[:, 256:384], jnp.ones((T, 128), BF16)], axis=1)
    for s, m in ((k_s, k), (v_s, v)):
        s[0] = m
        s[1, :SEQ] = m[GLOB:]
        s[1, SEQ:] = m[:GLOB]
    label = iota((128, LABELS), 1)
    outside = ((label < LEAD) | (label >= LEAD + RELS)) & (iota((128, LABELS), 0) == 0)
    rel_s[:128] = rel_ref[...]
    rel_s[128:] = jnp.where(outside, NEG, 0.0).astype(BF16)
    flip = flip_matrix(256)

    def queries(rows):
        x = by_head(qkv_ref[rows, :128].astype(F32) * 0.125)
        one = (iota(x.shape, 1) == 0).astype(F32)
        return jnp.concatenate([x, one], axis=1).astype(BF16)

    def weights(scores):
        return jnp.exp(scores - jnp.max(scores, axis=1, keepdims=True)).astype(BF16)

    rows = [slice(0, GLOB)] + [slice(GLOB + 128 * b, GLOB + 128 * (b + 1)) for b in range(4)]
    wins = [(0, slice(0, T))] + [(arr, slice(first, first + width)) for arr, first, width, _, _ in WINDOWS]
    qs = [queries(r) for r in rows]
    scores = [dot(q, k_s[arr, win], NT) for q, (arr, win) in zip(qs, wins)]
    biases = [dot(q, rel_s[...]) for q in qs[1:]]
    for b, window in enumerate(WINDOWS):
        bias = zero_glob(spread(biases[b], b), window[-1])
        scores[b + 1] = scores[b + 1] + jnp.concatenate(bias, axis=1)
    ps = [weights(x) for x in scores]
    pg_ref[0, 0] = ps[0]
    outs = [dot(p, v_s[arr, win]) for p, (arr, win) in zip(ps, wins)]
    turned = [dot(flip, p) for p in ps[1:]]
    for r, out in zip(rows, outs):
        inv = by_lane(1.0 / out[:, 128:])
        inv_ref[r] = inv
        mix_ref[r] = (by_lane(out[:, :128]) * inv).astype(BF16)
    for b, p in enumerate(turned):
        p_ref[0, 0, :, OFFSETS[b] : OFFSETS[b] + p.shape[1]] = p.astype(BF16)


def attend(deps, lengths, proj, rel, first_pair):
    rows = proj.shape[0]
    seqs = rows // T
    pairs = proj.shape[1] // WAYS
    return run(
        attend_kernel,
        deps,
        [lengths],
        [proj, rel],
        [
            jax.ShapeDtypeStruct((rows, pairs * 128), BF16),
            jax.ShapeDtypeStruct((rows, pairs * 128), F32),
            jax.ShapeDtypeStruct((seqs, pairs, 256, P_COLS), BF16),
            jax.ShapeDtypeStruct((seqs, pairs, 2 * GLOB, T), BF16),
        ],
        "attend",
        6.2 * pairs,
        grid=(seqs, pairs),
        in_specs=[
            pl.BlockSpec((T, WAYS), lambda s, p, *_: (s, p)),
            pl.BlockSpec((128, LABELS), lambda s, p, *_: (first_pair + p, 0)),
        ],
        out_specs=[
            pl.BlockSpec((T, 128), lambda s, p, *_: (s, p)),
            pl.BlockSpec((T, 128), lambda s, p, *_: (s, p)),
            pl.BlockSpec((1, 1, 256, P_COLS), lambda s, p, *_: (s, p, 0, 0)),
            pl.BlockSpec((1, 1, 2 * GLOB, T), lambda s, p, *_: (s, p, 0, 0)),
        ],
        scratch_shapes=[
            pltpu.VMEM((2, T, 256), BF16),
            pltpu.VMEM((2, T, 256), BF16),
            pltpu.VMEM((256, LABELS), BF16),
        ],
    )


def attend_back_kernel(qkv_ref, relt_ref, do_ref, o_ref, inv_ref, p_ref, pg_ref, grad_ref, grel_ref, gk_s, gv_s, k_s, v_s):
    k = qkv_ref[:, 128:256]
    v = qkv_ref[:, 256:384]
    for s, m in ((k_s, k), (v_s, v)):
        s[0] = m
        s[1, :SEQ] = m[GLOB:]
        s[1, SEQ:] = m[:GLOB]
    flip = flip_matrix(128)

    @pl.when(pl.program_id(1) == 0)
    def _():
        grel_ref[...] = jnp.zeros_like(grel_ref)

    ones = jnp.ones((256, 128), BF16)

    def score_grads(do, o, p, v_win):
        prod = by_head(do * o)
        high = prod.astype(BF16)
        low = (prod - high.astype(F32)).astype(BF16)
        centre = dot(jnp.concatenate([high, low], axis=1), ones)
        dom = by_head(do).astype(BF16)
        dp = dot(dom, v_win, NT)
        width = dp.shape[1]
        cols = [dp[:, c] - centre[:, : c.stop - c.start] for c in tiles(width, 128)]
        return dom, p.astype(F32) * jnp.concatenate(cols, axis=1)

    do = (do_ref[:GLOB].astype(F32) * inv_ref[:GLOB]).astype(BF16).astype(F32)
    p = pg_ref[0, 0]
    dom, ds = score_grads(do, o_ref[:GLOB].astype(F32), p, v_s[0])
    ds = ds.astype(BF16)
    qm = by_head(qkv_ref[:GLOB, :128].astype(F32)).astype(BF16)
    grad_ref[:GLOB, :128] = (by_lane(dot(ds, k_s[0])) * 0.125).astype(BF16)
    gk_s[...] = dot(ds, qm, TN)
    gv_s[...] = dot(p, dom, TN)
    blocks = range(4)
    rows = [slice(GLOB + 128 * b, GLOB + 128 * (b + 1)) for b in blocks]
    wins = [(arr, slice(first, first + width)) for arr, first, width, _, _ in WINDOWS]
    turned = [
        dot(
            flip,
            jnp.concatenate(
                [
                    qkv_ref[r, :128],
                    (do_ref[r].astype(F32) * inv_ref[r]).astype(BF16),
                    o_ref[r],
                ],
                axis=1,
            ),
        )
        for r in rows
    ]
    qms = [by_head(x[:, :128]) for x in turned]
    qm_ts = [x.T.astype(BF16) for x in qms]
    qms = [x.astype(BF16) for x in qms]
    ps = [p_ref[0, 0, :, OFFSETS[b] : OFFSETS[b] + WINDOWS[b][2]] for b in blocks]
    grads = [
        score_grads(x[:, 128:256], x[:, 256:], p, v_s[arr, win])
        for x, p, (arr, win) in zip(turned, ps, wins)
    ]
    doms = [dom for dom, _ in grads]
    dss = [ds.astype(BF16) for _, ds in grads]
    labs = []
    for b, window in enumerate(WINDOWS):
        labs.append(collect(zero_glob(grads[b][1], window[-1]), b).astype(BF16))
    gqs = [
        by_lane(dot(ds, k_s[arr, win]) + dot(lab, relt_ref[...])) * 0.125
        for ds, lab, (arr, win) in zip(dss, labs, wins)
    ]
    gks = [dot(ds, qm, TN) for ds, qm in zip(dss, qms)]
    gvs = [dot(p, dom, TN) for p, dom in zip(ps, doms)]
    grel = sum(dot(qm_t, lab) for qm_t, lab in zip(qm_ts, labs))
    grel_ref[...] += grel * 0.125
    for r, gq in zip(rows, gqs):
        grad_ref[r, :128] = dot(flip, gq.astype(BF16)).astype(BF16)
    for b, (arr, first, width, _, _) in enumerate(WINDOWS):
        win = wins[b][1]
        for acc, part in ((gk_s, gks[b]), (gv_s, gvs[b])):
            if arr == 0:
                acc[win] += part
            else:
                acc[GLOB + first : T] += part[: width - GLOB]
                acc[:GLOB] += part[width - GLOB :]
    grad_ref[:, 128:256] = (gk_s[...] * 0.125).astype(BF16)
    grad_ref[:, 256:384] = gv_s[...].astype(BF16)


def attend_back(deps, proj, relt, gmixed, mixed, inv, p, pg, first_pair, start, pairs):
    rows = proj.shape[0]
    seqs = rows // T
    return run(
        attend_back_kernel,
        deps,
        [],
        [proj, relt, gmixed, mixed, inv, p, pg],
        [
            jax.ShapeDtypeStruct((rows, pairs * WAYS), BF16),
            jax.ShapeDtypeStruct((pairs * 128, LABELS), F32),
        ],
        "attend_back",
        8 * pairs,
        grid=(pairs, seqs),
        in_specs=[
            pl.BlockSpec((T, WAYS), lambda p, s: (s, start + p)),
            pl.BlockSpec((LABELS, 128), lambda p, s: (0, first_pair + start + p)),
            pl.BlockSpec((T, 128), lambda p, s: (s, first_pair + start + p)),
            pl.BlockSpec((T, 128), lambda p, s: (s, start + p)),
            pl.BlockSpec((T, 128), lambda p, s: (s, start + p)),
            pl.BlockSpec((1, 1, 256, P_COLS), lambda p, s: (s, start + p, 0, 0)),
            pl.BlockSpec((1, 1, 2 * GLOB, T), lambda p, s: (s, start + p, 0, 0)),
        ],
        out_specs=[pl.BlockSpec((T, WAYS), lambda p, s: (s, p)), pl.BlockSpec((128, LABELS), lambda p, s: (p, 0))],
        scratch_shapes=[
            pltpu.VMEM((T, 128), F32),
            pltpu.VMEM((T, 128), F32),
            pltpu.VMEM((2, T, 128), BF16),
            pltpu.VMEM((2, T, 128), BF16),
        ],
    )


def mix_out_kernel(lines, n_pieces, first_col, n_mix, pos_ref, len_ref, long_ref, glob_ref, clong_ref, cglob_ref, vec_ref, *rest):
    mixed = rest[:n_mix]
    pieces = rest[n_mix : n_mix + n_pieces]
    res_ref, n2_ref, g_ref, w_s, sems = rest[n_mix + n_pieces :]
    copies = load_rows(pieces, pos_ref, lines, w_s, sems, first_col)
    seqs = long_ref.shape[0]
    for s in range(seqs):
        live = live_mask(len_ref[s], D)
        at = T * s
        g_ref[at : at + GLOB] = jnp.where(live[:GLOB], cglob_ref[s, 0].astype(F32), 0.0).astype(BF16)
        g_ref[at + GLOB : at + T] = jnp.where(live[GLOB:], clong_ref[s, 0].astype(F32), 0.0).astype(BF16)
    for copy in copies:
        copy.wait()
    for c in tiles(D):
        acc = vec_ref[OUT_B : OUT_B + 1, c]
        at = 0
        for m in mixed:
            acc = acc + dot(m[...], w_s[at : at + m.shape[1], c])
            at += m.shape[1]
        res_ref[:, c] = acc
    for s in range(seqs):
        for part, at, size in ((glob_ref, T * s, GLOB), (long_ref, T * s + GLOB, SEQ)):
            res = res_ref[at : at + size] + part[s, 0].astype(F32)
            res_ref[at : at + size] = res
            xhat, _ = norm_stats(res)
            n2_ref[at : at + size] = (
                xhat * vec_ref[GAIN2 : GAIN2 + 1] + vec_ref[BIAS2 : BIAS2 + 1]
            ).astype(BF16)


def mix_out(deps, pos, lengths, long_in, glob_in, cot_long, cot_glob, vec, mixed, pieces, first_col):
    rows = long_in.shape[0] * T
    lines = pos.shape[0]
    return run(
        functools.partial(mix_out_kernel, lines, len(pieces), first_col, len(mixed)),
        deps,
        [pos, lengths],
        [long_in, glob_in, cot_long, cot_glob, vec, *mixed, *pieces],
        [
            jax.ShapeDtypeStruct((rows, D), F32),
            jax.ShapeDtypeStruct((rows, D), BF16),
            jax.ShapeDtypeStruct((rows, D), BF16),
        ],
        "mix_out",
        10,
        grid=(1,),
        in_specs=[VMEM] * (5 + len(mixed)) + [ANY] * len(pieces),
        out_specs=[VMEM] * 3,
        scratch_shapes=[pltpu.VMEM((D, D), BF16), pltpu.SemaphoreType.DMA((lines,))],
    )


def store_rows(src, outs, rows, src_pos_ref, sems, first_col):
    cols = src.shape[1]
    copies = []
    k = 0
    for out in outs:
        for i in range(out.shape[0]):
            start = pl.multiple_of(src_pos_ref[k] * rows, 16)
            copies.append(
                pltpu.make_async_copy(
                    src.at[pl.ds(start, rows), :], out.at[i, :, pl.ds(first_col, cols)], sems.at[k]
                )
            )
            k += 1
    return copies


def gelu_parts(v):
    cdf = 0.5 * (1.0 + lax.erf(v * 0.7071067811865476))
    pdf = jnp.exp(v * v * -0.5) * 0.3989422804014327
    return v * cdf, cdf + v * pdf


def ffn_kernel(lines, n_in, n_parts, n_out, first, pos_ref, n2_ref, g_ref, vec_ref, *rest):
    pieces = rest[:n_in]
    y_ref, gn2_ref, gb_ref = rest[n_in : n_in + 3]
    outs = rest[n_in + 3 : n_in + 3 + n_out]
    w_in_s, w_down_s, act_s, gpre_s, gw_s, sems, out_sems = rest[n_in + 3 + n_out :]
    part = pl.program_id(0)
    piece_rows = outs[0].shape[1]

    @pl.when(part == 0)
    def _():
        copies = []
        for i in range(n_parts):
            copies += load_rows(pieces, pos_ref, lines, w_in_s.at[i], sems.at[2 * i], (2 * first + i) * D)
            copies += load_rows(pieces, pos_ref, lines, w_down_s.at[i], sems.at[2 * i + 1], (2 * first + n_parts + i) * D)
        for copy in copies:
            copy.wait()

    for c in tiles(D):
        pre = dot(n2_ref[...], w_in_s[part, :, c]) + vec_ref[pl.ds(IN_B + first + part, 1), c]
        act, slope = gelu_parts(pre)
        act_s[:, c] = act.astype(BF16)
        gpre = (dot(g_ref[...], w_down_s[part, c, :], NT) * slope).astype(BF16)
        gpre_s[:, c] = gpre
        gb_ref[:, c] = jnp.sum(gpre.astype(F32), axis=0, keepdims=True)

    def flush(which):
        first = pl.multiple_of((which * n_parts + part) * D, 128)
        return store_rows(gw_s.at[which], outs, piece_rows, pos_ref, out_sems.at[which], first)

    for which, (lhs, rhs) in enumerate(((n2_ref, gpre_s), (act_s, g_ref))):
        for c in tiles(D):
            gw_s[which, :, c] = dot(lhs[...], rhs[:, c], TN).astype(BF16)
        for copy in flush(which):
            copy.start()

    def outputs(add):
        for c in tiles(D):
            y = dot(act_s[...], w_down_s[part, :, c])
            gn2 = dot(gpre_s[...], w_in_s[part, c, :], NT)
            y_ref[:, c] = y_ref[:, c] + y if add else y
            gn2_ref[:, c] = gn2_ref[:, c] + gn2 if add else gn2

    pl.when(part == 0)(lambda: outputs(False))
    if n_parts > 1:
        pl.when(part > 0)(lambda: outputs(True))
    for which in range(2):
        for copy in flush(which):
            copy.wait()


def ffn(deps, pos, n2, g, vec, pieces, first, n_parts, out_groups):
    rows = n2.shape[0]
    lines = pos.shape[0]
    full = pl.BlockSpec((rows, D), lambda q, *_: (0, 0))
    return run(
        functools.partial(ffn_kernel, lines, len(pieces), n_parts, len(out_groups), first),
        deps,
        [pos],
        [n2, g, vec, *pieces],
        [
            jax.ShapeDtypeStruct((rows, D), F32),
            jax.ShapeDtypeStruct((rows, D), F32),
            jax.ShapeDtypeStruct((1, n_parts * D), F32),
        ]
        + [jax.ShapeDtypeStruct((k, D // lines, 2 * n_parts * D), BF16) for k in out_groups],
        "ffn",
        28,
        grid=(n_parts,),
        in_specs=[full, full, VMEM] + [ANY] * len(pieces),
        out_specs=[full, full, pl.BlockSpec((1, D), lambda q, *_: (0, q))] + [ANY] * len(out_groups),
        scratch_shapes=[
            pltpu.VMEM((n_parts, D, D), BF16),
            pltpu.VMEM((n_parts, D, D), BF16),
            pltpu.VMEM((rows, D), BF16),
            pltpu.VMEM((rows, D), BF16),
            pltpu.VMEM((2, D, D), BF16),
            pltpu.SemaphoreType.DMA((2 * n_parts, lines)),
            pltpu.SemaphoreType.DMA((2, lines)),
        ],
    )


def mid_kernel(lines, n_in, first_col, n_mix, n_part, pos_ref, len_ref, res_ref, g_ref, vec_ref, *rest):
    ys = rest[:n_part]
    gns = rest[n_part : 2 * n_part]
    mixed = rest[2 * n_part : 2 * n_part + n_mix]
    rest = rest[2 * n_part + n_mix :]
    pieces = rest[:n_in]
    long_ref, glob_ref, gres_ref, gmix_ref, small_ref, gw_ref = rest[n_in : n_in + 6]
    w_s, gattn_s, gw_s, sems = rest[n_in + 6 :]
    s = pl.program_id(0)

    @pl.when(s == 0)
    def _():
        for copy in load_rows(pieces, pos_ref, lines, w_s, sems, first_col):
            copy.wait()
        gw_s[...] = jnp.zeros_like(gw_s)
        small_ref[...] = jnp.zeros_like(small_ref)

    live = live_mask(len_ref[s], D)
    res = res_ref[...]
    y = res + vec_ref[DOWN_B : DOWN_B + 1]
    gn2 = gns[0][...]
    for ref in ys:
        y = y + ref[...]
    for ref in gns[1:]:
        gn2 = gn2 + ref[...]
    y = jnp.where(live, y, 0.0).astype(BF16)
    glob_ref[0, 0] = y[:GLOB]
    long_ref[0, 0] = y[GLOB:]
    xhat, rstd = norm_stats(res)
    g = g_ref[...].astype(F32)
    gres = g + norm_back(gn2, xhat, rstd, vec_ref[GAIN2 : GAIN2 + 1])
    gres_ref[...] = gres
    gattn = gres.astype(BF16)
    gattn_s[...] = gattn
    small_ref[0:1] += jnp.sum(gn2 * xhat, axis=0, keepdims=True)
    small_ref[1:2] += jnp.sum(gn2, axis=0, keepdims=True)
    small_ref[2:3] += jnp.sum(gattn.astype(F32), axis=0, keepdims=True)
    small_ref[3:4] += jnp.sum(g, axis=0, keepdims=True)

    for c in tiles(D):
        gmix_ref[:, c] = dot(gattn_s[...], w_s[c, :], NT).astype(BF16)
        at = 0
        for m in mixed:
            gw_s[at : at + m.shape[1], c] += dot(m[...], gattn_s[:, c], TN)
            at += m.shape[1]

    @pl.when(s == pl.num_programs(0) - 1)
    def _():
        gw_ref[...] = gw_s[...].astype(BF16)


def mid(deps, pos, lengths, res, g, vec, ys, gns, mixed, pieces, first_col, long_shape, glob_shape):
    rows = res.shape[0]
    lines = pos.shape[0]
    spec = pl.BlockSpec((T, D), lambda s, *_: (s, 0))
    return run(
        functools.partial(mid_kernel, lines, len(pieces), first_col, len(mixed), len(ys)),
        deps,
        [pos, lengths],
        [res, g, vec, *ys, *gns, *mixed, *pieces],
        [
            jax.ShapeDtypeStruct(long_shape, BF16),
            jax.ShapeDtypeStruct(glob_shape, BF16),
            jax.ShapeDtypeStruct((rows, D), F32),
            jax.ShapeDtypeStruct((rows, D), BF16),
            jax.ShapeDtypeStruct((8, D), F32),
            jax.ShapeDtypeStruct((D, D), BF16),
        ],
        "mid",
        17,
        grid=(rows // T,),
        in_specs=[spec, spec, VMEM]
        + [spec] * (2 * len(ys))
        + [pl.BlockSpec((T, m.shape[1]), lambda s, *_: (s, 0)) for m in mixed]
        + [ANY] * len(pieces),
        out_specs=[
            pl.BlockSpec((1, 1, SEQ, D), lambda s, *_: (s, 0, 0, 0)),
            pl.BlockSpec((1, 1, GLOB, D), lambda s, *_: (s, 0, 0, 0)),
            spec,
            spec,
            pl.BlockSpec((8, D), lambda s, *_: (0, 0)),
            pl.BlockSpec((D, D), lambda s, *_: (0, 0)),
        ],
        scratch_shapes=[
            pltpu.VMEM((D, D), BF16),
            pltpu.VMEM((T, D), BF16),
            pltpu.VMEM((D, D), F32),
            pltpu.SemaphoreType.DMA((lines,)),
        ],
    )


def weight_kernel(n_grads, n_out, owned, pos_ref, normed_ref, *rest):
    grads = rest[:n_grads]
    extra = rest[n_grads : len(rest) - n_out - 2]
    outs = rest[len(rest) - n_out - 2 : len(rest) - 2]
    gw_s, out_sems = rest[len(rest) - 2 :]
    piece_rows = outs[0].shape[1]
    width = sum(ref.shape[1] for ref in grads) // 3
    at = 3 * width
    if owned:
        grels, (small2_ref, small1_ref, qv_ref, *gbs) = extra[:3], extra[3:]
        sides = dot(qv_ref[:2].astype(BF16), owner_order(owned), NT)
        half = D // 2
        a = jnp.concatenate([sides[:1, :half], sides[1:, :half]], axis=1)
        b = jnp.concatenate([sides[:1, half:], sides[1:, half:]], axis=1)
        vecs = [small1_ref[:2], a, b, small2_ref[:4]]
        vecs += [ref[:, D * i : D * (i + 1)] for ref in gbs for i in range(ref.shape[1] // D)]
        vecs = jnp.concatenate(vecs + [jnp.zeros((128 - 12, D), F32)], axis=0).T
        gw_s[:, at + LABELS :] = vecs.astype(BF16)
        row = 0
        for ref in grels:
            gw_s[row : row + ref.shape[0], at : at + LABELS] = ref[...].astype(BF16)
            row += ref.shape[0]
    else:
        for ref in extra:
            gw_s[:, at : at + ref.shape[1]] = ref[...].astype(BF16)
            at += ref.shape[1]
    first_pair = 0
    for grad_ref in grads:
        cols = grad_ref.shape[1]
        for c in tiles(cols):
            out = dot(normed_ref[...], grad_ref[:, c], TN).astype(BF16)
            for at in range(c.start, c.stop, 128):
                pair, part = at // WAYS, at % WAYS // 128
                to = width * part + 128 * (first_pair + pair)
                gw_s[:, to : to + 128] = out[:, at - c.start : at - c.start + 128]
        first_pair += cols // WAYS
    copies = store_rows(gw_s, outs, piece_rows, pos_ref, out_sems, 0)
    for copy in copies:
        copy.start()
    for copy in copies:
        copy.wait()


def weight_grad(deps, pos, normed, grads, extra, out_groups, owned=0):
    rows = normed.shape[0]
    lines = pos.shape[0]
    cols = sum(g.shape[1] for g in grads)
    cols += LABELS + 128 if owned else sum(r.shape[1] for r in extra)
    return run(
        functools.partial(weight_kernel, len(grads), len(out_groups), owned),
        deps,
        [pos],
        [normed, *grads, *extra],
        [jax.ShapeDtypeStruct((k, D // lines, cols), BF16) for k in out_groups],
        "weight_grad",
        cols / 200,
        grid=(1,),
        in_specs=[VMEM] * (1 + len(grads) + len(extra)),
        out_specs=[ANY] * len(out_groups),
        scratch_shapes=[pltpu.VMEM((D, cols), BF16), pltpu.SemaphoreType.DMA((lines,))],
    )


def input_kernel(lines, n_grads, n_in, pos_ref, long_in_ref, glob_in_ref, gres_ref, vec_ref, *rest):
    grads = rest[:n_grads]
    pieces = rest[n_grads : n_grads + 2 * n_in]
    long_ref, glob_ref, small_ref, qv_ref, w_s, gn1_s, sems = rest[n_grads + 2 * n_in :]
    copies = []
    to = 0
    for i, width in enumerate((FIRST, SECOND)):
        for pair in range(width // 128):
            for part in range(3):
                copies += load_rows(
                    pieces[n_in * i : n_in * (i + 1)],
                    pos_ref,
                    lines,
                    w_s.at[:, to : to + 128],
                    sems.at[to // 128],
                    width * part + 128 * pair,
                )
                to += 128
    at = 0
    for ref in grads:
        for pair in range(ref.shape[1] // WAYS):
            for row, part in ((0, 0), (1, 2)):
                col = WAYS * pair + 128 * part
                qv_ref[row : row + 1, at : at + 128] = jnp.sum(
                    ref[:, col : col + 128].astype(F32), axis=0, keepdims=True
                )
            at += 128
    for copy in copies:
        copy.wait()
    for c in tiles(D):
        total = 0.0
        at = 0
        for ref in grads:
            total = total + dot(ref[...], w_s[c, at : at + ref.shape[1]], NT)
            at += ref.shape[1]
        gn1_s[:, c] = total
    for s in range(long_in_ref.shape[0]):
        for src, dst, at, size in (
            (glob_in_ref, glob_ref, T * s, GLOB),
            (long_in_ref, long_ref, T * s + GLOB, SEQ),
        ):
            rows = slice(at, at + size)
            xhat, rstd = norm_stats(src[s, 0].astype(F32))
            gn1 = gn1_s[rows]
            dst[s, 0] = (gres_ref[rows] + norm_back(gn1, xhat, rstd, vec_ref[GAIN1 : GAIN1 + 1])).astype(BF16)
            sums = [jnp.sum(gn1 * xhat, axis=0, keepdims=True), jnp.sum(gn1, axis=0, keepdims=True)]
            for row in range(2):
                if s == 0 and src is glob_in_ref:
                    small_ref[row : row + 1] = sums[row]
                else:
                    small_ref[row : row + 1] += sums[row]


def input_grad(deps, pos, long_in, glob_in, gres, vec, grads, pieces):
    rows = gres.shape[0]
    lines = pos.shape[0]
    n = len(grads)
    return run(
        functools.partial(input_kernel, lines, n, len(pieces[0])),
        deps,
        [pos],
        [long_in, glob_in, gres, vec, *grads, *[p for group in pieces for p in group]],
        [
            jax.ShapeDtypeStruct(long_in.shape, BF16),
            jax.ShapeDtypeStruct(glob_in.shape, BF16),
            jax.ShapeDtypeStruct((8, D), F32),
            jax.ShapeDtypeStruct((8, D), F32),
        ],
        "input_grad",
        15,
        grid=(1,),
        in_specs=[VMEM] * (4 + n) + [ANY] * sum(len(p) for p in pieces),
        out_specs=[VMEM] * 4,
        scratch_shapes=[
            pltpu.VMEM((D, 3 * D), BF16),
            pltpu.VMEM((rows, D), F32),
            pltpu.SemaphoreType.DMA((3 * D // 128, lines)),
        ],
    )


def pack_kernel(w_qkv_ref, rel_ref, vec_ref, out_ref):
    width = FIRST
    for n in range(3):
        out_ref[:, width * n : width * (n + 1)] = w_qkv_ref[:, D * n : D * n + width]
    rows = rel_ref.shape[0]
    after_labels = VEC_AT - LEAD - RELS
    rest = LABELS - VEC_AT - vec_ref.shape[1]
    rel = jnp.concatenate(
        [
            jnp.zeros((rows, LEAD), F32),
            rel_ref[...].astype(F32),
            jnp.zeros((rows, after_labels), F32),
            vec_ref[...].astype(F32),
            jnp.zeros((rows, rest), F32),
        ],
        axis=1,
    )
    out_ref[:, 3 * width :] = rel.astype(BF16)


def pack(w_qkv, rel_embed, vec):
    rows = w_qkv.shape[0]
    return run(
        pack_kernel,
        [],
        [],
        [w_qkv, rel_embed, vec],
        [jax.ShapeDtypeStruct((rows, 3 * FIRST + LABELS), BF16)],
        "pack",
        1.5,
        grid=(1,),
        in_specs=[VMEM] * 3,
        out_specs=[VMEM],
        scratch_shapes=[],
    )[0]


def pack_next_kernel(w_qkv_ref, w_out_ref, out_ref):
    width = SECOND
    for n in range(3):
        out_ref[:, width * n : width * (n + 1)] = w_qkv_ref[:, D * (n + 1) - width : D * (n + 1)]
    out_ref[:, 3 * width :] = w_out_ref[...]


def pack_next(deps, w_qkv, w_out):
    rows = w_qkv.shape[0]
    return run(
        pack_next_kernel,
        deps,
        [],
        [w_qkv, w_out],
        [jax.ShapeDtypeStruct((rows, 3 * SECOND + D), BF16)],
        "pack",
        1.5,
        grid=(1,),
        in_specs=[VMEM] * 2,
        out_specs=[VMEM],
        scratch_shapes=[],
    )[0]


def pack_ffn_kernel(chunks, w_in_ref, w_down_ref, out_ref):
    rows = w_in_ref.shape[0]
    parts = FF // D
    per = parts // chunks
    down = w_down_ref[...].astype(F32)
    for c in range(chunks):
        at = 2 * per * D * c
        out_ref[:, at : at + per * D] = w_in_ref[:, per * D * c : per * D * (c + 1)]
        for i in range(per):
            q = per * c + i
            to = at + (per + i) * D
            out_ref[:, to : to + D] = down[rows * q : rows * (q + 1)].astype(BF16)


def pack_ffn(deps, w_in, w_down, chunks):
    rows = w_in.shape[0]
    return run(
        functools.partial(pack_ffn_kernel, chunks),
        deps,
        [],
        [w_in, w_down],
        [jax.ShapeDtypeStruct((rows, 2 * FF), BF16)],
        "pack",
        1.5,
        grid=(1,),
        in_specs=[VMEM] * 2,
        out_specs=[VMEM],
        scratch_shapes=[],
    )[0]


def unpack_kernel(n, *refs):
    g_qkv_ref, g_out_ref, g_rel_ref, small_ref = refs[2 * n :]
    for g, width in enumerate((FIRST, SECOND)):
        total = refs[n * g][...].astype(F32)
        for ref in refs[n * g + 1 : n * (g + 1)]:
            total = total + ref[...].astype(F32)
        for part in range(3):
            at = D * part + FIRST * g
            g_qkv_ref[:, at : at + width] = total[:, width * part : width * (part + 1)]
        if g == 1:
            g_out_ref[...] = total[:, 3 * width :]
        else:
            g_rel_ref[...] = total[:, 3 * width + BACK_LEAD : 3 * width + BACK_LEAD + RELS]
            rows = total.shape[0]
            vecs = total[:, 3 * width + LABELS :]
            vecs = jnp.concatenate([vecs, jnp.zeros((128 - rows, 128), F32)], axis=0).T
            small_ref[...] = vecs[:16, :rows]


def unpack(first, second):
    rows = first[0].shape[0]
    shape = lambda cols: jax.ShapeDtypeStruct((rows, cols), F32)
    return run(
        functools.partial(unpack_kernel, len(first)),
        [],
        [],
        [*first, *second],
        [shape(3 * D), shape(D), shape(RELS), jax.ShapeDtypeStruct((16, rows), F32)],
        "unpack",
        2,
        grid=(1,),
        in_specs=[VMEM] * (2 * len(first)),
        out_specs=[VMEM] * 4,
        scratch_shapes=[],
    )


def order_kernel(z_ref, *refs):
    parts, out_ref, total_s = refs[:-2], refs[-2], refs[-1]
    for mask, part in enumerate(parts):
        total_s[z_ref[0] ^ mask] = part[...].astype(F32)
    out_ref[...] = total_s[...].reshape(out_ref.shape).astype(out_ref.dtype)


def order(deps, z, parts):
    rows, cols = parts[0].shape
    lines = len(parts)
    return run(
        order_kernel,
        deps,
        [z],
        parts,
        [jax.ShapeDtypeStruct((lines * rows, cols), parts[0].dtype)],
        "order",
        1.5,
        grid=(1,),
        in_specs=[VMEM] * lines,
        out_specs=[VMEM],
        scratch_shapes=[pltpu.VMEM((lines, rows, cols), F32)],
    )[0]


def join_kernel(x_ref, y_ref, out_ref):
    rows = x_ref.shape[0]
    out_ref[:rows] = x_ref[...]
    out_ref[rows:] = y_ref[...]


def join(deps, x, y):
    rows, cols = x.shape
    parts = 4 if cols % 512 == 0 else 1
    return run(
        join_kernel,
        deps,
        [],
        [x, y],
        [jax.ShapeDtypeStruct((2 * rows, cols), x.dtype)],
        "join",
        1.5,
        grid=(parts,),
        in_specs=[pl.BlockSpec((rows, cols // parts), lambda i: (0, i))] * 2,
        out_specs=[pl.BlockSpec((2 * rows, cols // parts), lambda i: (0, i))],
        scratch_shapes=[],
    )[0]


def split_kernel(lines, z_ref, *refs):
    terms = refs[: len(refs) - lines - 1]
    outs = refs[len(terms) : len(terms) + lines]
    total_s = refs[-1]
    total = terms[0][...].reshape(terms[0].shape[-2:]).astype(F32)
    for ref in terms[1:]:
        total = total + ref[...].reshape(ref.shape[-2:]).astype(F32)
    total_s[...] = total.reshape(total_s.shape)
    for mask, out in enumerate(outs):
        out[...] = total_s[z_ref[0] ^ mask].astype(out.dtype)


def split(deps, z, terms, lines):
    rows, cols = terms[0].shape[-2:]
    kind = terms[0].dtype
    specs = []
    for t in terms:
        if t.ndim == 3:
            specs.append(pl.BlockSpec((1, rows, cols), lambda i, *_: (0, 0, 0)))
        else:
            specs.append(pl.BlockSpec((rows, cols), lambda i, *_: (0, 0)))
    rows = rows // lines
    return run(
        functools.partial(split_kernel, lines),
        deps,
        [z],
        terms,
        [jax.ShapeDtypeStruct((rows, cols), F32 if m == 0 else kind) for m in range(lines)],
        "split",
        2,
        grid=(1,),
        in_specs=specs,
        out_specs=[VMEM] * lines,
        scratch_shapes=[pltpu.VMEM((lines, rows, cols), F32)],
    )


def sum_kernel(*refs):
    total = refs[0][...].astype(F32)
    for ref in refs[1:-1]:
        total = total + ref[...].astype(F32)
    refs[-1][...] = total.reshape(refs[-1].shape).astype(refs[-1].dtype)


def second(deps, terms):
    _, rows, cols = terms[0].shape
    return run(
        sum_kernel,
        deps,
        [],
        terms,
        [jax.ShapeDtypeStruct((rows, cols), terms[0].dtype)],
        "second",
        2,
        grid=(1,),
        in_specs=[pl.BlockSpec((1, rows, cols), lambda i: (1, 0, 0))] * len(terms),
        out_specs=[VMEM],
        scratch_shapes=[],
    )[0]


def both(deps, terms):
    lines, rows, cols = terms[0].shape
    spec = pl.BlockSpec((1, rows, cols), lambda i: (i, 0, 0))
    return run(
        sum_kernel,
        deps,
        [],
        terms,
        [jax.ShapeDtypeStruct(terms[0].shape, terms[0].dtype)],
        "both",
        2,
        grid=(lines,),
        in_specs=[spec] * len(terms),
        out_specs=[spec],
        scratch_shapes=[],
    )[0]


AXES = ("wide", "narrow")


class Links:
    def __init__(self, mesh):
        self.wide = mesh.shape["wide"]
        self.narrow = mesh.shape["narrow"]
        self.count = self.wide * self.narrow
        self.pairwise = self.wide == 8 and self.narrow == 4
        self.lines = self.wide if self.pairwise else 1
        self.groups = (2, 2, 2, 2) if self.pairwise else (1,)

    def setup(self):
        if not self.pairwise:
            self.pos = jnp.zeros((1,), jnp.int32)
            return
        w = lax.axis_index("wide")
        self.z = lax.axis_index("narrow")
        near = jnp.where(w % 2 == 0, 2, 4)
        far = 6 - near
        order = [0, near, far, 6, 1, 1 ^ far, 1 ^ near, 7]
        self.pos = jnp.stack([w ^ m for m in order]).astype(jnp.int32)

    def slot(self, *marks):
        self.marks = list(marks)

    def swap(self, x, wide_mask=0, narrow_mask=0):
        masks = wide_mask if isinstance(wide_mask, tuple) else (wide_mask, wide_mask)
        pairs = []
        for w in range(self.wide):
            for z in range(self.narrow):
                pairs.append(
                    (w * self.narrow + z, (w ^ masks[w % 2]) * self.narrow + (z ^ narrow_mask))
                )
        return lax.ppermute(x, AXES, pairs)

    def line(self, x):
        if not self.pairwise:
            return [lax.all_gather(x, AXES, axis=0, tiled=True)]
        return [x] + [self.swap(x, 0, mask) for mask in (1, 2, 3)]

    def near(self, parts):
        if not self.pairwise:
            return parts
        x = order(self.marks, self.z.reshape(1), parts)
        return [x, self.swap(x, (2, 4))]

    def far(self, parts):
        if not self.pairwise:
            return parts
        own = join(self.marks, *parts)
        return [own, self.swap(own, (4, 2)), self.swap(own, 1)]

    def core(self, pieces):
        if not self.pairwise:
            return pieces
        own, far, own_core = pieces
        if self.marks:
            far = after(far, self.marks)
        return [own, far, own_core, self.swap(far, 1)]

    def add(self, *parts):
        total = parts[0].astype(F32)
        for p in parts[1:]:
            total = total + p.astype(F32)
        return total


class Sum:
    def __init__(self, links, parts):
        self.links = links
        self.parts = parts
        self.kind = parts[0].dtype

    def core(self):
        links = self.links
        if not links.pairwise:
            self.out = lax.psum_scatter(self.parts[0][0].astype(F32), AXES, scatter_dimension=0, tiled=True)
            return (self.out,)
        self.got_b = links.swap(self.parts[3], 1)
        self.got_a = links.swap(self.parts[2], 1)
        return (self.got_b, self.got_a)

    def far(self):
        links = self.links
        if not links.pairwise:
            return (self.out,)
        self.from_far = links.swap(both(links.marks, [self.parts[1], self.got_b]), (4, 2))
        return (self.from_far,)

    def near(self):
        links = self.links
        if not links.pairwise:
            return (self.out,)
        self.from_near = links.swap(second(links.marks, [self.parts[0], self.got_a, self.from_far]), (2, 4))
        return (self.from_near,)

    def line(self):
        links = self.links
        if not links.pairwise:
            self.terms = [self.out]
            return (self.out,)
        terms = [self.parts[0], self.got_a, self.from_far, self.from_near]
        mine, *others = split(links.marks, links.z.reshape(1), terms, links.narrow)
        got = [links.swap(x, 0, mask) for mask, x in enumerate(others, 1)]
        self.terms = [mine] + got
        return tuple(got)

    def total(self):
        return self.links.add(*self.terms)


CHUNKS = 2
PARTS = FF // D
PAIRS = 6


def body(links, long_in, glob_in, lengths, ln1_gain, ln1_bias, w_qkv, qv_bias, rel_embed, w_out, out_bias, ln2_gain, ln2_bias, w_in, in_bias, w_down, down_bias, cot_long, cot_glob):
    links.setup()
    pos = links.pos
    groups = links.groups
    count = links.count
    micro = long_in.shape[0]
    r = w_qkv.shape[0]
    lens = lengths.reshape(micro)
    per = PARTS // CHUNKS
    first, second = 3 * FIRST, 3 * SECOND
    n_first, n_second = FIRST // 128, SECOND // 128

    columns = [ln1_gain, ln1_bias, qv_bias, out_bias, ln2_gain, ln2_bias, down_bias, in_bias]
    columns = jnp.concatenate([v.reshape(-1, r) for v in columns], axis=0).T
    w_in_parts = w_in.reshape(r, count, PARTS, r).transpose(0, 2, 1, 3).reshape(r, FF)

    links.slot()
    line_a0 = links.line(pack(w_qkv, rel_embed, columns))
    near_a0 = links.near(line_a0)
    line_a1 = links.line(pack_next([line_a0[-1]], w_qkv, w_out))
    ffn_shard = pack_ffn([], w_in_parts, w_down, CHUNKS)
    links.slot(line_a1[0], ffn_shard)
    far_a0 = links.far(near_a0)
    links.slot(line_a1[-1])
    attn = [links.core(far_a0)]
    line_f = links.line(after(ffn_shard, [attn[0][-1]]))

    proj0, normed, rel_all, rel_turned, vec = project_first([], pos, long_in, glob_in, attn[0], r, first)
    links.slot(attn[0][-1])
    near_a1 = links.near(line_a1)
    mixed0, inv0, p0, pg0 = attend([near_a1[-1], line_f[-1]], lens, proj0, rel_all, 0)
    links.slot(proj0, near_a1[-1])
    far_a1 = links.far(near_a1)
    near_f = links.near(line_f)
    links.slot(mixed0)
    attn.append(links.core(far_a1))
    proj1 = project_next([near_f[-1], mixed0], pos, normed, vec, attn[1], second)
    links.slot(mixed0, far_a1[-1], near_f[-1])
    far_f = links.far(near_f)
    mixed1, inv1, p1, pg1 = attend([], lens, proj1, rel_all, n_first)
    mixed = [mixed0, mixed1]
    links.slot(mixed1)
    ffn_all = links.core(far_f)
    res, n2, g_ffn = mix_out(
        [ffn_all[len(ffn_all) // 4]], pos, lens, long_in, glob_in, cot_long, cot_glob, vec, mixed, attn[1], second
    )
    y0, gn0, gb0, *gw0 = ffn([], pos, n2, g_ffn, vec, ffn_all, 0, per, groups)
    sum0 = Sum(links, gw0)
    y1, gn1, gb1, *gw1 = ffn([y0], pos, n2, g_ffn, vec, ffn_all, per, per, groups)
    steps = sum0.core()
    sum1 = Sum(links, gw1)
    block_long, block_glob, gres, gmix, small2, gw_out = mid(
        [*steps], pos, lens, res, g_ffn, vec, [y0, y1], [gn0, gn1], mixed, attn[1], second, long_in.shape, glob_in.shape
    )
    links.slot(y1, *steps)
    steps = sum0.far() + sum1.core()
    gproj1, grel1 = attend_back([*steps], proj1, rel_turned, gmix, mixed1, inv1, p1, pg1, n_first, 0, 2)
    links.slot(gmix, *steps)
    steps = sum0.near() + sum1.far()
    gproj2, grel2 = attend_back([*steps], proj1, rel_turned, gmix, mixed1, inv1, p1, pg1, n_first, 2, 2)
    links.slot(gproj1, *steps)
    steps = sum0.line() + sum1.near()
    gw_a1 = weight_grad([*steps], pos, normed, [gproj1, gproj2], [gw_out], groups)
    sum2 = Sum(links, gw_a1)
    sum2.core()
    links.slot(gw_a1[0], *steps)
    steps = sum1.line() + sum2.far()
    gproj0, grel0 = attend_back([gw_a1[0]], proj0, rel_turned, gmix, mixed0, inv0, p0, pg0, 0, 0, n_first)
    grad_long, grad_glob, small1, small_qv = input_grad(
        [*steps], pos, long_in, glob_in, gres, vec, [gproj0, gproj1, gproj2], attn
    )
    links.slot(gproj0, *steps)
    steps = sum2.near()
    gw_a0 = weight_grad(
        [*steps], pos, normed, [gproj0], [grel0, grel1, grel2, small2, small1, small_qv, gb0, gb1], groups, r
    )
    sum3 = Sum(links, gw_a0)
    links.slot(small1, *steps)
    sum2.line()
    sum3.core()
    w_sums = [sum0.total(), sum1.total()]
    g_in = jnp.concatenate([w[:, : per * D] for w in w_sums], axis=1)
    g_in = g_in.reshape(r, PARTS, count, r).transpose(0, 2, 1, 3).reshape(r, FF)
    g_down = jnp.concatenate([w[:, D * (per + i) : D * (per + i + 1)] for w in w_sums for i in range(per)], axis=0)
    links.slot(gw_a0[0], *sum2.terms[1:])
    sum3.far()
    links.slot(g_in, g_down)
    sum3.near()
    links.slot()
    sum3.line()
    g_qkv, g_out, g_rel, small = unpack(sum3.terms, sum2.terms)
    g_gain1, g_bias1 = small[GAIN1], small[BIAS1]
    g_qv = small[2:4].reshape(-1)
    g_gain2, g_bias2, g_out_b, g_down_b = small[4], small[5], small[6], small[7]
    g_in_b = small[8:12].reshape(-1)
    return (
        block_long, block_glob, grad_long, grad_glob,
        g_gain1, g_bias1, g_qkv, g_qv, g_rel, g_out, g_out_b,
        g_gain2, g_bias2, g_in, g_in_b, g_down, g_down_b,
    )


def solution(mesh):
    rows = P(None, AXES, None, None)
    vec = P(AXES)
    mat = P(AXES, None)
    placed = (rows, rows, P(None, AXES), vec, vec, mat, vec, mat, mat, vec, vec, vec, mat, vec, mat, vec, rows, rows)
    return jax.shard_map(
        functools.partial(body, Links(mesh)),
        mesh=mesh,
        in_specs=placed,
        out_specs=(rows, rows, rows, rows, vec, vec, mat, vec, mat, mat, vec, vec, vec, mat, vec, mat, vec),
        check_vma=False,
    )
```

time: 508 us -> 375 us (0.74)
  waiting for transfers between devices: 160 us -> 36 us
  other arithmetic: 16.3 us -> 2.92 us
    ppermute x54 -> x49, waiting for transfers between devices: 160 us -> 36 us  [swap(): return lax.ppermute(x, AXES, pairs)]
    concatenate x21 -> x2, other arithmetic: 11.3 us -> 0.76 us  [the longest x1 0.74 us: body(): jnp.concatenate([w[:, D * (per + i):D * (per + i + 1)] for w in w_sums fo...]
    slice x18 -> x7, local copies, waits for them, and re-layouts: 10.2 us -> 2.08 us  [the longest x2 0.7 us: body(): w[:, D * (per + i):D * (per + i + 1)]]
    unnamed x93 -> x64, local copies, waits for them, and re-layouts: 4.09 us -> 9.2 us
    pallas_call x12 -> x40, Pallas kernels: 237 us -> 242 us  [the longest x36 242 us: run(): pl.pallas_call(with_deps, grid_spec=pltpu.PrefetchScalarGridSpec(num_scal...]
    reshape x14 -> x16, local copies, waits for them, and re-layouts: 9.14 us -> 14.2 us  [the longest x10 6.16 us: body(): columns = jnp.concatenate([v.reshape(-1, r) for v in columns], axis=0).T]
    ppermute x54 -> x49, starting transfers between devices: 54.4 us -> 58.6 us  [swap(): return lax.ppermute(x, AXES, pairs)]
  transfers between devices with their start and end apart: 54 -> 49, of which waited for: 29 -> 14; matrix products, arithmetic and copies ran while one was open for 5% -> 3% of each run, Pallas kernels for 25% -> 49%
where the time goes in v2:
time: 375 us; the launch traced here: 371 us
  Pallas kernels  242 us (65%)
  starting transfers between devices  58.6 us (16%)
  waiting for transfers between devices  36 us (10%)
  local copies, waits for them, and re-layouts  29.6 us (8%)
    pallas_call x36, Pallas kernels, run(): pl.pallas_call(with_deps, grid_spec=pltpu.PrefetchScalarGridSpec(num_scal...  242 us
    ppermute x49, starting transfers between devices, swap(): return lax.ppermute(x, AXES, pairs)  58.6 us
    ppermute x49, waiting for transfers between devices, swap(): return lax.ppermute(x, AXES, pairs)  36 us
    unnamed x64, local copies, waits for them, and re-layouts  9.2 us
  transfers between devices with their start and end apart: 49, of which 14 were waited for; matrix products, arithmetic and copies ran while one was open for 3% of the time, Pallas kernels for 49%

profile of v2, /device:TPU:0, one launch (start us, length us, event | category | flops | bytes accessed | tf_op | source)
XLA Modules:
  0.0 370.8 jit_solution(6523683774732501951)
XLA Ops:
  7.5 1.6 pack.3.refs_1_
  9.2 4.0 %collective-permute-start.2 = (bf16[24,1024]{1,0:T(8,128)(2,1)}, bf16[24,1024]{1,0:T(8,128)(2,1)S(1)}, u32[]{:S(2)}, u32[]{:S(2)}) collective-permute-start(bf16[24,1024]{1,0:T(8,128)(2,1)} %pack.3.refs_1_), channel_id=1, source_target_pairs={{0,2},{1,3},{2,0},{3,1},{4,6},{5,7},{6,4},{7,5},{8,10},{9,11},{10,... | collective-permute-start | bytes 147464 | tf_op jit(solution)/shard_map/ppermute | solution.py:1195
  13.2 1.6 collective-permute-start.1
  16.2 1.9 reshape.99.refs_0_
  18.1 2.8 collective-permute-done.refs_0_.refs_4_
  21.5 1.6 order.3.refs_2_
  23.1 1.5 collective-permute-start.3
  24.6 1.7 pack.5.refs_1_.refs_0_
  26.3 1.6 pack.4.refs_0_.refs_2_
  29.6 3.3 join.3.refs_3_.refs_12_
  32.9 1.5 collective-permute-start.4
  35.5 5.5 %collective-permute-done.5.refs_1_.refs_5_ = bf16[24,2304]{1,0:T(8,128)(2,1)S(1)} collective-permute-done((bf16[24,2304]{1,0:T(8,128)(2,1)S(1)}, bf16[24,2304]{1,0:T(8,128)(2,1)S(1)}, u32[]{:S(2)}, u32[]{:S(2)}) %collective-permute-start.5) | collective-permute-done | bytes 110624 | tf_op jit(solution)/shard_map/ppermute | solution.py:1195
  42.9 1.6 collective-permute-start.7
  47.3 2.0 collective-permute-start.13
  51.1 2.7 collective-permute-start.10
  53.8 1.9 order.4.refs_2_
  55.7 1.5 collective-permute-start.9
  57.9 7.9 %project.2 = (bf16[1088,768]{1,0:T(8,128)(2,1)}, bf16[1088,768]{1,0:T(8,128)(2,1)}, bf16[768,256]{1,0:T(8,128)(2,1)}, bf16[256,768]{1,0:T(8,128)(2,1)}, f32[16,768]{1,0:T(8,128)}) custom-call(s32[8]{0:T(128)} %stack.35.refs_0_, bf16[2,1,512,768]{3,2,1,0:T(8,128)(2,1)} %refs_5_.3, bf16[2,1,32,768]{3,2,1,0:T(8,128)(2,1)} %refs_6_.3, ...), custom_call_target="tpu_custom_call" | custom-call | flops 10350000128 | bytes 1048576 | tf_op jit(solution)/shard_map/project/pallas_call | solution.py:50
  66.7 2.1 join.4.refs_5_.refs_10_.refs_13_.refs_16_
  68.8 5.8 %collective-permute-start.17 = (bf16[192,2304]{1,0:T(8,128)(2,1)}, bf16[192,2304]{1,0:T(8,128)(2,1)}, u32[]{:S(2)}, u32[]{:S(2)}) collective-permute-start(bf16[192,2304]{1,0:T(8,128)(2,1)} %join.4.refs_5_.refs_10_.refs_13_.refs_16_), channel_id=1, source_target_pairs={{0,16},{1,17},{2,18},{3,19},{4,12},{5,13},{6,14},{7,15},{8,24},{9,... | collective-permute-start | bytes 2654216 | tf_op jit(solution)/shard_map/ppermute | solution.py:1195
  74.6 2.5 order.5.refs_3_
  77.1 11.5 %attend.2 = (bf16[1088,256]{1,0:T(8,128)(2,1)}, f32[1088,256]{1,0:T(8,128)}, bf16[2,2,256,1280]{3,2,1,0:T(8,128)(2,1)}, bf16[2,2,64,544]{3,2,1,0:T(8,128)(2,1)}) custom-call(s32[2]{0:T(128)} %bitcast.42, bf16[96,2304]{1,0:T(8,128)(2,1)} %copy-done.18, bf16[24,6144]{1,0:T(8,128)(2,1)} %collective-permute-done.10.refs_2_.refs_6_, ...), custom_call_target="tpu_custom_call" | custom-call | flops 14259999744 | bytes 1048576 | tf_op jit(solution)/shard_map/attend/pallas_call | solution.py:50
  88.6 3.9 %collective-permute-done.17.refs_0_ = bf16[192,2304]{1,0:T(8,128)(2,1)} collective-permute-done((bf16[192,2304]{1,0:T(8,128)(2,1)}, bf16[192,2304]{1,0:T(8,128)(2,1)}, u32[]{:S(2)}, u32[]{:S(2)}) %collective-permute-start.17) | collective-permute-done | bytes 884768 | tf_op jit(solution)/shard_map/ppermute | solution.py:1195
  93.6 3.9 %join.5.refs_4_.refs_5_ = bf16[192,6144]{1,0:T(8,128)(2,1)} custom-call(bf16[1088,256]{1,0:T(8,128)(2,1)} %get-tuple-element.93.refs_0_.refs_1_.refs_2_.refs_8_.refs_11_.refs_4_, bf16[192,2304]{1,0:T(8,128)(2,1)} %copy-done.1, bf16[96,6144]{1,0:T(8,128)(2,1)} %collective-permute-done.15.refs_2_.refs_4_.refs_1_, bf16[96,6144]{1,0:T(8,128)(2,1)} %order.5.refs_3_, ...), custom_call_target="tpu_custom_call" | custom-call | flops 1724999936 | bytes 1048576 | tf_op jit(solution)/shard_map/join/pallas_call | solution.py:50
  97.5 4.7 %collective-permute-start.19 = (bf16[192,6144]{1,0:T(8,128)(2,1)}, bf16[192,6144]{1,0:T(8,128)(2,1)}, u32[]{:S(2)}, u32[]{:S(2)}) collective-permute-start(bf16[192,6144]{1,0:T(8,128)(2,1)} %join.5.refs_4_.refs_5_), channel_id=1, source_target_pairs={{0,4},{1,5},{2,6},{3,7},{4,0},{5,1},{6,2},{7,3},{8,12},{9,13},{10,... | collective-permute-start | bytes 7077896 | tf_op jit(solution)/shard_map/ppermute | solution.py:1195
  102.2 2.0 collective-permute-start.16
  104.3 8.3 %project.3.refs_1_.refs_3_.refs_2_ = bf16[1088,1536]{1,0:T(8,128)(2,1)} custom-call(s32[8]{0:T(128)} %stack.35.refs_0_, bf16[96,6144]{1,0:T(8,128)(2,1)} %collective-permute-done.15.refs_2_.refs_4_.refs_1_, bf16[1088,256]{1,0:T(8,128)(2,1)} %get-tuple-element.93.refs_0_.refs_1_.refs_2_.refs_8_.refs_11_.refs_4_, ...), custom_call_target="tpu_custom_call" | custom-call | flops 9200000000 | bytes 1048576 | tf_op jit(solution)/shard_map/project/pallas_call | solution.py:50
  112.6 21.0 %attend.3 = (bf16[1088,512]{1,0:T(8,128)(2,1)}, f32[1088,512]{1,0:T(8,128)}, bf16[2,4,256,1280]{3,2,1,0:T(8,128)(2,1)}, bf16[2,4,64,544]{3,2,1,0:T(8,128)(2,1)}) custom-call(s32[2]{0:T(128)} %bitcast.43, bf16[1088,1536]{1,0:T(8,128)(2,1)} %project.3.refs_1_.refs_3_.refs_2_, bf16[768,256]{1,0:T(8,128)(2,1)} %get-tuple-element.92.refs_4_.refs_2_), custom_call_target="tpu_custom_call" | custom-call | flops 28519999488 | bytes 1048576 | tf_op jit(solution)/shard_map/attend/pallas_call | solution.py:50
  133.7 9.4 %mix_out.1 = (f32[1088,768]{1,0:T(8,128)}, bf16[1088,768]{1,0:T(8,128)(2,1)}, bf16[1088,768]{1,0:T(8,128)(2,1)}) custom-call(s32[8]{0:T(128)} %stack.35.refs_0_, s32[2]{0:T(128)} %bitcast.44, bf16[192,6144]{1,0:T(8,128)(2,1)} %after.7.refs_2_.refs_5_.refs_6_, bf16[2,1,512,768]{3,2,1,0:T(8,128)(2,1)} %refs_5_.3, bf16[2,1,32,768]{3,2,1,0:T(8,128)(2,1)} %refs_6_.3, ...), custom_call_target="tpu_custom_call" | custom-call | flops 11500000256 | bytes 1048576 | tf_op jit(solution)/shard_map/mix_out/pallas_call | solution.py:50
  143.1 27.7 %ffn.2 = (f32[1088,768]{1,0:T(8,128)}, f32[1088,768]{1,0:T(8,128)}, f32[1,1536]{1,0:T(1,128)}, bf16[2,96,3072]{2,1,0:T(8,128)(2,1)}, bf16[2,96,3072]{2,1,0:T(8,1...) custom-call(s32[8]{0:T(128)} %stack.35.refs_0_, ...), custom_call_target="tpu_custom_call" | custom-call | flops 32199999488 | bytes 1048576 | tf_op jit(solution)/shard_map/ffn/pallas_call | solution.py:50
  171.4 27.9 %ffn.3 = (f32[1088,768]{1,0:T(8,128)}, f32[1088,768]{1,0:T(8,128)}, f32[1,1536]{1,0:T(1,128)}, bf16[2,96,3072]{2,1,0:T(8,128)(2,1)}, bf16[2,96,3072]{2,1,0:T(8,1...) custom-call(s32[8]{0:T(128)} %stack.35.refs_0_, f32[1088,768]{1,0:T(8,128)} %get-tuple-element.102.refs_1_.refs_7_, ...), custom_call_target="tpu_custom_call" | custom-call | flops 32199999488 | bytes 1048576 | tf_op jit(solution)/shard_map/ffn/pallas_call | solution.py:50
  199.9 2.6 both.4
  202.5 17.1 %mid.1 = (bf16[2,1,512,768]{3,2,1,0:T(8,128)(2,1)}, bf16[2,1,32,768]{3,2,1,0:T(8,128)(2,1)}, f32[1088,768]{1,0:T(8,128)}, bf16[1088,768]{1,0:T(8,128)(2,1)}, f32[8,768]{1,0:T(8,128)}, /*index=5*/bf16[768,768]{1,0:T(8,128)(2,1)}) custom-call(s32[8]{0:T(128)} %stack.35.refs_0_, s32[2]{0:T(128)} %bitcast.45, ...), custom_call_target="tpu_custom_call" | custom-call | flops 19549999104 | bytes 1048576 | tf_op jit(solution)/shard_map/mid/pallas_call | solution.py:50
  219.6 2.5 second.4
  222.1 1.7 collective-permute-start.26
  223.8 2.6 both.5
  226.7 9.8 %attend_back.3 = (bf16[1088,768]{1,0:T(8,128)(2,1)}, f32[256,256]{1,0:T(8,128)}) custom-call(bf16[2,96,3072]{2,1,0:T(8,128)(2,1)} %collective-permute-done.23.refs_0_.refs_1_.refs_6_, bf16[2,96,3072]{2,1,0:T(8,128)(2,1)} %collective-permute-done.24.refs_1_.refs_2_.refs_5_, bf16[2,96,3072]{2,1,0:T(8,128)(2,1)} %collective-permute-done.25.refs_2_.refs_3_.refs_4_.refs_7_, ...), custom_call_target="tpu_custom_call" | custom-call | flops 18400000000 | bytes 1048576 | tf_op jit(solution)/shard_map/attend_back/pallas_call | solution.py:50
  236.5 7.9 %collective-permute-done.27.refs_3_.refs_2_.refs_5_.refs_1_.refs_8_ = bf16[2,96,3072]{2,1,0:T(8,128)(2,1)} collective-permute-done((bf16[2,96,3072]{2,1,0:T(8,128)(2,1)}, bf16[2,96,3072]{2,1,0:T(8,128)(2,1)}, u32[]{:S(2)}, u32[]{:S(2)}) %collective-permute-start.27) | collective-permute-done | bytes 1179680 | tf_op jit(solution)/shard_map/ppermute | solution.py:1195
  244.4 3.0 split.4
  247.9 3.8 %collective-permute-start.30 = (bf16[24,3072]{1,0:T(8,128)(2,1)}, bf16[24,3072]{1,0:T(8,128)(2,1)S(1)}, u32[]{:S(2)}, u32[]{:S(2)}) collective-permute-start(bf16[24,3072]{1,0:T(8,128)(2,1)} %get-tuple-element.121), channel_id=1, source_target_pairs={{0,3},{1,2},{2,1},{3,0},{4,7},{5,6},{6,5},{7,4},{8,11},{9,10},{10,... | collective-permute-start | bytes 442376 | tf_op jit(solution)/shard_map/ppermute | solution.py:1195
  251.8 2.4 second.5
  254.2 1.7 collective-permute-start.31
  255.9 10.0 %attend_back.4 = (bf16[1088,768]{1,0:T(8,128)(2,1)}, f32[256,256]{1,0:T(8,128)}) custom-call(bf16[96,3072]{1,0:T(8,128)(2,1)} %copy-done.16, bf16[2,96,3072]{2,1,0:T(8,128)(2,1)} %collective-permute-done.27.refs_3_.refs_2_.refs_5_.refs_1_.refs_8_, bf16[1088,1536]{1,0:T(8,128)(2,1)} %project.3.refs_1_.refs_3_.refs_2_, ...), custom_call_target="tpu_custom_call" | custom-call | flops 18400000000 | bytes 1048576 | tf_op jit(solution)/shard_map/attend_back/pallas_call | solution.py:50
  266.8 8.8 %weight_grad.2 = (bf16[2,96,2304]{2,1,0:T(8,128)(2,1)}, bf16[2,96,2304]{2,1,0:T(8,128)(2,1)}, bf16[2,96,2304]{2,1,0:T(8,128)(2,1)}, bf16[2,96,2304]{2,1,0:T(8,128)(2,1)}) custom-call(s32[8]{0:T(128)} %stack.35.refs_0_, bf16[24,3072]{1,0:T(8,128)(2,1)} %copy-done.12, bf16[24,3072]{1,0:T(8,128)(2,1)} %copy-done.13, bf16[24,3072]{1,0:T(8,128)(2,1)} %copy-done.14, ...), custom_call_target="tpu_custom_call" | custom-call | flops 13248000000 | bytes 1048576 | tf_op jit(solution)/shard_map/weight_grad/pallas_call | solution.py:50
  277.4 2.9 split.5
  281.0 3.8 %collective-permute-start.34 = (bf16[24,3072]{1,0:T(8,128)(2,1)}, bf16[24,3072]{1,0:T(8,128)(2,1)S(1)}, u32[]{:S(2)}, u32[]{:S(2)}) collective-permute-start(bf16[24,3072]{1,0:T(8,128)(2,1)} %get-tuple-element.128), channel_id=1, source_target_pairs={{0,3},{1,2},{2,1},{3,0},{4,7},{5,6},{6,5},{7,4},{8,11},{9,10},{10,... | collective-permute-start | bytes 442376 | tf_op jit(solution)/shard_map/ppermute | solution.py:1195
  284.8 2.3 both.6
  287.4 10.1 %attend_back.5 = (bf16[1088,768]{1,0:T(8,128)(2,1)}, f32[256,256]{1,0:T(8,128)}) custom-call(bf16[2,96,2304]{2,1,0:T(8,128)(2,1)} %get-tuple-element.125.refs_1_.refs_0_.refs_5_.refs_3_, bf16[1088,768]{1,0:T(8,128)(2,1)} %get-tuple-element.91.refs_3_.refs_0_.refs_1_, bf16[256,768]{1,0:T(8,128)(2,1)} %get-tuple-element.111.refs_4_.refs_3_.refs_2_, ...), custom_call_target="tpu_custom_call" | custom-call | flops 18400000000 | bytes 1048576 | tf_op jit(solution)/shard_map/attend_back/pallas_call | solution.py:50
  297.6 2.8 collective-permute-done.36.refs_4_.refs_7_.refs_5_
  300.5 2.2 second.6
  303.0 14.9 %input_grad.1 = (bf16[2,1,512,768]{3,2,1,0:T(8,128)(2,1)}, bf16[2,1,32,768]{3,2,1,0:T(8,128)(2,1)}, f32[8,768]{1,0:T(8,128)}, f32[8,768]{1,0:T(8,128)}) custom-call(s32[8]{0:T(128)} %stack.35.refs_0_, bf16[24,3072]{1,0:T(8,128)(2,1)} %copy-done.8, bf16[24,3072]{1,0:T(8,128)(2,1)} %copy-done.10, bf16[24,3072]{1,0:T(8,128)(2,1)} %copy-done.11, ...), custom_call_target="tpu_custom_call" | custom-call | flops 17250000896 | bytes 1048576 | tf_op jit(solution)/shard_map/input_grad/pallas_call | solution.py:50
  318.7 2.6 split.6
  321.9 3.8 %collective-permute-start.42 = (bf16[24,2304]{1,0:T(8,128)(2,1)}, bf16[24,2304]{1,0:T(8,128)(2,1)}, u32[]{:S(2)}, u32[]{:S(2)}) collective-permute-start(bf16[24,2304]{1,0:T(8,128)(2,1)} %get-tuple-element.151), channel_id=1, source_target_pairs={{0,3},{1,2},{2,1},{3,0},{4,7},{5,6},{6,5},{7,4},{8,11},{9,10},{10,... | collective-permute-start | bytes 331784 | tf_op jit(solution)/shard_map/ppermute | solution.py:1195
  325.7 6.3 %weight_grad.3 = (bf16[2,96,1152]{2,1,0:T(8,128)(2,1)}, bf16[2,96,1152]{2,1,0:T(8,128)(2,1)}, bf16[2,96,1152]{2,1,0:T(8,128)(2,1)}, bf16[2,96,1152]{2,1,0:T(8,128)(2,1)}) custom-call(s32[8]{0:T(128)} %stack.35.refs_0_, bf16[96,2304]{1,0:T(8,128)(2,1)} %copy-done.17, bf16[1088,768]{1,0:T(8,128)(2,1)} %get-tuple-element.94.refs_3_.refs_5_.refs_2_, ...), custom_call_target="tpu_custom_call" | custom-call | flops 6624000000 | bytes 1048576 | tf_op jit(solution)/shard_map/weight_grad/pallas_call | solution.py:50
  334.8 2.2 both.7
  340.5 2.6 reshape.101.refs_0_
  343.9 1.9 collective-permute-done.44.refs_4_.refs_3_
  345.7 1.9 second.7
  347.6 1.7 collective-permute-start.45
  349.4 4.4 %collective-permute-done.45.refs_4_ = bf16[96,1152]{1,0:T(8,128)(2,1)S(1)} collective-permute-done((bf16[96,1152]{1,0:T(8,128)(2,1)}, bf16[96,1152]{1,0:T(8,128)(2,1)S(1)}, u32[]{:S(2)}, u32[]{:S(2)}) %collective-permute-start.45) | collective-permute-done | bytes 221216 | tf_op jit(solution)/shard_map/ppermute | solution.py:1195
  354.5 2.1 split.7
  357.3 3.6 collective-permute-start.48
  362.4 1.7 collective-permute-done.48.refs_3_
  364.6 2.0 unpack.1
  (170 shorter events, 42.6 us)
Async XLA Ops:
  7.5 7.3 %copy-start.7 = (bf16[24,3072]{1,0:T(8,128)(2,1)S(1)}, bf16[24,3072]{1,0:T(8,128)(2,1)}, u32[]{:S(2)}) copy-start(bf16[24,3072]{1,0:T(8,128)(2,1)} %param.30) | copy-start | bytes 442372
  9.2 8.9 %collective-permute-start.2 = (bf16[24,1024]{1,0:T(8,128)(2,1)}, bf16[24,1024]{1,0:T(8,128)(2,1)S(1)}, u32[]{:S(2)}, u32[]{:S(2)}) collective-permute-start(bf16[24,1024]{1,0:T(8,128)(2,1)} %pack.3.refs_1_), channel_id=1, source_target_pairs={{0,2},{1,3},{2,0},{3,1},{4,6},{5,7},{6,4},{7,5},{8,10},{9,11},{10,... | collective-permute-start | bytes 147464 | tf_op jit(solution)/shard_map/ppermute | solution.py:1195
  13.2 4.9 %collective-permute-start.1 = (bf16[24,1024]{1,0:T(8,128)(2,1)}, bf16[24,1024]{1,0:T(8,128)(2,1)S(1)}, u32[]{:S(2)}, u32[]{:S(2)}) collective-permute-start(bf16[24,1024]{1,0:T(8,128)(2,1)} %pack.3.refs_1_), channel_id=1, source_target_pairs={{0,1},{1,0},{2,3},{3,2},{4,5},{5,4},{6,7},{7,6},{8,9},{9,8},{10,11... | collective-permute-start | bytes 147464 | tf_op jit(solution)/shard_map/ppermute | solution.py:1195
  14.8 6.1 %collective-permute-start = (bf16[24,1024]{1,0:T(8,128)(2,1)}, bf16[24,1024]{1,0:T(8,128)(2,1)S(1)}, u32[]{:S(2)}, u32[]{:S(2)}) collective-permute-start(bf16[24,1024]{1,0:T(8,128)(2,1)} %pack.3.refs_1_), channel_id=1, source_target_pairs={{0,3},{1,2},{2,1},{3,0},{4,7},{5,6},{6,5},{7,4},{8,11},{9,10},{10,... | collective-permute-start | bytes 147464 | tf_op jit(solution)/shard_map/ppermute | solution.py:1195
  18.1 2.8 copy-start.30
  18.1 2.8 copy-start.31
  23.1 5.9 %collective-permute-start.3 = (bf16[96,1024]{1,0:T(8,128)(2,1)}, bf16[96,1024]{1,0:T(8,128)(2,1)S(1)}, u32[]{:S(2)}, u32[]{:S(2)}) collective-permute-start(bf16[96,1024]{1,0:T(8,128)(2,1)} %order.3.refs_2_), channel_id=1, source_target_pairs={{0,8},{1,9},{2,10},{3,11},{4,20},{5,21},{6,22},{7,23},{8,0},{9,1},... | collective-permute-start | bytes 589832 | tf_op jit(solution)/shard_map/ppermute | solution.py:1195
  27.8 6.6 %copy-start.24 = (bf16[24,2304]{1,0:T(8,128)(2,1)S(1)}, bf16[24,2304]{1,0:T(8,128)(2,1)}, u32[]{:S(2)}) copy-start(bf16[24,2304]{1,0:T(8,128)(2,1)} %pack.4.refs_0_.refs_2_) | copy-start | bytes 331780
  32.9 8.1 %collective-permute-start.4 = (bf16[192,1024]{1,0:T(8,128)(2,1)}, bf16[192,1024]{1,0:T(8,128)(2,1)S(1)}, u32[]{:S(2)}, u32[]{:S(2)}) collective-permute-start(bf16[192,1024]{1,0:T(8,128)(2,1)} %join.3.refs_3_.refs_12_), channel_id=1, source_target_pairs={{0,16},{1,17},{2,18},{3,19},{4,12},{5,13},{6,14},{7,15},{8,24},{9,... | collective-permute-start | bytes 1179656 | tf_op jit(solution)/shard_map/ppermute | solution.py:1195
  34.4 6.5 %collective-permute-start.5 = (bf16[24,2304]{1,0:T(8,128)(2,1)S(1)}, bf16[24,2304]{1,0:T(8,128)(2,1)S(1)}, u32[]{:S(2)}, u32[]{:S(2)}) collective-permute-start(bf16[24,2304]{1,0:T(8,128)(2,1)S(1)} %copy-done.24), channel_id=1, source_target_pairs={{0,3},{1,2},{2,1},{3,0},{4,7},{5,6},{6,5},{7,4},{8,11},{9,10},{10,... | collective-permute-start | bytes 331784 | tf_op jit(solution)/shard_map/ppermute | solution.py:1195
  42.4 2.8 collective-permute-start.6
  42.4 14.8 %collective-permute-start.11 = (bf16[192,1024]{1,0:T(8,128)(2,1)}, bf16[192,1024]{1,0:T(8,128)(2,1)S(1)}, u32[]{:S(2)}, u32[]{:S(2)}) collective-permute-start(bf16[192,1024]{1,0:T(8,128)(2,1)} %join.3.refs_3_.refs_12_), channel_id=1, source_target_pairs={{0,4},{1,5},{2,6},{3,7},{4,0},{5,1},{6,2},{7,3},{8,12},{9,13},{10,... | collective-permute-start | bytes 1179656 | tf_op jit(solution)/shard_map/ppermute | solution.py:1195
  42.9 7.5 %collective-permute-start.8 = (bf16[24,2304]{1,0:T(8,128)(2,1)S(1)}, bf16[24,2304]{1,0:T(8,128)(2,1)S(1)}, u32[]{:S(2)}, u32[]{:S(2)}) collective-permute-start(bf16[24,2304]{1,0:T(8,128)(2,1)S(1)} %copy-done.24), channel_id=1, source_target_pairs={{0,2},{1,3},{2,0},{3,1},{4,6},{5,7},{6,4},{7,5},{8,10},{9,11},{10,... | collective-permute-start | bytes 331784 | tf_op jit(solution)/shard_map/ppermute | solution.py:1195
  42.9 10.9 %collective-permute-start.7 = (bf16[24,2304]{1,0:T(8,128)(2,1)S(1)}, bf16[24,2304]{1,0:T(8,128)(2,1)}, u32[]{:S(2)}, u32[]{:S(2)}) collective-permute-start(bf16[24,2304]{1,0:T(8,128)(2,1)S(1)} %copy-done.24), channel_id=1, source_target_pairs={{0,1},{1,0},{2,3},{3,2},{4,5},{5,4},{6,7},{7,6},{8,9},{9,8},{10,11... | collective-permute-start | bytes 331784 | tf_op jit(solution)/shard_map/ppermute | solution.py:1195
  46.0 28.6 %collective-permute-start.14 = (bf16[24,6144]{1,0:T(8,128)(2,1)}, bf16[24,6144]{1,0:T(8,128)(2,1)}, u32[]{:S(2)}, u32[]{:S(2)}) collective-permute-start(bf16[24,6144]{1,0:T(8,128)(2,1)} %after.5.refs_3_), channel_id=1, source_target_pairs={{0,2},{1,3},{2,0},{3,1},{4,6},{5,7},{6,4},{7,5},{8,10},{9,11},{10,... | collective-permute-start | bytes 884744 | tf_op jit(solution)/shard_map/ppermute | solution.py:1195
  47.3 27.3 %collective-permute-start.13 = (bf16[24,6144]{1,0:T(8,128)(2,1)}, bf16[24,6144]{1,0:T(8,128)(2,1)}, u32[]{:S(2)}, u32[]{:S(2)}) collective-permute-start(bf16[24,6144]{1,0:T(8,128)(2,1)} %after.5.refs_3_), channel_id=1, source_target_pairs={{0,1},{1,0},{2,3},{3,2},{4,5},{5,4},{6,7},{7,6},{8,9},{9,8},{10,11... | collective-permute-start | bytes 884744 | tf_op jit(solution)/shard_map/ppermute | solution.py:1195
  51.1 23.5 %collective-permute-start.10 = (bf16[24,6144]{1,0:T(8,128)(2,1)}, bf16[24,6144]{1,0:T(8,128)(2,1)}, u32[]{:S(2)}, u32[]{:S(2)}) collective-permute-start(bf16[24,6144]{1,0:T(8,128)(2,1)} %after.5.refs_3_), channel_id=1, source_target_pairs={{0,3},{1,2},{2,1},{3,0},{4,7},{5,6},{6,5},{7,4},{8,11},{9,10},{10,... | collective-permute-start | bytes 884744 | tf_op jit(solution)/shard_map/ppermute | solution.py:1195
  55.7 10.2 %collective-permute-start.9 = (bf16[96,2304]{1,0:T(8,128)(2,1)}, bf16[96,2304]{1,0:T(8,128)(2,1)S(1)}, u32[]{:S(2)}, u32[]{:S(2)}) collective-permute-start(bf16[96,2304]{1,0:T(8,128)(2,1)} %order.4.refs_2_), channel_id=1, source_target_pairs={{0,8},{1,9},{2,10},{3,11},{4,20},{5,21},{6,22},{7,23},{8,0},{9,1},... | collective-permute-start | bytes 1327112 | tf_op jit(solution)/shard_map/ppermute | solution.py:1195
  68.8 23.7 %collective-permute-start.17 = (bf16[192,2304]{1,0:T(8,128)(2,1)}, bf16[192,2304]{1,0:T(8,128)(2,1)}, u32[]{:S(2)}, u32[]{:S(2)}) collective-permute-start(bf16[192,2304]{1,0:T(8,128)(2,1)} %join.4.refs_5_.refs_10_.refs_13_.refs_16_), channel_id=1, source_target_pairs={{0,16},{1,17},{2,18},{3,19},{4,12},{5,13},{6,14},{7,15},{8,24},{9,... | collective-permute-start | bytes 2654216 | tf_op jit(solution)/shard_map/ppermute | solution.py:1195
  74.5 17.9 %collective-permute-start.12 = (bf16[192,2304]{1,0:T(8,128)(2,1)}, bf16[192,2304]{1,0:T(8,128)(2,1)S(1)}, u32[]{:S(2)}, u32[]{:S(2)}) collective-permute-start(bf16[192,2304]{1,0:T(8,128)(2,1)} %join.4.refs_5_.refs_10_.refs_13_.refs_16_), channel_id=1, source_target_pairs={{0,4},{1,5},{2,6},{3,7},{4,0},{5,1},{6,2},{7,3},{8,12},{9,13},{10,... | collective-permute-start | bytes 2654216 | tf_op jit(solution)/shard_map/ppermute | solution.py:1195
  77.1 16.5 %collective-permute-start.15 = (bf16[96,6144]{1,0:T(8,128)(2,1)}, bf16[96,6144]{1,0:T(8,128)(2,1)}, u32[]{:S(2)}, u32[]{:S(2)}) collective-permute-start(bf16[96,6144]{1,0:T(8,128)(2,1)} %order.5.refs_3_), channel_id=1, source_target_pairs={{0,8},{1,9},{2,10},{3,11},{4,20},{5,21},{6,22},{7,23},{8,0},{9,1},... | collective-permute-start | bytes 3538952 | tf_op jit(solution)/shard_map/ppermute | solution.py:1195
  92.5 11.8 %collective-permute-start.18 = (bf16[192,2304]{1,0:T(8,128)(2,1)}, bf16[192,2304]{1,0:T(8,128)(2,1)}, u32[]{:S(2)}, u32[]{:S(2)}) collective-permute-start(bf16[192,2304]{1,0:T(8,128)(2,1)} %after.6.refs_6_.refs_11_.refs_14_.refs_17_), channel_id=1, source_target_pairs={{0,4},{1,5},{2,6},{3,7},{4,0},{5,1},{6,2},{7,3},{8,12},{9,13},{10,... | collective-permute-start | bytes 2654216 | tf_op jit(solution)/shard_map/ppermute | solution.py:1195
  97.5 45.6 %collective-permute-start.19 = (bf16[192,6144]{1,0:T(8,128)(2,1)}, bf16[192,6144]{1,0:T(8,128)(2,1)}, u32[]{:S(2)}, u32[]{:S(2)}) collective-permute-start(bf16[192,6144]{1,0:T(8,128)(2,1)} %join.5.refs_4_.refs_5_), channel_id=1, source_target_pairs={{0,4},{1,5},{2,6},{3,7},{4,0},{5,1},{6,2},{7,3},{8,12},{9,13},{10,... | collective-permute-start | bytes 7077896 | tf_op jit(solution)/shard_map/ppermute | solution.py:1195
  102.2 31.4 %collective-permute-start.16 = (bf16[192,6144]{1,0:T(8,128)(2,1)}, bf16[192,6144]{1,0:T(8,128)(2,1)}, u32[]{:S(2)}, u32[]{:S(2)}) collective-permute-start(bf16[192,6144]{1,0:T(8,128)(2,1)} %join.5.refs_4_.refs_5_), channel_id=1, source_target_pairs={{0,16},{1,17},{2,18},{3,19},{4,12},{5,13},{6,14},{7,15},{8,24},{9,... | collective-permute-start | bytes 7077896 | tf_op jit(solution)/shard_map/ppermute | solution.py:1195
  133.6 9.5 %collective-permute-start.20 = (bf16[192,6144]{1,0:T(8,128)(2,1)}, bf16[192,6144]{1,0:T(8,128)(2,1)}, u32[]{:S(2)}, u32[]{:S(2)}) collective-permute-start(bf16[192,6144]{1,0:T(8,128)(2,1)} %after.7.refs_2_.refs_5_.refs_6_), channel_id=1, source_target_pairs={{0,4},{1,5},{2,6},{3,7},{4,0},{5,1},{6,2},{7,3},{8,12},{9,13},{10,... | collective-permute-start | bytes 7077896 | tf_op jit(solution)/shard_map/ppermute | solution.py:1195
  170.8 29.1 %collective-permute-start.21 = (bf16[2,96,3072]{2,1,0:T(8,128)(2,1)}, bf16[2,96,3072]{2,1,0:T(8,128)(2,1)}, u32[]{:S(2)}, u32[]{:S(2)}) collective-permute-start(bf16[2,96,3072]{2,1,0:T(8,128)(2,1)} %get-tuple-element.99), channel_id=1, source_target_pairs={{0,4},{1,5},{2,6},{3,7},{4,0},{5,1},{6,2},{7,3},{8,12},{9,13},{10,... | collective-permute-start | bytes 3538952 | tf_op jit(solution)/shard_map/ppermute | solution.py:1195
  171.4 28.5 %collective-permute-start.22 = (bf16[2,96,3072]{2,1,0:T(8,128)(2,1)}, bf16[2,96,3072]{2,1,0:T(8,128)(2,1)}, u32[]{:S(2)}, u32[]{:S(2)}) collective-permute-start(bf16[2,96,3072]{2,1,0:T(8,128)(2,1)} %get-tuple-element.100), channel_id=1, source_target_pairs={{0,4},{1,5},{2,6},{3,7},{4,0},{5,1},{6,2},{7,3},{8,12},{9,13},{10,... | collective-permute-start | bytes 3538952 | tf_op jit(solution)/shard_map/ppermute | solution.py:1195
  199.3 20.3 %collective-permute-start.24 = (bf16[2,96,3072]{2,1,0:T(8,128)(2,1)}, bf16[2,96,3072]{2,1,0:T(8,128)(2,1)}, u32[]{:S(2)}, u32[]{:S(2)}) collective-permute-start(bf16[2,96,3072]{2,1,0:T(8,128)(2,1)} %get-tuple-element.109), channel_id=1, source_target_pairs={{0,4},{1,5},{2,6},{3,7},{4,0},{5,1},{6,2},{7,3},{8,12},{9,13},{10,... | collective-permute-start | bytes 3538952 | tf_op jit(solution)/shard_map/ppermute | solution.py:1195
  199.8 19.8 %collective-permute-start.25 = (bf16[2,96,3072]{2,1,0:T(8,128)(2,1)}, bf16[2,96,3072]{2,1,0:T(8,128)(2,1)}, u32[]{:S(2)}, u32[]{:S(2)}) collective-permute-start(bf16[2,96,3072]{2,1,0:T(8,128)(2,1)} %get-tuple-element.110), channel_id=1, source_target_pairs={{0,4},{1,5},{2,6},{3,7},{4,0},{5,1},{6,2},{7,3},{8,12},{9,13},{10,... | collective-permute-start | bytes 3538952 | tf_op jit(solution)/shard_map/ppermute | solution.py:1195
  202.5 17.2 %collective-permute-start.23 = (bf16[2,96,3072]{2,1,0:T(8,128)(2,1)}, bf16[2,96,3072]{2,1,0:T(8,128)(2,1)}, u32[]{:S(2)}, u32[]{:S(2)}) collective-permute-start(bf16[2,96,3072]{2,1,0:T(8,128)(2,1)} %both.4), channel_id=1, source_target_pairs={{0,16},{1,17},{2,18},{3,19},{4,12},{5,13},{6,14},{7,15},{8,24},{9,... | collective-permute-start | bytes 3538952 | tf_op jit(solution)/shard_map/ppermute | solution.py:1195
  222.1 14.4 %collective-permute-start.26 = (bf16[96,3072]{1,0:T(8,128)(2,1)}, bf16[96,3072]{1,0:T(8,128)(2,1)S(1)}, u32[]{:S(2)}, u32[]{:S(2)}) collective-permute-start(bf16[96,3072]{1,0:T(8,128)(2,1)} %second.4), channel_id=1, source_target_pairs={{0,8},{1,9},{2,10},{3,11},{4,20},{5,21},{6,22},{7,23},{8,0},{9,1},... | collective-permute-start | bytes 1769480 | tf_op jit(solution)/shard_map/ppermute | solution.py:1195
  226.4 18.1 %collective-permute-start.27 = (bf16[2,96,3072]{2,1,0:T(8,128)(2,1)}, bf16[2,96,3072]{2,1,0:T(8,128)(2,1)}, u32[]{:S(2)}, u32[]{:S(2)}) collective-permute-start(bf16[2,96,3072]{2,1,0:T(8,128)(2,1)} %both.5), channel_id=1, source_target_pairs={{0,16},{1,17},{2,18},{3,19},{4,12},{5,13},{6,14},{7,15},{8,24},{9,... | collective-permute-start | bytes 3538952 | tf_op jit(solution)/shard_map/ppermute | solution.py:1195
  236.5 7.9 %copy-start.16 = (bf16[96,3072]{1,0:T(8,128)(2,1)}, bf16[96,3072]{1,0:T(8,128)(2,1)S(1)}, u32[]{:S(2)}) copy-start(bf16[96,3072]{1,0:T(8,128)(2,1)S(1)} %collective-permute-done.26.refs_2_.refs_7_.refs_1_.refs_0_) | copy-start | bytes 1769476
  247.4 18.6 %collective-permute-start.28 = (bf16[24,3072]{1,0:T(8,128)(2,1)}, bf16[24,3072]{1,0:T(8,128)(2,1)S(1)}, u32[]{:S(2)}, u32[]{:S(2)}) collective-permute-start(bf16[24,3072]{1,0:T(8,128)(2,1)} %get-tuple-element.119), channel_id=1, source_target_pairs={{0,1},{1,0},{2,3},{3,2},{4,5},{5,4},{6,7},{7,6},{8,9},{9,8},{10,11... | collective-permute-start | bytes 442376 | tf_op jit(solution)/shard_map/ppermute | solution.py:1195
  247.4 18.6 %collective-permute-start.29 = (bf16[24,3072]{1,0:T(8,128)(2,1)}, bf16[24,3072]{1,0:T(8,128)(2,1)S(1)}, u32[]{:S(2)}, u32[]{:S(2)}) collective-permute-start(bf16[24,3072]{1,0:T(8,128)(2,1)} %get-tuple-element.120), channel_id=1, source_target_pairs={{0,2},{1,3},{2,0},{3,1},{4,6},{5,7},{6,4},{7,5},{8,10},{9,11},{10,... | collective-permute-start | bytes 442376 | tf_op jit(solution)/shard_map/ppermute | solution.py:1195
  247.9 18.1 %collective-permute-start.30 = (bf16[24,3072]{1,0:T(8,128)(2,1)}, bf16[24,3072]{1,0:T(8,128)(2,1)S(1)}, u32[]{:S(2)}, u32[]{:S(2)}) collective-permute-start(bf16[24,3072]{1,0:T(8,128)(2,1)} %get-tuple-element.121), channel_id=1, source_target_pairs={{0,3},{1,2},{2,1},{3,0},{4,7},{5,6},{6,5},{7,4},{8,11},{9,10},{10,... | collective-permute-start | bytes 442376 | tf_op jit(solution)/shard_map/ppermute | solution.py:1195
  254.2 11.8 %collective-permute-start.31 = (bf16[96,3072]{1,0:T(8,128)(2,1)}, bf16[96,3072]{1,0:T(8,128)(2,1)}, u32[]{:S(2)}, u32[]{:S(2)}) collective-permute-start(bf16[96,3072]{1,0:T(8,128)(2,1)} %second.5), channel_id=1, source_target_pairs={{0,8},{1,9},{2,10},{3,11},{4,20},{5,21},{6,22},{7,23},{8,0},{9,1},... | collective-permute-start | bytes 1769480 | tf_op jit(solution)/shard_map/ppermute | solution.py:1195
  266.8 8.9 %copy-start.6 = (f32[24,3072]{1,0:T(8,128)S(1)}, f32[24,3072]{1,0:T(8,128)}, u32[]{:S(2)}) copy-start(f32[24,3072]{1,0:T(8,128)} %get-tuple-element.154) | copy-start | bytes 884740
  275.5 9.2 %collective-permute-start.35 = (bf16[2,96,2304]{2,1,0:T(8,128)(2,1)}, bf16[2,96,2304]{2,1,0:T(8,128)(2,1)}, u32[]{:S(2)}, u32[]{:S(2)}) collective-permute-start(bf16[2,96,2304]{2,1,0:T(8,128)(2,1)} %get-tuple-element.130), channel_id=1, source_target_pairs={{0,4},{1,5},{2,6},{3,7},{4,0},{5,1},{6,2},{7,3},{8,12},{9,13},{10,... | collective-permute-start | bytes 2654216 | tf_op jit(solution)/shard_map/ppermute | solution.py:1195
  276.8 3.6 copy-start
  280.4 17.2 %collective-permute-start.32 = (bf16[24,3072]{1,0:T(8,128)(2,1)}, bf16[24,3072]{1,0:T(8,128)(2,1)S(1)}, u32[]{:S(2)}, u32[]{:S(2)}) collective-permute-start(bf16[24,3072]{1,0:T(8,128)(2,1)} %get-tuple-element.126), channel_id=1, source_target_pairs={{0,1},{1,0},{2,3},{3,2},{4,5},{5,4},{6,7},{7,6},{8,9},{9,8},{10,11... | collective-permute-start | bytes 442376 | tf_op jit(solution)/shard_map/ppermute | solution.py:1195
  280.4 17.2 %collective-permute-start.33 = (bf16[24,3072]{1,0:T(8,128)(2,1)}, bf16[24,3072]{1,0:T(8,128)(2,1)S(1)}, u32[]{:S(2)}, u32[]{:S(2)}) collective-permute-start(bf16[24,3072]{1,0:T(8,128)(2,1)} %get-tuple-element.127), channel_id=1, source_target_pairs={{0,2},{1,3},{2,0},{3,1},{4,6},{5,7},{6,4},{7,5},{8,10},{9,11},{10,... | collective-permute-start | bytes 442376 | tf_op jit(solution)/shard_map/ppermute | solution.py:1195
  281.0 16.7 %collective-permute-start.34 = (bf16[24,3072]{1,0:T(8,128)(2,1)}, bf16[24,3072]{1,0:T(8,128)(2,1)S(1)}, u32[]{:S(2)}, u32[]{:S(2)}) collective-permute-start(bf16[24,3072]{1,0:T(8,128)(2,1)} %get-tuple-element.128), channel_id=1, source_target_pairs={{0,3},{1,2},{2,1},{3,0},{4,7},{5,6},{6,5},{7,4},{8,11},{9,10},{10,... | collective-permute-start | bytes 442376 | tf_op jit(solution)/shard_map/ppermute | solution.py:1195
  284.8 12.9 %collective-permute-start.37 = (bf16[2,96,2304]{2,1,0:T(8,128)(2,1)}, bf16[2,96,2304]{2,1,0:T(8,128)(2,1)}, u32[]{:S(2)}, u32[]{:S(2)}) collective-permute-start(bf16[2,96,2304]{2,1,0:T(8,128)(2,1)} %get-tuple-element.138), channel_id=1, source_target_pairs={{0,4},{1,5},{2,6},{3,7},{4,0},{5,1},{6,2},{7,3},{8,12},{9,13},{10,... | collective-permute-start | bytes 2654216 | tf_op jit(solution)/shard_map/ppermute | solution.py:1195
  287.1 13.4 %collective-permute-start.36 = (bf16[2,96,2304]{2,1,0:T(8,128)(2,1)}, bf16[2,96,2304]{2,1,0:T(8,128)(2,1)}, u32[]{:S(2)}, u32[]{:S(2)}) collective-permute-start(bf16[2,96,2304]{2,1,0:T(8,128)(2,1)} %both.6), channel_id=1, source_target_pairs={{0,16},{1,17},{2,18},{3,19},{4,12},{5,13},{6,14},{7,15},{8,24},{9,... | collective-permute-start | bytes 2654216 | tf_op jit(solution)/shard_map/ppermute | solution.py:1195
  297.6 2.9 copy-start.8
  297.6 2.9 copy-start.10
  297.6 2.9 copy-start.11
  302.7 15.2 %collective-permute-start.38 = (bf16[96,2304]{1,0:T(8,128)(2,1)}, bf16[96,2304]{1,0:T(8,128)(2,1)S(1)}, u32[]{:S(2)}, u32[]{:S(2)}) collective-permute-start(bf16[96,2304]{1,0:T(8,128)(2,1)} %second.6), channel_id=1, source_target_pairs={{0,8},{1,9},{2,10},{3,11},{4,20},{5,21},{6,22},{7,23},{8,0},{9,1},... | collective-permute-start | bytes 1327112 | tf_op jit(solution)/shard_map/ppermute | solution.py:1195
  321.3 12.4 %collective-permute-start.40 = (bf16[24,2304]{1,0:T(8,128)(2,1)}, bf16[24,2304]{1,0:T(8,128)(2,1)S(1)}, u32[]{:S(2)}, u32[]{:S(2)}) collective-permute-start(bf16[24,2304]{1,0:T(8,128)(2,1)} %get-tuple-element.149), channel_id=1, source_target_pairs={{0,1},{1,0},{2,3},{3,2},{4,5},{5,4},{6,7},{7,6},{8,9},{9,8},{10,11... | collective-permute-start | bytes 331784 | tf_op jit(solution)/shard_map/ppermute | solution.py:1195
  321.3 12.4 %collective-permute-start.41 = (bf16[24,2304]{1,0:T(8,128)(2,1)}, bf16[24,2304]{1,0:T(8,128)(2,1)}, u32[]{:S(2)}, u32[]{:S(2)}) collective-permute-start(bf16[24,2304]{1,0:T(8,128)(2,1)} %get-tuple-element.150), channel_id=1, source_target_pairs={{0,2},{1,3},{2,0},{3,1},{4,6},{5,7},{6,4},{7,5},{8,10},{9,11},{10,... | collective-permute-start | bytes 331784 | tf_op jit(solution)/shard_map/ppermute | solution.py:1195
  321.9 11.8 %collective-permute-start.42 = (bf16[24,2304]{1,0:T(8,128)(2,1)}, bf16[24,2304]{1,0:T(8,128)(2,1)}, u32[]{:S(2)}, u32[]{:S(2)}) collective-permute-start(bf16[24,2304]{1,0:T(8,128)(2,1)} %get-tuple-element.151), channel_id=1, source_target_pairs={{0,3},{1,2},{2,1},{3,0},{4,7},{5,6},{6,5},{7,4},{8,11},{9,10},{10,... | collective-permute-start | bytes 331784 | tf_op jit(solution)/shard_map/ppermute | solution.py:1195
  325.7 6.4 %copy-start.5 = (f32[24,3072]{1,0:T(8,128)S(1)}, f32[24,3072]{1,0:T(8,128)}, u32[]{:S(2)}) copy-start(f32[24,3072]{1,0:T(8,128)} %get-tuple-element.155) | copy-start | bytes 884740
  325.7 6.4 %copy-start.9 = (bf16[24,3072]{1,0:T(8,128)(2,1)S(1)}, bf16[24,3072]{1,0:T(8,128)(2,1)}, u32[]{:S(2)}) copy-start(bf16[24,3072]{1,0:T(8,128)(2,1)} %copy-done.8) | copy-start | bytes 442372
  332.0 2.1 collective-permute-start.43
  333.2 10.7 %collective-permute-start.39 = (bf16[2,96,1152]{2,1,0:T(8,128)(2,1)}, bf16[2,96,1152]{2,1,0:T(8,128)(2,1)}, u32[]{:S(2)}, u32[]{:S(2)}) collective-permute-start(bf16[2,96,1152]{2,1,0:T(8,128)(2,1)} %get-tuple-element.148), channel_id=1, source_target_pairs={{0,4},{1,5},{2,6},{3,7},{4,0},{5,1},{6,2},{7,3},{8,12},{9,13},{10,... | collective-permute-start | bytes 1327112 | tf_op jit(solution)/shard_map/ppermute | solution.py:1195
  334.8 3.3 slice-start
  337.0 8.7 %collective-permute-start.44 = (bf16[2,96,1152]{2,1,0:T(8,128)(2,1)}, bf16[2,96,1152]{2,1,0:T(8,128)(2,1)}, u32[]{:S(2)}, u32[]{:S(2)}) collective-permute-start(bf16[2,96,1152]{2,1,0:T(8,128)(2,1)} %both.7), channel_id=1, source_target_pairs={{0,16},{1,17},{2,18},{3,19},{4,12},{5,13},{6,14},{7,15},{8,24},{9,... | collective-permute-start | bytes 1327112 | tf_op jit(solution)/shard_map/ppermute | solution.py:1195
  340.5 2.6 copy-start.4
  347.6 6.1 %collective-permute-start.45 = (bf16[96,1152]{1,0:T(8,128)(2,1)}, bf16[96,1152]{1,0:T(8,128)(2,1)S(1)}, u32[]{:S(2)}, u32[]{:S(2)}) collective-permute-start(bf16[96,1152]{1,0:T(8,128)(2,1)} %second.7), channel_id=1, source_target_pairs={{0,8},{1,9},{2,10},{3,11},{4,20},{5,21},{6,22},{7,23},{8,0},{9,1},... | collective-permute-start | bytes 663560 | tf_op jit(solution)/shard_map/ppermute | solution.py:1195
  356.6 4.5 %collective-permute-start.46 = (bf16[24,1152]{1,0:T(8,128)(2,1)}, bf16[24,1152]{1,0:T(8,128)(2,1)S(1)}, u32[]{:S(2)}, u32[]{:S(2)}) collective-permute-start(bf16[24,1152]{1,0:T(8,128)(2,1)} %get-tuple-element.157), channel_id=1, source_target_pairs={{0,1},{1,0},{2,3},{3,2},{4,5},{5,4},{6,7},{7,6},{8,9},{9,8},{10,11... | collective-permute-start | bytes 165896 | tf_op jit(solution)/shard_map/ppermute | solution.py:1195
  357.1 5.3 %collective-permute-start.47 = (bf16[24,1152]{1,0:T(8,128)(2,1)}, bf16[24,1152]{1,0:T(8,128)(2,1)S(1)}, u32[]{:S(2)}, u32[]{:S(2)}) collective-permute-start(bf16[24,1152]{1,0:T(8,128)(2,1)} %get-tuple-element.158), channel_id=1, source_target_pairs={{0,2},{1,3},{2,0},{3,1},{4,6},{5,7},{6,4},{7,5},{8,10},{9,11},{10,... | collective-permute-start | bytes 165896 | tf_op jit(solution)/shard_map/ppermute | solution.py:1195
  357.3 6.7 %collective-permute-start.48 = (bf16[24,1152]{1,0:T(8,128)(2,1)}, bf16[24,1152]{1,0:T(8,128)(2,1)S(1)}, u32[]{:S(2)}, u32[]{:S(2)}) collective-permute-start(bf16[24,1152]{1,0:T(8,128)(2,1)} %get-tuple-element.159), channel_id=1, source_target_pairs={{0,3},{1,2},{2,1},{3,0},{4,7},{5,6},{6,5},{7,4},{8,11},{9,10},{10,... | collective-permute-start | bytes 165896 | tf_op jit(solution)/shard_map/ppermute | solution.py:1195
  361.1 2.9 copy-start.26
  (18 other events, 14.4 us)
